TPU v7x, 32 devices: a whole 2x2x4 slice. The times are simulated.
32 devices in a mesh: hi: 8 (over z, y), lo: 4 (over x, core).
Axes of the slice: x: 2, y: 2, z: 4, core: 2. Of those that a mesh axis runs over, the one named last changes fastest.
Arguments:
- amplitudes: float32 [2, 32, 512, 256], P(None, ('hi', 'lo')), may hold values from -6 to 6
- joined_gates: float32 [2, 2, 512, 512], replicated, may hold values from -0.1875 to 0.1875
- pair_gates: float32 [2, 2, 2, 2], replicated, may hold values from -3 to 3
- global_angles: float32 [2, 32], P(None, ('hi', 'lo')), may hold values from -3.140625 to 3.140625
- local_phases: float32 [2, 17], replicated, may hold values from -3.140625 to 3.140625
- slice_bits: int32 [17], replicated, may hold values from 0 to 1
- coupled_qubits: int32 [2, 17], replicated, may hold values from 0 to 16
- gate_layout: int32 [9], replicated, may hold values from 0 to 8, each once
Outputs:
- evolved: float32 [2, 32, 512, 256], P(None, ('hi', 'lo'))
Inputs may be any that keep to these rules, and one draw needn't show every extreme that they name: `gate_layout`: each of 0 to 8 once.
All inputs are finite; a program needn't handle non-finite values.
Results may differ from a plain program's by a relative error of at most 0.0001.
Values sent between devices are 32-bit elements; how exact they have to be, the bound alone decides.
No kernel may reach another device: no remote copies, remote signals or barrier semaphores. Data moves between devices by JAX's collectives and lax.ppermute only.
A program may use at most 64 MiB of HBM per device.

v0:
```python
import math

import jax
import jax.numpy as jnp
from jax import lax
from jax.sharding import PartitionSpec as P

ROW_BITS = 9
COL_BITS = 8
LAYERS = 2
ROWS = 512
COLS = 256
LQ = 17


def partner_2(value, axis, bit):
    mask = 2**bit
    pairs = [(source, source ^ mask) for source in range(lax.axis_size(axis))]
    return lax.ppermute(value, axis, pairs)


def bit_angles(angles, bit_count, length):
    positions = jnp.arange(length, dtype=jnp.int32)
    summed = jnp.zeros((length,), jnp.float32)
    for bit_pos in range(bit_count):
        chosen = (positions >> bit_pos & 1).astype(jnp.float32)
        summed = summed + chosen * angles[bit_pos]
    return summed


def qubit_angles(local_phases, slice_bits, coupled_qubits, layer_id):
    qubits = jnp.arange(LQ, dtype=jnp.int32)
    matches = (coupled_qubits[layer_id][:, None] == qubits[None, :]).astype(jnp.float32)
    flipped = jnp.sum(matches * slice_bits[:, None].astype(jnp.float32), axis=0)
    return local_phases[layer_id] + math.pi * flipped


def folded_gate(joined_gates, layer_id, device_angle, row_angles):
    turned = row_angles + device_angle
    cosine = jnp.cos(turned)[None, :]
    sine = jnp.sin(turned)[None, :]
    gate_real = joined_gates[layer_id, 0]
    gate_imag = joined_gates[layer_id, 1]
    return (gate_real * cosine - gate_imag * sine, gate_real * sine + gate_imag * cosine)


def row_order(gate_layout):
    positions = jnp.arange(ROWS, dtype=jnp.int32)
    source = jnp.zeros((ROWS,), jnp.int32)
    for bit_pos in range(ROW_BITS):
        place = jnp.left_shift(jnp.ones((), jnp.int32), gate_layout[bit_pos])
        source = source + (positions >> bit_pos & 1) * place
    return source


def stacked_product(weight_real, weight_imag, block_real, block_imag):
    weights = jnp.concatenate([weight_real, weight_imag], axis=0)
    col_total = block_real.shape[1]
    row_total = weight_real.shape[0]
    inputs = jnp.concatenate([block_real, block_imag], axis=1)
    product = jnp.dot(
        weights, inputs, precision=lax.Precision.HIGHEST, preferred_element_type=jnp.float32
    )
    new_real = product[:row_total, :col_total] - product[row_total:, col_total:]
    new_imag = product[:row_total, col_total:] + product[row_total:, :col_total]
    return (new_real, new_imag)


def column_phase(new_real, new_imag, col_angles):
    cosine = jnp.cos(col_angles)[None, :]
    sine = jnp.sin(col_angles)[None, :]
    turned = jnp.stack([new_real * cosine - new_imag * sine, new_real * sine + new_imag * cosine])
    return turned[:, None]


def combine(self_real, self_imag, first, cross_real, cross_imag, second):
    new_real = (
        self_real * first[0]
        - self_imag * first[1]
        + cross_real * second[0]
        - cross_imag * second[1]
    )
    new_imag = (
        self_real * first[1]
        + self_imag * first[0]
        + cross_real * second[1]
        + cross_imag * second[0]
    )
    return jnp.stack([new_real, new_imag])


def pair_update(block, pair_gates, layer_id, bit_pos):
    own_bit = lax.axis_index("lo") >> bit_pos & 1
    other_bit = 1 - own_bit
    coeff_real = pair_gates[layer_id, 0]
    coeff_imag = pair_gates[layer_id, 1]
    partner = partner_2(block, "lo", bit_pos)
    return combine(
        coeff_real[own_bit, own_bit],
        coeff_imag[own_bit, own_bit],
        block,
        coeff_real[own_bit, other_bit],
        coeff_imag[own_bit, other_bit],
        partner,
    )


def shards(
    amplitudes,
    joined_gates,
    pair_gates,
    global_angles,
    local_phases,
    slice_bits,
    coupled_qubits,
    gate_layout,
):
    row_total = amplitudes.shape[2]
    col_total = amplitudes.shape[3]
    hi_count = lax.axis_size("hi")
    top_bit = lax.axis_size("lo").bit_length() - 2
    source = row_order(gate_layout)
    block = amplitudes
    for layer_id in range(LAYERS):
        angles = qubit_angles(local_phases, slice_bits, coupled_qubits, layer_id)
        row_angles = bit_angles(angles[COL_BITS:], ROW_BITS, ROWS)
        col_angles = bit_angles(angles, COL_BITS, COLS)
        weight_real, weight_imag = folded_gate(
            joined_gates, layer_id, global_angles[layer_id, 0], row_angles
        )
        if layer_id == 0:
            new_real, new_imag = stacked_product(weight_real, weight_imag, block[0, 0], block[1, 0])
        else:
            shaped = block.reshape(2, hi_count, row_total // hi_count, col_total)

            def apply_gate(pieces, weight_real=weight_real, weight_imag=weight_imag):
                item_count = pieces.shape[3]
                flat = pieces.reshape(2, row_total, item_count)
                part_real, part_imag = stacked_product(weight_real, weight_imag, flat[0], flat[1])
                return jnp.stack([part_real, part_imag]).reshape(2, 1, row_total, item_count)

            gated = apply_gate(
                lax.all_to_all(shaped, "hi", split_axis=1, concat_axis=1, tiled=True)
            )
            new_real = gated[0, 0]
            new_imag = gated[1, 0]
        block = column_phase(new_real, new_imag, col_angles)
        block = pair_update(block, pair_gates, layer_id, top_bit if layer_id % 2 == 0 else 0)
        if layer_id + 1 < LAYERS:
            block = jnp.take(block, source, axis=2)
    return block


def solution(mesh):
    placed = (
        P(None, ("hi", "lo"), None, None),
        P(),
        P(),
        P(None, ("hi", "lo")),
        P(),
        P(),
        P(),
        P(),
    )
    return jax.shard_map(
        shards,
        mesh=mesh,
        in_specs=placed,
        out_specs=P(None, ("hi", "lo"), None, None),
        check_vma=False,
    )
```

profile of v0, /device:TPU:0, one launch (start us, length us, event | category | flops | bytes accessed | tf_op | source)
XLA Modules:
  0.0 115.8 jit_solution(5642536331948287851)
XLA Ops:
  0.0 0.8 slice_bitcast_fusion.3
  0.8 0.7 convert_element_type.331
  1.4 0.1 select_reduce_fusion
  1.5 0.8 bitcast_add_fusion.5
  2.3 0.7 fusion.33
  3.0 0.7 fusion.35
  3.7 1.4 %fusion.34 = (f32[1,1]{0,1:T(1,128)}, f32[1,1]{0,1:T(1,128)}) fusion(f32[2,1]{0,1:T(1,128)} %param.11), kind=kLoop, calls=%fused_computation.107 | loop fusion | bytes 16 | tf_op jit(solution)/shard_map/slice | solution.py:129
  5.1 9.8 %fusion.28 = (f32[256]{0:T(256)S(1)}, f32[256]{0:T(256)S(1)}, f32[256]{0:T(256)S(1)}, f32[256]{0:T(256)S(1)}) fusion(f32[]{:T(128)} %bitcast.48, f32[]{:T(128)} %bitcast.47, f32[]{:T(128)} %bitcast.46, f32[]{:T(128)} %bitcast.45, f32[]{:T(128)} %bitcast.44, f32[]{:T(128)} %bitcast.43, f32[]{:T(128)} %bitcast.42, f32[]{:T(128)} %bitcast.41, f32[]{:T(128)} %bitcast.75, ...), kind=kLoop, calls=%fused_computation.101 | loop fusion | flops 13824 | bytes 4160 | tf_op jit(solution)/shard_map/cos | solution.py:70
  14.9 1.3 %slice_bitcast_fusion.1 = (f32[512,256]{1,0:T(8,128)S(1)}, f32[512,256]{1,0:T(8,128)S(1)}) fusion(f32[2,1,512,256]{3,2,1,0:T(8,128)} %param.8), kind=kLoop, calls=%fused_computation.53 | loop fusion | bytes 2097152 | tf_op jit(solution)/shard_map/squeeze | solution.py:132
  16.2 6.4 %fusion.24 = (f32[512]{0:T(512)S(1)}, f32[512]{0:T(512)S(1)}) fusion(f32[]{:T(128)} %bitcast.37, f32[]{:T(128)} %bitcast.36, f32[]{:T(128)} %bitcast.35, f32[]{:T(128)} %bitcast.34, f32[]{:T(128)} %bitcast.33, f32[]{:T(128)} %bitcast.32, f32[]{:T(128)} %bitcast.31, f32[]{:T(128)} %bitcast.30, f32[]{:T(128)} %bitcast.29, f32[]{:T(128)} %bitcast.28), kind=kLoop, calls=%fused_computation.97 | loop fusion | flops 23040 | bytes 4136 | tf_op jit(solution)/shard_map/sin | solution.py:41
  22.5 6.4 %fusion.22 = (f32[512]{0:T(512)S(1)}, f32[512]{0:T(512)S(1)}) fusion(f32[]{:T(128)} %bitcast.13, f32[]{:T(128)} %bitcast.12, f32[]{:T(128)} %bitcast.11, f32[]{:T(128)} %bitcast.10, f32[]{:T(128)} %bitcast.9, f32[]{:T(128)} %bitcast.8, f32[]{:T(128)} %bitcast.7, f32[]{:T(128)} %bitcast.6, f32[]{:T(128)} %bitcast.5, f32[]{:T(128)} %bitcast.4), kind=kLoop, calls=%fused_computation.95 | loop fusion | flops 23040 | bytes 4136 | tf_op jit(solution)/shard_map/sin | solution.py:41
  28.9 2.9 %fusion.14 = (f32[512,512]{1,0:T(8,128)S(1)}, f32[512,512]{1,0:T(8,128)S(1)}, f32[512,512]{1,0:T(8,128)S(1)}, f32[512,512]{1,0:T(8,128)S(1)}) fusion(f32[2,2,512,512]{3,2,1,0:T(8,128)} %param.9, f32[512]{0:T(512)S(1)} %get-tuple-element.92, f32[512]{0:T(512)S(1)} %get-tuple-element.93, f32[512]{0:T(512)S(1)} %get-tuple-element.91, f32[512]{0:T(512)S(1)} %get-tuple-element.90), kind=kLoop, calls=%fused_computation.21 | loop fusion | flops 3145728 | bytes 8396800 | tf_op jit(solution)/shard_map/sub | solution.py:44
  31.8 3.4 %fusion.4 = f32[1024,512]{1,0:T(8,128)S(1)} fusion(f32[512,512]{1,0:T(8,128)S(1)} %get-tuple-element.12, f32[512,512]{1,0:T(8,128)S(1)} %get-tuple-element.11, f32[512,256]{1,0:T(8,128)S(1)} %get-tuple-element.28, f32[512,256]{1,0:T(8,128)S(1)} %get-tuple-element.27), kind=kOutput, calls=%fused_computation.5 | convolution fusion | flops 3222011904 | bytes 5242880 | tf_op jit(solution)/shard_map/dot_general | solution.py:61
  35.2 0.0 copy-start
  35.2 0.0 copy-start.1
  35.3 0.2 multiply_add_fusion.1
  35.4 1.0 maximum_bitcast_fusion
  36.5 2.9 %collective-permute-start = (f32[2,1,512,256]{3,2,0,1:T(8,128)}, f32[2,1,512,256]{3,2,0,1:T(8,128)}, u32[]{:S(2)}, u32[]{:S(2)}) collective-permute-start(f32[2,1,512,256]{3,2,0,1:T(8,128)} %maximum_bitcast_fusion), channel_id=1, source_target_pairs={{0,2},{1,3},{2,0},{3,1},{4,6},{5,7},{6,4},{7,5},{8,10},{9,11},{10,... | collective-permute-start | bytes 3145736 | tf_op jit(solution)/shard_map/ppermute | solution.py:19
  39.4 0.0 copy-done
  39.4 0.7 fusion.32
  45.6 0.0 copy-done.1
  45.6 0.7 constant_dynamic-slice_fusion.2
  46.3 0.7 constant_dynamic-slice_fusion.6
  47.1 15.8 %collective-permute-done = f32[2,1,512,256]{3,2,0,1:T(8,128)} collective-permute-done((f32[2,1,512,256]{3,2,0,1:T(8,128)}, f32[2,1,512,256]{3,2,0,1:T(8,128)}, u32[]{:S(2)}, u32[]{:S(2)}) %collective-permute-start) | collective-permute-done | bytes 1048608 | tf_op jit(solution)/shard_map/ppermute | solution.py:19
  62.9 3.8 %fusion.21 = (f32[1,1,512,256]{3,2,1,0:T(8,128)S(1)}, f32[1,1,512,256]{3,2,1,0:T(8,128)S(1)}) fusion(f32[512,256]{1,0:T(8,128)S(1)} %get-tuple-element.23, f32[512,256]{1,0:T(8,128)S(1)} %get-tuple-element.24, f32[2,1,512,256]{3,2,1,0:T(8,128)} %bitcast.58, f32[2,1,512,256]{3,2,0,1:T(8,128)} %collective-permute-done, f32[]{:T(128)} %bitcast.56, f32[]{:T(128)} %bitcast.50, ...), kind=kLoop, calls=%fused_computation.45 | loop fusion | flops 1835008 | bytes 3148288 | tf_op jit(solution)/shard_map/stack | solution.py:89
  66.7 0.1 maximum_bitcast_fusion.1
  66.8 0.8 copy.27
  67.6 3.1 %gather_fusion = f32[512,2,256]{2,1,0:T(2,128)} fusion(f32[2,512,256]{2,0,1:T(2,128)S(1)} %copy.27, s32[1024]{0:T(1024)S(1)} %pad_clamp_fusion), kind=kCustom, calls=%fused_computation | custom fusion | bytes 2099200 | tf_op jit(solution)/shard_map/jit(_take)/gather | solution.py:150
  70.7 2.5 %broadcast_select_fusion = f32[2,8,64,256]{3,0,2,1:T(2,128)} fusion(f32[2,8,64,256]{3,0,2,1:T(2,128)} %bitcast.155, pred[8,64]{1,0:T(8,128)(4,1)S(1)} %compare_and_fusion), kind=kLoop, calls=%fused_computation.31 | loop fusion | flops 262144 | bytes 2097664 | tf_op jit(solution)/shard_map/jit(_take)/select_n | solution.py:150
  73.3 6.1 %all-to-all-start = ((f32[2,8,64,256]{3,0,2,1:T(2,128)}), f32[2,8,64,256]{3,0,2,1:T(2,128)S(1)}, u32[]{:S(2)}, u32[]{:S(2)}) async-start(f32[2,8,64,256]{3,0,2,1:T(2,128)} %broadcast_select_fusion), calls=%async_computation | async-start | bytes 2097152 | tf_op jit(solution)/shard_map/all_to_all | solution.py:143
  79.4 25.1 %all-to-all-done = f32[2,8,64,256]{3,0,2,1:T(2,128)S(1)} async-done(((f32[2,8,64,256]{3,0,2,1:T(2,128)}), f32[2,8,64,256]{3,0,2,1:T(2,128)S(1)}, u32[]{:S(2)}, u32[]{:S(2)}) %all-to-all-start) | async-done | bytes 1048608 | tf_op jit(solution)/shard_map/all_to_all | solution.py:143
  104.5 1.0 fusion.30
  105.6 3.4 %fusion = f32[1024,512]{1,0:T(8,128)S(1)} fusion(f32[512,512]{1,0:T(8,128)S(1)} %get-tuple-element.15, f32[512,512]{1,0:T(8,128)S(1)} %get-tuple-element.16, f32[512,256]{1,0:T(8,128)S(1)} %bitcast.156, f32[512,256]{1,0:T(8,128)S(1)} %bitcast.157), kind=kOutput, calls=%fused_computation.1 | convolution fusion | flops 3222011904 | bytes 5242880 | tf_op jit(solution)/shard_map/dot_general | solution.py:61
  109.0 0.2 multiply_add_fusion
  109.2 0.1 maximum_bitcast_fusion.2
  109.3 0.1 collective-permute-start.1
  109.3 2.6 %collective-permute-done.1 = f32[2,1,512,256]{3,2,0,1:T(8,128)S(1)} collective-permute-done((f32[2,1,512,256]{3,2,0,1:T(8,128)S(1)}, f32[2,1,512,256]{3,2,0,1:T(8,128)S(1)}, u32[]{:S(2)}, u32[]{:S(2)}) %collective-permute-start.1) | collective-permute-done | bytes 1048608 | tf_op jit(solution)/shard_map/ppermute | solution.py:19
  112.0 2.7 %fusion.19 = (f32[1,1,512,256]{3,2,1,0:T(8,128)S(1)}, f32[1,1,512,256]{3,2,1,0:T(8,128)S(1)}) fusion(f32[512,256]{1,0:T(8,128)S(1)} %get-tuple-element.21, f32[512,256]{1,0:T(8,128)S(1)} %get-tuple-element.22, f32[2,1,512,256]{3,2,1,0:T(8,128)S(1)} %bitcast.158, f32[2,1,512,256]{3,2,0,1:T(8,128)S(1)} %collective-permute-done.1, f32[]{:T(128)} %bitcast.83, ...), kind=kLoop, calls=%fused_computation.40 | loop fusion | flops 1835008 | bytes 3148288 | tf_op jit(solution)/shard_map/sub | solution.py:78
  114.7 1.0 pad_maximum_fusion
  (8 shorter events, 0.2 us)
Async XLA Ops:
  35.2 4.2 %copy-start = (s32[9]{0:T(128)S(1)}, s32[9]{0:T(128)}, u32[]{:S(2)}) copy-start(s32[9]{0:T(128)} %param.15) | copy-start | bytes 112
  35.2 10.4 %copy-start.1 = (f32[2,2,2,2]{3,2,1,0:T(2,128)S(1)}, f32[2,2,2,2]{3,2,1,0:T(2,128)}, u32[]{:S(2)}) copy-start(f32[2,2,2,2]{3,2,1,0:T(2,128)} %param.10) | copy-start | bytes 196
  36.5 26.4 %collective-permute-start = (f32[2,1,512,256]{3,2,0,1:T(8,128)}, f32[2,1,512,256]{3,2,0,1:T(8,128)}, u32[]{:S(2)}, u32[]{:S(2)}) collective-permute-start(f32[2,1,512,256]{3,2,0,1:T(8,128)} %maximum_bitcast_fusion), channel_id=1, source_target_pairs={{0,2},{1,3},{2,0},{3,1},{4,6},{5,7},{6,4},{7,5},{8,10},{9,11},{10,... | collective-permute-start | bytes 3145736 | tf_op jit(solution)/shard_map/ppermute | solution.py:19
  73.3 31.2 %all-to-all-start = ((f32[2,8,64,256]{3,0,2,1:T(2,128)}), f32[2,8,64,256]{3,0,2,1:T(2,128)S(1)}, u32[]{:S(2)}, u32[]{:S(2)}) async-start(f32[2,8,64,256]{3,0,2,1:T(2,128)} %broadcast_select_fusion), calls=%async_computation | async-start | bytes 2097152 | tf_op jit(solution)/shard_map/all_to_all | solution.py:143
  109.3 2.7 %collective-permute-start.1 = (f32[2,1,512,256]{3,2,0,1:T(8,128)S(1)}, f32[2,1,512,256]{3,2,0,1:T(8,128)S(1)}, u32[]{:S(2)}, u32[]{:S(2)}) collective-permute-start(f32[2,1,512,256]{3,2,0,1:T(8,128)S(1)} %maximum_bitcast_fusion.2), channel_id=1, source_target_pairs={{0,1},{1,0},{2,3},{3,2},{4,5},{5,4},{6,7},{7,6},{8,9},{9,8},{10,11... | collective-permute-start | bytes 3145736 | tf_op jit(solution)/shard_map/ppermute | solution.py:19
where the time goes:
time: 117 us; the launch traced here: 116 us
  waiting for transfers between devices  43.5 us (37%)
  other arithmetic  38.6 us (33%)
  local copies, waits for them, and re-layouts  12 us (10%)
  starting transfers between devices  9.09 us (8%)
  matrix products  6.89 us (6%)
  between operations  5.71 us (5%)
    all_to_all x1, waiting for transfers between devices, shards(): lax.all_to_all(shaped, 'hi', split_axis=1, concat_axis=1, tiled=True)  25.1 us
    ppermute x2, waiting for transfers between devices, partner_2(): return lax.ppermute(value, axis, pairs)  18.5 us
    sin x2, other arithmetic, folded_gate(): sine = jnp.sin(turned)[None, :]  12.7 us
    cos x1, other arithmetic, column_phase(): cosine = jnp.cos(col_angles)[None, :]  9.78 us
    dot_general x2, matrix products, stacked_product(): jnp.dot(weights, inputs, precision=lax.Precision.HIGHEST, preferred_eleme...  6.89 us
    all_to_all x1, starting transfers between devices, shards(): lax.all_to_all(shaped, 'hi', split_axis=1, concat_axis=1, tiled=True)  6.08 us
    another operation x3, other arithmetic, combine(): return jnp.stack([new_real, new_imag])  4.94 us
    gather x1, local copies, waits for them, and re-layouts, shards(): block = jnp.take(block, source, axis=2)  3.12 us
  transfers between devices with their start and end apart: 3, of which 3 were waited for; matrix products, arithmetic and copies ran while one was open for 2% of the time, Pallas kernels for 0%

commit v1 on v0

v1 whole, which is shorter than its diff:
```python
import functools

import jax
import jax.numpy as jnp
from jax import lax
from jax.experimental import pallas as pl
from jax.experimental.pallas import tpu as pltpu
from jax.sharding import PartitionSpec as P

F32 = jnp.float32
BF16 = jnp.bfloat16
VMEM_BYTES = 32 * 1024 * 1024


def sincos(x):
    turns = jnp.floor(x * 0.6366197723675814 + 0.5)
    r = x - turns * 1.5703125
    r = r - turns * 4.837512969970703125e-4
    r = r - turns * 7.54978995489188216e-8
    z = r * r
    sine = r + r * z * ((-1.9515295891e-4 * z + 8.3321608736e-3) * z - 1.6666654611e-1)
    cosine = 1.0 - 0.5 * z + z * z * (
        (2.443315711809948e-5 * z - 1.388731625493765e-3) * z + 4.166664568298827e-2
    )
    quarter = turns.astype(jnp.int32) & 3
    odd = (quarter & 1) == 1
    new_sine = jnp.where(odd, cosine, sine)
    new_cosine = jnp.where(odd, sine, cosine)
    new_sine = jnp.where((quarter & 2) == 2, -new_sine, new_sine)
    new_cosine = jnp.where(((quarter + 1) & 2) == 2, -new_cosine, new_cosine)
    return new_cosine, new_sine


def qubit_factors(layer, phases_ref, bits_ref, coupled_ref):
    qubits = phases_ref.shape[1]
    lane = lax.broadcasted_iota(jnp.int32, (1, qubits), 1)
    odd = jnp.zeros((1, qubits), jnp.int32)
    for f in range(bits_ref.shape[0]):
        odd = odd ^ jnp.where(lane == coupled_ref[layer, f], bits_ref[f], 0)
    sign = 1.0 - 2.0 * odd.astype(F32)
    cosine, sine = sincos(phases_ref[layer : layer + 1, :])
    return cosine * sign, sine * sign


def turn(real, imag, cosine, sine):
    return real * cosine - imag * sine, real * sine + imag * cosine


def row_phases(cosine, sine, first, row_bits, base_real, base_imag):
    sub = lax.broadcasted_iota(jnp.int32, (8, 128), 0)
    real = jnp.broadcast_to(base_real, (8, 128))
    imag = jnp.broadcast_to(base_imag, (8, 128))
    for k in range(row_bits):
        c = cosine[:, first + k : first + k + 1]
        s = sine[:, first + k : first + k + 1]
        if k < 3:
            chosen = ((sub >> k) & 1) == 1
            real, imag = turn(real, imag, jnp.where(chosen, c, 1.0), jnp.where(chosen, s, 0.0))
        else:
            up_real, up_imag = turn(real, imag, c, s)
            real = jnp.concatenate([real, up_real], axis=0)
            imag = jnp.concatenate([imag, up_imag], axis=0)
    return real, imag


def col_phases(cosine, sine, col_bits, cols):
    lane = lax.broadcasted_iota(jnp.int32, (1, cols), 1)
    real = jnp.ones((1, cols), F32)
    imag = jnp.zeros((1, cols), F32)
    for k in range(col_bits):
        chosen = ((lane >> k) & 1) == 1
        c = cosine[:, k : k + 1]
        s = sine[:, k : k + 1]
        real, imag = turn(real, imag, jnp.where(chosen, c, 1.0), jnp.where(chosen, s, 0.0))
    return real, imag


def split(x):
    high = x.astype(BF16)
    low = (x - high.astype(F32)).astype(BF16)
    return high, low


def dot(a, b):
    return jnp.dot(a, b, preferred_element_type=F32)


def turned_rows(real, imag, phase_real, phase_imag):
    reps = real.shape[1] // phase_real.shape[1]
    phase_real = jnp.concatenate([phase_real] * reps, axis=1)
    phase_imag = jnp.concatenate([phase_imag] * reps, axis=1)
    real, imag = turn(real, imag, phase_real, phase_imag)
    real_high, real_low = split(real)
    imag_high, imag_low = split(imag)

    def block(r, i):
        return jnp.concatenate(
            [jnp.concatenate([r, i], axis=1), jnp.concatenate([-i, r], axis=1)], axis=0
        )

    return block(real_high, imag_high), block(real_low, imag_low)


def product(left_high, left_low, right_high, right_low):
    return dot(left_high, right_high) + dot(left_high, right_low) + dot(left_low, right_high)


def first_gate_kernel(
    groups,
    piece_rows,
    col_bits,
    amplitudes_ref,
    gates_ref,
    phases_ref,
    angles_ref,
    bits_ref,
    coupled_ref,
    layout_ref,
    *out_refs,
):
    me = lax.axis_index("hi")
    rows = amplitudes_ref.shape[2]
    cols = amplitudes_ref.shape[3]
    row_bits = rows.bit_length() - 1
    cosine, sine = qubit_factors(0, phases_ref, bits_ref, coupled_ref)
    base_real, base_imag = sincos(angles_ref[0:1, 0:1])
    phase_real, phase_imag = row_phases(cosine, sine, col_bits, row_bits, base_real, base_imag)
    right_high, right_low = turned_rows(
        amplitudes_ref[0, 0], amplitudes_ref[1, 0], phase_real, phase_imag
    )
    sub = lax.broadcasted_iota(jnp.int32, (8, 128), 0)
    inner = jnp.zeros((8, 128), jnp.int32)
    inner_bits = piece_rows.bit_length() - 1
    for k in range(inner_bits):
        place = jnp.left_shift(jnp.int32(1), layout_ref[k])
        if k < 3:
            inner = inner + ((sub >> k) & 1) * place
        else:
            inner = jnp.concatenate([inner, inner + place], axis=0)
    places = []
    for group in groups:
        for step in group:
            block = me ^ step
            base = jnp.int32(0)
            for k in range(inner_bits, row_bits):
                base = base + jnp.left_shift((block >> (k - inner_bits)) & 1, layout_ref[k])
            places.append(inner + base)
    places = jnp.concatenate(places, axis=0)
    lane = lax.broadcasted_iota(jnp.int32, places.shape, 1)
    chosen = jnp.concatenate(
        [
            jnp.where(places == lane + start, 1.0, 0.0).astype(BF16)
            for start in range(0, rows, 128)
        ],
        axis=1,
    )
    gate_real_high, gate_real_low = split(gates_ref[0, 0])
    gate_imag_high, gate_imag_low = split(gates_ref[0, 1])
    left_high = dot(chosen, jnp.concatenate([gate_real_high, gate_imag_high], axis=1)).astype(BF16)
    left_low = dot(chosen, jnp.concatenate([gate_real_low, gate_imag_low], axis=1)).astype(BF16)
    out = product(left_high, left_low, right_high, right_low)
    start = 0
    for group, out_ref in zip(groups, out_refs, strict=True):
        size = len(group) * piece_rows
        out_ref[0] = out[start : start + size, :cols]
        out_ref[1] = out[start : start + size, cols:]
        start += size


def smem():
    return pl.BlockSpec(memory_space=pltpu.SMEM)


def vmem():
    return pl.BlockSpec(memory_space=pltpu.VMEM)


def first_gate(groups, piece_rows, col_bits, amplitudes, gates, phases, angles, bits, coupled, layout):
    cols = amplitudes.shape[3]
    whole = lambda a: pl.BlockSpec(a.shape, lambda i: (0,) * a.ndim)
    shapes = [
        jax.ShapeDtypeStruct((2, len(group) * piece_rows, cols), F32) for group in groups
    ]
    return pl.pallas_call(
        functools.partial(first_gate_kernel, groups, piece_rows, col_bits),
        grid=(1,),
        out_shape=shapes,
        in_specs=[
            whole(amplitudes),
            pl.BlockSpec((1,) + gates.shape[1:], lambda i: (0, 0, 0, 0)),
            whole(phases),
            whole(angles),
            smem(),
            smem(),
            smem(),
        ],
        out_specs=[pl.BlockSpec(s.shape, lambda i: (0, 0, 0)) for s in shapes],
        compiler_params=pltpu.CompilerParams(vmem_limit_bytes=VMEM_BYTES),
        name="first_gate",
    )(amplitudes, gates, phases, angles, bits, coupled, layout)


def pair_coefficients(pair_ref, layer, bit):
    own = bit
    other = 1 - bit
    return (
        pair_ref[layer, 0, own, own],
        pair_ref[layer, 1, own, own],
        pair_ref[layer, 0, own, other],
        pair_ref[layer, 1, own, other],
    )


def combined(own, other, c):
    own_real, own_imag = turn(own[0], own[1], c[0], c[1])
    other_real, other_imag = turn(other[0], other[1], c[2], c[3])
    return own_real + other_real, own_imag + other_imag


def combine_kernel(top_bit, own_ref, other_ref, pair_ref, *out_refs):
    bit = (lax.axis_index("lo") >> top_bit) & 1
    c = pair_coefficients(pair_ref, 0, bit)
    size = out_refs[0].shape[1]
    for i, out_ref in enumerate(out_refs):
        rows = slice(i * size, (i + 1) * size)
        out_ref[0], out_ref[1] = combined(
            (own_ref[0, rows], own_ref[1, rows]), (other_ref[0, rows], other_ref[1, rows]), c
        )


def combine(top_bit, count, own, other, pair_gates):
    shape = (2, own.shape[1] // count, own.shape[2])
    return pl.pallas_call(
        functools.partial(combine_kernel, top_bit),
        out_shape=[jax.ShapeDtypeStruct(shape, F32)] * count,
        in_specs=[vmem(), vmem(), smem()],
        out_specs=[vmem()] * count,
        compiler_params=pltpu.CompilerParams(vmem_limit_bytes=VMEM_BYTES),
        name="combine",
    )(own, other, pair_gates)


def second_gate_kernel(
    exchanged,
    ready,
    piece_rows,
    col_bits,
    top_bit,
    gates_ref,
    phases_ref,
    angles_ref,
    bits_ref,
    coupled_ref,
    pair_ref,
    *refs,
):
    me = lax.axis_index("hi")
    bit = (lax.axis_index("lo") >> top_bit) & 1
    c = pair_coefficients(pair_ref, 0, bit)
    out_ref, real_ref, imag_ref = refs[-3:]
    rows, cols = real_ref.shape
    row_bits = rows.bit_length() - 1
    position = 0

    def place(step, real, imag):
        start = pl.multiple_of((me ^ step) * piece_rows, piece_rows)
        real_ref[pl.ds(start, piece_rows), :] = real
        imag_ref[pl.ds(start, piece_rows), :] = imag

    for group in exchanged:
        own_ref, other_ref = refs[position : position + 2]
        position += 2
        for i, step in enumerate(group):
            part = slice(i * piece_rows, (i + 1) * piece_rows)
            place(
                step,
                *combined(
                    (own_ref[0, part], own_ref[1, part]),
                    (other_ref[0, part], other_ref[1, part]),
                    c,
                ),
            )
    for step in ready:
        place(step, refs[position][0], refs[position][1])
        position += 1
    cosine, sine = qubit_factors(1, phases_ref, bits_ref, coupled_ref)
    base_real, base_imag = sincos(angles_ref[1:2, 0:1])
    phase_real, phase_imag = row_phases(cosine, sine, col_bits, row_bits, base_real, base_imag)
    right_high, right_low = turned_rows(real_ref[...], imag_ref[...], phase_real, phase_imag)
    gate_real_high, gate_real_low = split(gates_ref[0, 0])
    gate_imag_high, gate_imag_low = split(gates_ref[0, 1])
    out = product(
        jnp.concatenate([gate_real_high, gate_imag_high], axis=1),
        jnp.concatenate([gate_real_low, gate_imag_low], axis=1),
        right_high,
        right_low,
    )
    out_ref[0] = out[:, :cols]
    out_ref[1] = out[:, cols:]


def second_gate(
    exchanged, ready, piece_rows, col_bits, top_bit, gates, phases, angles, bits, coupled, pair, arrays
):
    rows = gates.shape[2]
    cols = arrays[0].shape[2]
    whole = lambda a: pl.BlockSpec(a.shape, lambda i: (0,) * a.ndim)
    return pl.pallas_call(
        functools.partial(second_gate_kernel, exchanged, ready, piece_rows, col_bits, top_bit),
        grid=(1,),
        out_shape=jax.ShapeDtypeStruct((2, rows, cols), F32),
        in_specs=[
            pl.BlockSpec((1,) + gates.shape[1:], lambda i: (1, 0, 0, 0)),
            whole(phases),
            whole(angles),
            smem(),
            smem(),
            smem(),
        ]
        + [whole(a) for a in arrays],
        out_specs=pl.BlockSpec((2, rows, cols), lambda i: (0, 0, 0)),
        scratch_shapes=[pltpu.VMEM((rows, cols), F32)] * 2,
        compiler_params=pltpu.CompilerParams(vmem_limit_bytes=VMEM_BYTES),
        name="second_gate",
    )(gates, phases, angles, bits, coupled, pair, *arrays)


def last_kernel(col_bits, own_ref, other_ref, phases_ref, bits_ref, coupled_ref, pair_ref, out_ref):
    bit = lax.axis_index("lo") & 1
    cols = own_ref.shape[2]
    first_real, first_imag = col_phases(
        *qubit_factors(0, phases_ref, bits_ref, coupled_ref), col_bits, cols
    )
    second_real, second_imag = col_phases(
        *qubit_factors(1, phases_ref, bits_ref, coupled_ref), col_bits, cols
    )
    phase_real, phase_imag = turn(first_real, first_imag, second_real, second_imag)
    c = pair_coefficients(pair_ref, 1, bit)
    c = turn(phase_real, phase_imag, c[0], c[1]) + turn(phase_real, phase_imag, c[2], c[3])
    out_ref[0, 0], out_ref[1, 0] = combined(own_ref, other_ref, c)


def last(col_bits, own, other, phases, bits, coupled, pair):
    rows, cols = own.shape[1:]
    return pl.pallas_call(
        functools.partial(last_kernel, col_bits),
        out_shape=jax.ShapeDtypeStruct((2, 1, rows, cols), F32),
        in_specs=[vmem(), vmem(), vmem(), smem(), smem(), smem()],
        out_specs=vmem(),
        compiler_params=pltpu.CompilerParams(vmem_limit_bytes=VMEM_BYTES),
        name="last",
    )(own, other, phases, bits, coupled, pair)


def swap(value, axis, mask):
    return lax.ppermute(value, axis, [(i, i ^ mask) for i in range(lax.axis_size(axis))])


def shards(amplitudes, gates, pair, angles, phases, bits, coupled, layout):
    rows = amplitudes.shape[2]
    cols = amplitudes.shape[3]
    col_bits = cols.bit_length() - 1
    count = lax.axis_size("hi")
    piece_rows = rows // count
    top_bit = lax.axis_size("lo").bit_length() - 2
    quarter = count // 4
    near = tuple(range(1, 2 * quarter))
    far = tuple(range(2 * quarter, 3 * quarter))
    early = tuple(range(3 * quarter, count))
    first = functools.partial(
        first_gate,
        piece_rows=piece_rows,
        col_bits=col_bits,
        amplitudes=amplitudes,
        gates=gates,
        phases=phases,
        angles=angles,
        bits=bits,
        coupled=coupled,
        layout=layout,
    )
    cross = functools.partial(swap, axis="lo", mask=1 << top_bit)
    *far_parts, early_part = first(tuple((d,) for d in far) + (early,))
    far_parts = [swap(part, "hi", d) for part, d in zip(far_parts, far, strict=True)]
    early_other = cross(early_part)
    own_part, *near_parts = first(((0,),) + tuple((d,) for d in near))
    early_parts = combine(top_bit, len(early), early_part, early_other, pair)
    early_parts = [swap(part, "hi", d) for part, d in zip(early_parts, early, strict=True)]
    near_parts = [swap(part, "hi", d) for part, d in zip(near_parts, near, strict=True)]
    own_other = cross(own_part)
    near_part = jnp.concatenate(near_parts, axis=1)
    near_other = cross(near_part)
    far_part = jnp.concatenate(far_parts, axis=1)
    far_other = cross(far_part)
    gated = second_gate(
        ((0,), near, far),
        early,
        piece_rows,
        col_bits,
        top_bit,
        gates,
        phases,
        angles,
        bits,
        coupled,
        pair,
        [own_part, own_other, near_part, near_other, far_part, far_other, *early_parts],
    )
    return last(col_bits, gated, swap(gated, "lo", 1), phases, bits, coupled, pair)


def solution(mesh):
    placed = (
        P(None, ("hi", "lo"), None, None),
        P(),
        P(),
        P(None, ("hi", "lo")),
        P(),
        P(),
        P(),
        P(),
    )
    return jax.shard_map(
        shards,
        mesh=mesh,
        in_specs=placed,
        out_specs=P(None, ("hi", "lo"), None, None),
        check_vma=False,
    )
```

time: 117 us -> 53.6 us (0.46)
  other arithmetic: 38.6 us -> 0 us
  waiting for transfers between devices: 43.5 us -> 18.6 us
  Pallas kernels: 0 us -> 10.6 us
  starting transfers between devices: 9.09 us -> 17.1 us
  matrix products: 6.89 us -> 0 us
  between operations: 5.71 us -> 0.11 us
  local copies, waits for them, and re-layouts: 12 us -> 6.88 us
    all_to_all x1 -> x0, waiting for transfers between devices: 25.1 us -> none  [shards(): lax.all_to_all(shaped, 'hi', split_axis=1, concat_axis=1, tiled=True)]
    ppermute x2 -> x12, starting transfers between devices: 3.01 us -> 17.1 us  [swap(): lax.ppermute(value, axis, [(i, i ^ mask) for i in range(lax.axis_size(axi...]
    sin x2 -> x0, other arithmetic: 12.7 us -> none  [folded_gate(): sine = jnp.sin(turned)[None, :]]
    pallas_call x0 -> x5, Pallas kernels: none -> 10.6 us  [the longest x2 4.63 us: first_gate(): pl.pallas_call(functools.partial(first_gate_kernel, groups, piece_rows, c...]
    cos x1 -> x0, other arithmetic: 9.78 us -> none  [column_phase(): cosine = jnp.cos(col_angles)[None, :]]
    dot_general x2 -> x0, matrix products: 6.89 us -> none  [stacked_product(): jnp.dot(weights, inputs, precision=lax.Precision.HIGHEST, preferred_eleme...]
    unnamed x6 -> x20, local copies, waits for them, and re-layouts: 0.08 us -> 6.86 us
    all_to_all x1 -> x0, starting transfers between devices: 6.08 us -> none  [shards(): lax.all_to_all(shaped, 'hi', split_axis=1, concat_axis=1, tiled=True)]
  transfers between devices with their start and end apart: 3 -> 12, of which waited for: 3 -> 5; matrix products, arithmetic and copies ran while one was open for 2% -> 0% of each run, Pallas kernels for 0% -> 6%
where the time goes in v1:
time: 53.6 us; the launch traced here: 53.3 us
  waiting for transfers between devices  18.6 us (35%)
  starting transfers between devices  17.1 us (32%)
  Pallas kernels  10.6 us (20%)
  local copies, waits for them, and re-layouts  6.88 us (13%)
    ppermute x12, waiting for transfers between devices, swap(): lax.ppermute(value, axis, [(i, i ^ mask) for i in range(lax.axis_size(axi...  18.6 us
    ppermute x12, starting transfers between devices, swap(): lax.ppermute(value, axis, [(i, i ^ mask) for i in range(lax.axis_size(axi...  17.1 us
    unnamed x20, local copies, waits for them, and re-layouts  6.86 us
    pallas_call x2, Pallas kernels, first_gate(): pl.pallas_call(functools.partial(first_gate_kernel, groups, piece_rows, c...  4.63 us
    pallas_call x1, Pallas kernels, second_gate(): pl.pallas_call(functools.partial(second_gate_kernel, exchanged, ready, pi...  2.99 us
    pallas_call x1, Pallas kernels, last(): pl.pallas_call(functools.partial(last_kernel, col_bits), out_shape=jax.Sh...  2.3 us
  transfers between devices with their start and end apart: 12, of which 5 were waited for; matrix products, arithmetic and copies ran while one was open for 0% of the time, Pallas kernels for 6%

profile of v1, /device:TPU:0, one launch (start us, length us, event | category | flops | bytes accessed | tf_op | source)
XLA Modules:
  0.0 53.3 jit_solution(11949870832219791654)
XLA Ops:
  0.0 0.7 %copy.11.angles_ref = f32[2,1]{1,0:T(2,128)S(1)} copy(f32[2,1]{0,1:T(1,128)} %param.11) | data formatting | bytes 16 | tf_op args[3]
  0.7 0.0 copy-start
  0.7 2.2 %copy-done = f32[2,2,512,512]{3,2,1,0:T(8,128)S(1)} copy-done((f32[2,2,512,512]{3,2,1,0:T(8,128)S(1)}, f32[2,2,512,512]{3,2,1,0:T(8,128)}, u32[]{:S(2)}) %copy-start) | copy-done | bytes 4194328
  2.9 0.0 copy-start.2
  2.9 1.2 %copy-done.2 = f32[2,1,512,256]{3,2,1,0:T(8,128)S(1)} copy-done((f32[2,1,512,256]{3,2,1,0:T(8,128)S(1)}, f32[2,1,512,256]{3,2,1,0:T(8,128)}, u32[]{:S(2)}) %copy-start.2) | copy-done | bytes 1048600
  4.2 0.0 copy-start.4
  4.2 0.7 %copy-done.4 = f32[2,17]{1,0:T(2,128)S(1)} copy-done((f32[2,17]{1,0:T(2,128)S(1)}, f32[2,17]{1,0:T(2,128)}, u32[]{:S(2)}) %copy-start.4) | copy-done | bytes 160
  4.8 0.0 copy-start.5
  4.8 0.7 %copy-done.5 = s32[2,17]{1,0:T(2,128)S(1)} copy-done((s32[2,17]{1,0:T(2,128)S(1)}, s32[2,17]{1,0:T(2,128)}, u32[]{:S(2)}) %copy-start.5) | copy-done | bytes 160
  5.5 0.0 copy-start.6
  5.5 0.7 %copy-done.6 = s32[17]{0:T(128)S(1)} copy-done((s32[17]{0:T(128)S(1)}, s32[17]{0:T(128)}, u32[]{:S(2)}) %copy-start.6) | copy-done | bytes 92
  6.2 0.0 copy-start.7
  6.2 0.7 %copy-done.7 = s32[9]{0:T(128)S(1)} copy-done((s32[9]{0:T(128)S(1)}, s32[9]{0:T(128)}, u32[]{:S(2)}) %copy-start.7) | copy-done | bytes 60
  6.8 2.3 %first_gate.2 = (f32[2,64,256]{2,1,0:T(8,128)S(1)}, f32[2,64,256]{2,1,0:T(8,128)S(1)}, f32[2,64,256]{2,1,0:T(8,128)S(1)}, f32[2,64,256]{2,1,0:T(8,128)S(1)}) custom-call(f32[2,1,512,256]{3,2,1,0:T(8,128)S(1)} %copy-done.2, f32[2,2,512,512]{3,2,1,0:T(8,128)S(1)} %copy-done, f32[2,17]{1,0:T(2,128)S(1)} %copy-done.4, f32[2,1]{1,0:T(2,128)S(1)} %copy.11.angles_ref, ...), custom_call_target="tpu_custom_call" | custom-call | tf_op jit(solution)/shard_map/first_gate/pallas_call | solution.py:184
  9.2 0.0 copy-start.3
  9.2 0.0 copy-start.1
  9.2 3.0 %collective-permute-start.1 = (f32[2,64,256]{2,1,0:T(8,128)S(1)}, f32[2,64,256]{2,1,0:T(8,128)S(1)}, u32[]{:S(2)}, u32[]{:S(2)}) collective-permute-start(f32[2,64,256]{2,1,0:T(8,128)S(1)} %get-tuple-element.15), channel_id=1, source_target_pairs={{0,4},{4,0},{8,12},{12,8},{16,20},{20,16},{24,28},{28,24},{1,5},{5... | collective-permute-start | bytes 393224 | tf_op jit(solution)/shard_map/ppermute | solution.py:356
  12.2 1.6 %collective-permute-start.2 = (f32[2,64,256]{2,1,0:T(8,128)S(1)}, f32[2,64,256]{2,1,0:T(8,128)S(1)}, u32[]{:S(2)}, u32[]{:S(2)}) collective-permute-start(f32[2,64,256]{2,1,0:T(8,128)S(1)} %get-tuple-element.16), channel_id=1, source_target_pairs={{0,8},{4,12},{8,0},{12,4},{16,24},{20,28},{24,16},{28,20},{1,9},{5... | collective-permute-start | bytes 393224 | tf_op jit(solution)/shard_map/ppermute | solution.py:356
  13.8 0.0 collective-permute-start.3
  13.8 2.3 %first_gate.3 = (f32[2,64,256]{2,1,0:T(8,128)S(1)}, f32[2,64,256]{2,1,0:T(8,128)S(1)}, f32[2,128,256]{2,1,0:T(8,128)S(1)}) custom-call(f32[2,1,512,256]{3,2,1,0:T(8,128)S(1)} %copy-done.2, f32[2,2,512,512]{3,2,1,0:T(8,128)S(1)} %copy-done, f32[2,17]{1,0:T(2,128)S(1)} %copy-done.4, f32[2,1]{1,0:T(2,128)S(1)} %copy.11.angles_ref, s32[17]{0:T(128)S(1)} %copy-done.6, ...), custom_call_target="tpu_custom_call" | custom-call | tf_op jit(solution)/shard_map/first_gate/pallas_call | solution.py:184
  16.1 3.1 %collective-permute-start.5 = (f32[2,64,256]{2,1,0:T(8,128)S(1)}, f32[2,64,256]{2,1,0:T(8,128)S(1)}, u32[]{:S(2)}, u32[]{:S(2)}) collective-permute-start(f32[2,64,256]{2,1,0:T(8,128)S(1)} %get-tuple-element.18), channel_id=1, source_target_pairs={{0,16},{4,20},{8,24},{12,28},{16,0},{20,4},{24,8},{28,12},{1,17},{... | collective-permute-start | bytes 393224 | tf_op jit(solution)/shard_map/ppermute | solution.py:356
  19.2 1.3 %collective-permute-start.6 = (f32[2,64,256]{2,1,0:T(8,128)S(1)}, f32[2,64,256]{2,1,0:T(8,128)S(1)}, u32[]{:S(2)}, u32[]{:S(2)}) collective-permute-start(f32[2,64,256]{2,1,0:T(8,128)S(1)} %get-tuple-element.19), channel_id=1, source_target_pairs={{0,20},{4,16},{8,28},{12,24},{16,4},{20,0},{24,12},{28,8},{1,21},{... | collective-permute-start | bytes 393224 | tf_op jit(solution)/shard_map/ppermute | solution.py:356
  20.5 0.0 collective-permute-done.1
  20.5 1.5 %collective-permute-start.8 = (f32[2,128,256]{2,1,0:T(8,128)S(1)}, f32[2,128,256]{2,1,0:T(8,128)S(1)}, u32[]{:S(2)}, u32[]{:S(2)}) collective-permute-start(f32[2,128,256]{2,1,0:T(8,128)S(1)} %get-tuple-element.20.own_ref), channel_id=1, source_target_pairs={{0,2},{1,3},{2,0},{3,1},{4,6},{5,7},{6,4},{7,5},{8,10},{9,11},{10,... | collective-permute-start | bytes 786440 | tf_op jit(solution)/shard_map/ppermute | solution.py:356
  22.0 0.0 collective-permute-done.2
  22.0 0.0 collective-permute-done.3
  22.0 0.6 %collective-permute-start.4 = (f32[2,192,256]{2,1,0:T(8,128)S(1)}, f32[2,192,256]{2,1,0:T(8,128)S(1)}, u32[]{:S(2)}, u32[]{:S(2)}) collective-permute-start(f32[2,192,256]{2,1,0:T(8,128)S(1)} %constant_dynamic-update-slice_fusion.refs_2_), channel_id=1, source_target_pairs={{0,2},{1,3},{2,0},{3,1},{4,6},{5,7},{6,4},{7,5},{8,10},{9,11},{10,... | collective-permute-start | bytes 1179656 | tf_op jit(solution)/shard_map/ppermute | solution.py:356
  22.6 5.5 %collective-permute-done.5 = f32[2,64,256]{2,1,0:T(8,128)S(1)} collective-permute-done((f32[2,64,256]{2,1,0:T(8,128)S(1)}, f32[2,64,256]{2,1,0:T(8,128)S(1)}, u32[]{:S(2)}, u32[]{:S(2)}) %collective-permute-start.5) | collective-permute-done | bytes 131104 | tf_op jit(solution)/shard_map/ppermute | solution.py:356
  28.2 3.1 %collective-permute-done.6 = f32[2,64,256]{2,1,0:T(8,128)S(1)} collective-permute-done((f32[2,64,256]{2,1,0:T(8,128)S(1)}, f32[2,64,256]{2,1,0:T(8,128)S(1)}, u32[]{:S(2)}, u32[]{:S(2)}) %collective-permute-start.6) | collective-permute-done | bytes 131104 | tf_op jit(solution)/shard_map/ppermute | solution.py:356
  31.3 1.6 %collective-permute-start.7 = (f32[2,128,256]{2,1,0:T(8,128)S(1)}, f32[2,128,256]{2,1,0:T(8,128)S(1)}, u32[]{:S(2)}, u32[]{:S(2)}) collective-permute-start(f32[2,128,256]{2,1,0:T(8,128)S(1)} %constant_dynamic-update-slice_fusion.3.refs_4_), channel_id=1, source_target_pairs={{0,2},{1,3},{2,0},{3,1},{4,6},{5,7},{6,4},{7,5},{8,10},{9,11},{10,... | collective-permute-start | bytes 786440 | tf_op jit(solution)/shard_map/ppermute | solution.py:356
  32.9 0.5 collective-permute-start
  33.4 0.0 collective-permute-done.8.other_ref
  33.4 0.0 copy-done.3
  33.4 0.7 %combine.1 = (f32[2,64,256]{2,1,0:T(8,128)S(1)}, f32[2,64,256]{2,1,0:T(8,128)S(1)}) custom-call(f32[2,128,256]{2,1,0:T(8,128)S(1)} %get-tuple-element.20.own_ref, f32[2,128,256]{2,1,0:T(8,128)S(1)} %collective-permute-done.8.other_ref, f32[2,2,2,2]{3,2,1,0:T(2,128)S(1)} %copy-done.3), custom_call_target="tpu_custom_call" | custom-call | tf_op jit(solution)/shard_map/combine/pallas_call | solution.py:233
  34.1 3.5 %collective-permute-start.9 = (f32[2,64,256]{2,1,0:T(8,128)S(1)}, f32[2,64,256]{2,1,0:T(8,128)S(1)}, u32[]{:S(2)}, u32[]{:S(2)}) collective-permute-start(f32[2,64,256]{2,1,0:T(8,128)S(1)} %get-tuple-element.21), channel_id=1, source_target_pairs={{0,24},{4,28},{8,16},{12,20},{16,8},{20,12},{24,0},{28,4},{1,25},{... | collective-permute-start | bytes 393224 | tf_op jit(solution)/shard_map/ppermute | solution.py:356
  37.6 0.4 collective-permute-start.10
  38.0 5.9 %collective-permute-done.refs_1_ = f32[2,64,256]{2,1,0:T(8,128)S(1)} collective-permute-done((f32[2,64,256]{2,1,0:T(8,128)S(1)}, f32[2,64,256]{2,1,0:T(8,128)S(1)}, u32[]{:S(2)}, u32[]{:S(2)}) %collective-permute-start) | collective-permute-done | bytes 131104 | tf_op jit(solution)/shard_map/ppermute | solution.py:356
  44.0 0.0 collective-permute-done.7.refs_5_
  44.0 0.0 collective-permute-done.9.refs_6_
  44.0 1.3 %collective-permute-done.10.refs_7_ = f32[2,64,256]{2,1,0:T(8,128)S(1)} collective-permute-done((f32[2,64,256]{2,1,0:T(8,128)S(1)}, f32[2,64,256]{2,1,0:T(8,128)S(1)}, u32[]{:S(2)}, u32[]{:S(2)}) %collective-permute-start.10) | collective-permute-done | bytes 131104 | tf_op jit(solution)/shard_map/ppermute | solution.py:356
  45.3 0.0 collective-permute-done.4.refs_3_
  45.3 0.0 copy-done.1
  45.3 3.0 %second_gate.1.own_ref = f32[2,512,256]{2,1,0:T(8,128)S(1)} custom-call(f32[2,2,512,512]{3,2,1,0:T(8,128)S(1)} %copy-done.1, f32[2,17]{1,0:T(2,128)S(1)} %copy-done.4, f32[2,1]{1,0:T(2,128)S(1)} %copy.11.angles_ref, s32[17]{0:T(128)S(1)} %copy-done.6, s32[2,17]{1,0:T(2,128)S(1)} %copy-done.5, f32[2,2,2,2]{3,2,1,0:T(2,128)S(1)} %copy-done.3, ...), custom_call_target="tpu_custom_call" | custom-call | tf_op jit(solution)/shard_map/second_gate/pallas_call | solution.py:308
  48.2 0.1 collective-permute-start.11
  48.3 2.6 %collective-permute-done.11.other_ref = f32[2,512,256]{2,1,0:T(8,128)S(1)} collective-permute-done((f32[2,512,256]{2,1,0:T(8,128)S(1)}, f32[2,512,256]{2,1,0:T(8,128)S(1)}, u32[]{:S(2)}, u32[]{:S(2)}) %collective-permute-start.11) | collective-permute-done | bytes 1048608 | tf_op jit(solution)/shard_map/ppermute | solution.py:356
  51.0 2.3 %last.1 = f32[2,1,512,256]{3,2,1,0:T(8,128)} custom-call(f32[2,512,256]{2,1,0:T(8,128)S(1)} %second_gate.1.own_ref, f32[2,512,256]{2,1,0:T(8,128)S(1)} %collective-permute-done.11.other_ref, f32[2,17]{1,0:T(2,128)S(1)} %copy-done.4, s32[17]{0:T(128)S(1)} %copy-done.6, s32[2,17]{1,0:T(2,128)S(1)} %copy-done.5, f32[2,2,2,2]{3,2,1,0:T(2,128)S(1)} %copy-done.3), custom_call_target="tpu_custom_call" | custom-call | tf_op jit(solution)/shard_map/last/pallas_call | solution.py:345
  (5 shorter events, 0.1 us)
Async XLA Ops:
  0.7 2.2 %copy-start = (f32[2,2,512,512]{3,2,1,0:T(8,128)S(1)}, f32[2,2,512,512]{3,2,1,0:T(8,128)}, u32[]{:S(2)}) copy-start(f32[2,2,512,512]{3,2,1,0:T(8,128)} %gates_ref.5) | copy-start | bytes 12582916
  2.9 1.2 %copy-start.2 = (f32[2,1,512,256]{3,2,1,0:T(8,128)S(1)}, f32[2,1,512,256]{3,2,1,0:T(8,128)}, u32[]{:S(2)}) copy-start(f32[2,1,512,256]{3,2,1,0:T(8,128)} %amplitudes_ref.3) | copy-start | bytes 3145732
  4.2 0.7 %copy-start.4 = (f32[2,17]{1,0:T(2,128)S(1)}, f32[2,17]{1,0:T(2,128)}, u32[]{:S(2)}) copy-start(f32[2,17]{1,0:T(2,128)} %phases_ref.7) | copy-start | bytes 412
  4.8 0.7 %copy-start.5 = (s32[2,17]{1,0:T(2,128)S(1)}, s32[2,17]{1,0:T(2,128)}, u32[]{:S(2)}) copy-start(s32[2,17]{1,0:T(2,128)} %coupled_ref.7) | copy-start | bytes 412
  5.5 0.7 %copy-start.6 = (s32[17]{0:T(128)S(1)}, s32[17]{0:T(128)}, u32[]{:S(2)}) copy-start(s32[17]{0:T(128)} %bits_ref.7) | copy-start | bytes 208
  6.2 0.7 %copy-start.7 = (s32[9]{0:T(128)S(1)}, s32[9]{0:T(128)}, u32[]{:S(2)}) copy-start(s32[9]{0:T(128)} %layout_ref.3) | copy-start | bytes 112
  9.2 24.3 %copy-start.3 = (f32[2,2,2,2]{3,2,1,0:T(2,128)S(1)}, f32[2,2,2,2]{3,2,1,0:T(2,128)}, u32[]{:S(2)}) copy-start(f32[2,2,2,2]{3,2,1,0:T(2,128)} %pair_ref.5) | copy-start | bytes 196
  9.2 36.1 %copy-start.1 = (f32[2,2,512,512]{3,2,1,0:T(8,128)S(1)}, f32[2,2,512,512]{3,2,1,0:T(8,128)}, u32[]{:S(2)}) copy-start(f32[2,2,512,512]{3,2,1,0:T(8,128)} %gates_ref.5) | copy-start | bytes 12582916
  9.2 11.3 %collective-permute-start.1 = (f32[2,64,256]{2,1,0:T(8,128)S(1)}, f32[2,64,256]{2,1,0:T(8,128)S(1)}, u32[]{:S(2)}, u32[]{:S(2)}) collective-permute-start(f32[2,64,256]{2,1,0:T(8,128)S(1)} %get-tuple-element.15), channel_id=1, source_target_pairs={{0,4},{4,0},{8,12},{12,8},{16,20},{20,16},{24,28},{28,24},{1,5},{5... | collective-permute-start | bytes 393224 | tf_op jit(solution)/shard_map/ppermute | solution.py:356
  12.2 9.8 %collective-permute-start.2 = (f32[2,64,256]{2,1,0:T(8,128)S(1)}, f32[2,64,256]{2,1,0:T(8,128)S(1)}, u32[]{:S(2)}, u32[]{:S(2)}) collective-permute-start(f32[2,64,256]{2,1,0:T(8,128)S(1)} %get-tuple-element.16), channel_id=1, source_target_pairs={{0,8},{4,12},{8,0},{12,4},{16,24},{20,28},{24,16},{28,20},{1,9},{5... | collective-permute-start | bytes 393224 | tf_op jit(solution)/shard_map/ppermute | solution.py:356
  13.8 8.2 %collective-permute-start.3 = (f32[2,64,256]{2,1,0:T(8,128)S(1)}, f32[2,64,256]{2,1,0:T(8,128)S(1)}, u32[]{:S(2)}, u32[]{:S(2)}) collective-permute-start(f32[2,64,256]{2,1,0:T(8,128)S(1)} %get-tuple-element.17), channel_id=1, source_target_pairs={{0,12},{4,8},{8,4},{12,0},{16,28},{20,24},{24,20},{28,16},{1,13},{... | collective-permute-start | bytes 393224 | tf_op jit(solution)/shard_map/ppermute | solution.py:356
  16.1 12.1 %collective-permute-start.5 = (f32[2,64,256]{2,1,0:T(8,128)S(1)}, f32[2,64,256]{2,1,0:T(8,128)S(1)}, u32[]{:S(2)}, u32[]{:S(2)}) collective-permute-start(f32[2,64,256]{2,1,0:T(8,128)S(1)} %get-tuple-element.18), channel_id=1, source_target_pairs={{0,16},{4,20},{8,24},{12,28},{16,0},{20,4},{24,8},{28,12},{1,17},{... | collective-permute-start | bytes 393224 | tf_op jit(solution)/shard_map/ppermute | solution.py:356
  19.2 12.2 %collective-permute-start.6 = (f32[2,64,256]{2,1,0:T(8,128)S(1)}, f32[2,64,256]{2,1,0:T(8,128)S(1)}, u32[]{:S(2)}, u32[]{:S(2)}) collective-permute-start(f32[2,64,256]{2,1,0:T(8,128)S(1)} %get-tuple-element.19), channel_id=1, source_target_pairs={{0,20},{4,16},{8,28},{12,24},{16,4},{20,0},{24,12},{28,8},{1,21},{... | collective-permute-start | bytes 393224 | tf_op jit(solution)/shard_map/ppermute | solution.py:356
  20.5 13.0 %collective-permute-start.8 = (f32[2,128,256]{2,1,0:T(8,128)S(1)}, f32[2,128,256]{2,1,0:T(8,128)S(1)}, u32[]{:S(2)}, u32[]{:S(2)}) collective-permute-start(f32[2,128,256]{2,1,0:T(8,128)S(1)} %get-tuple-element.20.own_ref), channel_id=1, source_target_pairs={{0,2},{1,3},{2,0},{3,1},{4,6},{5,7},{6,4},{7,5},{8,10},{9,11},{10,... | collective-permute-start | bytes 786440 | tf_op jit(solution)/shard_map/ppermute | solution.py:356
  22.0 23.2 %collective-permute-start.4 = (f32[2,192,256]{2,1,0:T(8,128)S(1)}, f32[2,192,256]{2,1,0:T(8,128)S(1)}, u32[]{:S(2)}, u32[]{:S(2)}) collective-permute-start(f32[2,192,256]{2,1,0:T(8,128)S(1)} %constant_dynamic-update-slice_fusion.refs_2_), channel_id=1, source_target_pairs={{0,2},{1,3},{2,0},{3,1},{4,6},{5,7},{6,4},{7,5},{8,10},{9,11},{10,... | collective-permute-start | bytes 1179656 | tf_op jit(solution)/shard_map/ppermute | solution.py:356
  31.3 12.6 %collective-permute-start.7 = (f32[2,128,256]{2,1,0:T(8,128)S(1)}, f32[2,128,256]{2,1,0:T(8,128)S(1)}, u32[]{:S(2)}, u32[]{:S(2)}) collective-permute-start(f32[2,128,256]{2,1,0:T(8,128)S(1)} %constant_dynamic-update-slice_fusion.3.refs_4_), channel_id=1, source_target_pairs={{0,2},{1,3},{2,0},{3,1},{4,6},{5,7},{6,4},{7,5},{8,10},{9,11},{10,... | collective-permute-start | bytes 786440 | tf_op jit(solution)/shard_map/ppermute | solution.py:356
  32.9 11.1 %collective-permute-start = (f32[2,64,256]{2,1,0:T(8,128)S(1)}, f32[2,64,256]{2,1,0:T(8,128)S(1)}, u32[]{:S(2)}, u32[]{:S(2)}) collective-permute-start(f32[2,64,256]{2,1,0:T(8,128)S(1)} %get-tuple-element.14.refs_0_), channel_id=1, source_target_pairs={{0,2},{1,3},{2,0},{3,1},{4,6},{5,7},{6,4},{7,5},{8,10},{9,11},{10,... | collective-permute-start | bytes 393224 | tf_op jit(solution)/shard_map/ppermute | solution.py:356
  34.1 9.9 %collective-permute-start.9 = (f32[2,64,256]{2,1,0:T(8,128)S(1)}, f32[2,64,256]{2,1,0:T(8,128)S(1)}, u32[]{:S(2)}, u32[]{:S(2)}) collective-permute-start(f32[2,64,256]{2,1,0:T(8,128)S(1)} %get-tuple-element.21), channel_id=1, source_target_pairs={{0,24},{4,28},{8,16},{12,20},{16,8},{20,12},{24,0},{28,4},{1,25},{... | collective-permute-start | bytes 393224 | tf_op jit(solution)/shard_map/ppermute | solution.py:356
  37.6 7.7 %collective-permute-start.10 = (f32[2,64,256]{2,1,0:T(8,128)S(1)}, f32[2,64,256]{2,1,0:T(8,128)S(1)}, u32[]{:S(2)}, u32[]{:S(2)}) collective-permute-start(f32[2,64,256]{2,1,0:T(8,128)S(1)} %get-tuple-element.22), channel_id=1, source_target_pairs={{0,28},{4,24},{8,20},{12,16},{16,12},{20,8},{24,4},{28,0},{1,29},{... | collective-permute-start | bytes 393224 | tf_op jit(solution)/shard_map/ppermute | solution.py:356
  48.2 2.7 %collective-permute-start.11 = (f32[2,512,256]{2,1,0:T(8,128)S(1)}, f32[2,512,256]{2,1,0:T(8,128)S(1)}, u32[]{:S(2)}, u32[]{:S(2)}) collective-permute-start(f32[2,512,256]{2,1,0:T(8,128)S(1)} %second_gate.1.own_ref), channel_id=1, source_target_pairs={{0,1},{1,0},{2,3},{3,2},{4,5},{5,4},{6,7},{7,6},{8,9},{9,8},{10,11... | collective-permute-start | bytes 3145736 | tf_op jit(solution)/shard_map/ppermute | solution.py:356

commit v2 on v1

v2 whole, which is shorter than its diff:
```python
import functools

import jax
import jax.numpy as jnp
from jax import lax
from jax.experimental import pallas as pl
from jax.experimental.pallas import tpu as pltpu
from jax.sharding import PartitionSpec as P

F32 = jnp.float32
BF16 = jnp.bfloat16
VMEM_BYTES = 32 * 1024 * 1024
MIDDLE_COST = 3000000000
HALF_COST = 1000
READY_COST = 1500001000
LATE_COST = 1000


def sincos(x):
    turns = jnp.floor(x * 0.6366197723675814 + 0.5)
    r = x - turns * 1.5703125
    r = r - turns * 4.837512969970703125e-4
    r = r - turns * 7.54978995489188216e-8
    z = r * r
    sine = r + r * z * ((-1.9515295891e-4 * z + 8.3321608736e-3) * z - 1.6666654611e-1)
    cosine = 1.0 - 0.5 * z + z * z * (
        (2.443315711809948e-5 * z - 1.388731625493765e-3) * z + 4.166664568298827e-2
    )
    quarter = turns.astype(jnp.int32) & 3
    odd = (quarter & 1) == 1
    new_sine = jnp.where(odd, cosine, sine)
    new_cosine = jnp.where(odd, sine, cosine)
    new_sine = jnp.where((quarter & 2) == 2, -new_sine, new_sine)
    new_cosine = jnp.where(((quarter + 1) & 2) == 2, -new_cosine, new_cosine)
    return new_cosine, new_sine


def qubit_factors(layer, phases_ref, bits_ref, coupled_ref):
    qubits = phases_ref.shape[1]
    lane = lax.broadcasted_iota(jnp.int32, (1, qubits), 1)
    odd = jnp.zeros((1, qubits), jnp.int32)
    for f in range(bits_ref.shape[0]):
        odd = odd ^ jnp.where(lane == coupled_ref[layer, f], bits_ref[f], 0)
    sign = 1.0 - 2.0 * odd.astype(F32)
    cosine, sine = sincos(phases_ref[layer : layer + 1, :])
    return cosine * sign, sine * sign


def turn(real, imag, cosine, sine):
    return real * cosine - imag * sine, real * sine + imag * cosine


def row_phases(cosine, sine, first, row_bits, base_real, base_imag):
    sub = lax.broadcasted_iota(jnp.int32, (8, 128), 0)
    real = jnp.broadcast_to(base_real, (8, 128))
    imag = jnp.broadcast_to(base_imag, (8, 128))
    for k in range(row_bits):
        c = cosine[:, first + k : first + k + 1]
        s = sine[:, first + k : first + k + 1]
        if k < 3:
            chosen = ((sub >> k) & 1) == 1
            real, imag = turn(real, imag, jnp.where(chosen, c, 1.0), jnp.where(chosen, s, 0.0))
        else:
            up_real, up_imag = turn(real, imag, c, s)
            real = jnp.concatenate([real, up_real], axis=0)
            imag = jnp.concatenate([imag, up_imag], axis=0)
    return real, imag


def col_phases(cosine, sine, col_bits, cols):
    lane = lax.broadcasted_iota(jnp.int32, (1, cols), 1)
    real = jnp.ones((1, cols), F32)
    imag = jnp.zeros((1, cols), F32)
    for k in range(col_bits):
        chosen = ((lane >> k) & 1) == 1
        c = cosine[:, k : k + 1]
        s = sine[:, k : k + 1]
        real, imag = turn(real, imag, jnp.where(chosen, c, 1.0), jnp.where(chosen, s, 0.0))
    return real, imag


def split(x):
    high = x.astype(BF16)
    low = (x - high.astype(F32)).astype(BF16)
    return high, low


def dot(a, b):
    return jnp.dot(a, b, preferred_element_type=F32)


def turned_rows(real, imag, phase_real, phase_imag):
    reps = real.shape[1] // phase_real.shape[1]
    phase_real = jnp.concatenate([phase_real] * reps, axis=1)
    phase_imag = jnp.concatenate([phase_imag] * reps, axis=1)
    real, imag = turn(real, imag, phase_real, phase_imag)
    real_high, real_low = split(real)
    imag_high, imag_low = split(imag)

    def block(r, i):
        return jnp.concatenate(
            [jnp.concatenate([r, i], axis=1), jnp.concatenate([-i, r], axis=1)], axis=0
        )

    return block(real_high, imag_high), block(real_low, imag_low)


def product(left_high, left_low, right_high, right_low):
    return dot(left_high, right_high) + dot(left_high, right_low) + dot(left_low, right_high)


def hbm(array):
    return pltpu.with_memory_space_constraint(array, pltpu.HBM)


def any_space():
    return pl.BlockSpec(memory_space=pl.ANY)


def smem():
    return pl.BlockSpec(memory_space=pltpu.SMEM)


def vmem():
    return pl.BlockSpec(memory_space=pltpu.VMEM)


def cost(flops=1000):
    return pl.CostEstimate(flops=flops, bytes_accessed=1000, transcendentals=0)


def params():
    return pltpu.CompilerParams(vmem_limit_bytes=VMEM_BYTES)


def chosen_rows(steps, piece_rows, rows, layout_ref):
    me = lax.axis_index("hi")
    row_bits = rows.bit_length() - 1
    sub = lax.broadcasted_iota(jnp.int32, (8, 128), 0)
    inner = jnp.zeros((8, 128), jnp.int32)
    inner_bits = piece_rows.bit_length() - 1
    for k in range(inner_bits):
        place = jnp.left_shift(jnp.int32(1), layout_ref[k])
        if k < 3:
            inner = inner + ((sub >> k) & 1) * place
        else:
            inner = jnp.concatenate([inner, inner + place], axis=0)
    places = []
    for step in steps:
        block = me ^ step
        base = jnp.int32(0)
        for k in range(inner_bits, row_bits):
            base = base + jnp.left_shift((block >> (k - inner_bits)) & 1, layout_ref[k])
        places.append(inner + base)
    places = jnp.concatenate(places, axis=0)
    lane = lax.broadcasted_iota(jnp.int32, places.shape, 1)
    return jnp.concatenate(
        [
            jnp.where(places == lane + start, 1.0, 0.0).astype(BF16)
            for start in range(0, rows, 128)
        ],
        axis=1,
    )


def gate_pieces(groups, piece_rows, layout_ref, gate_high, gate_low, right_high, right_low, out_refs):
    rows = gate_high.shape[0]
    cols = right_high.shape[1] // 2
    chosen = chosen_rows([d for group in groups for d in group], piece_rows, rows, layout_ref)
    left_high = dot(chosen, gate_high).astype(BF16)
    left_low = dot(chosen, gate_low).astype(BF16)
    out = product(left_high, left_low, right_high, right_low)
    start = 0
    for group, out_ref in zip(groups, out_refs, strict=True):
        size = len(group) * piece_rows
        out_ref[0] = out[start : start + size, :cols]
        out_ref[1] = out[start : start + size, cols:]
        start += size


def first_kernel(
    groups,
    piece_rows,
    col_bits,
    amplitudes_hbm,
    gates_hbm,
    phases_hbm,
    angles_hbm,
    bits_hbm,
    coupled_hbm,
    layout_hbm,
    *refs,
):
    (
        *out_refs,
        amplitudes_ref,
        gates_ref,
        phases_ref,
        angles_ref,
        bits_ref,
        coupled_ref,
        layout_ref,
        sems,
    ) = refs
    copies = [
        pltpu.make_async_copy(source, target, sems.at[i])
        for i, (source, target) in enumerate(
            (
                (phases_hbm, phases_ref),
                (angles_hbm, angles_ref),
                (bits_hbm, bits_ref),
                (coupled_hbm, coupled_ref),
                (layout_hbm, layout_ref),
                (gates_hbm.at[0, 0], gates_ref.at[0]),
                (gates_hbm.at[0, 1], gates_ref.at[1]),
                (amplitudes_hbm, amplitudes_ref),
            )
        )
    ]
    for copy in copies:
        copy.start()
    for copy in copies[:5]:
        copy.wait()
    rows = amplitudes_ref.shape[2]
    row_bits = rows.bit_length() - 1
    cosine, sine = qubit_factors(0, phases_ref, bits_ref, coupled_ref)
    base_real, base_imag = sincos(angles_ref[0:1, 0:1])
    phase_real, phase_imag = row_phases(cosine, sine, col_bits, row_bits, base_real, base_imag)
    high, low = [], []
    for i in range(2):
        copies[5 + i].wait()
        for parts, part in zip((high, low), split(gates_ref[i]), strict=True):
            parts.append(part)
    copies[7].wait()
    right_high, right_low = turned_rows(
        amplitudes_ref[0, 0], amplitudes_ref[1, 0], phase_real, phase_imag
    )
    gate_pieces(
        groups,
        piece_rows,
        layout_ref,
        jnp.concatenate(high, axis=1),
        jnp.concatenate(low, axis=1),
        right_high,
        right_low,
        out_refs,
    )


def first(groups, piece_rows, col_bits, amplitudes, gates, phases, angles, bits, coupled, layout):
    rows, cols = amplitudes.shape[2:]
    shapes = [jax.ShapeDtypeStruct((2, len(group) * piece_rows, cols), F32) for group in groups]
    sources = (amplitudes, gates, phases, angles, bits, coupled, layout)
    return pl.pallas_call(
        functools.partial(first_kernel, groups, piece_rows, col_bits),
        out_shape=shapes,
        in_specs=[any_space()] * len(sources),
        out_specs=[vmem()] * len(shapes),
        scratch_shapes=[
            pltpu.VMEM(amplitudes.shape, F32),
            pltpu.VMEM(gates.shape[1:], F32),
            pltpu.VMEM(phases.shape, F32),
            pltpu.VMEM(angles.shape, F32),
            pltpu.SMEM(bits.shape, jnp.int32),
            pltpu.SMEM(coupled.shape, jnp.int32),
            pltpu.SMEM(layout.shape, jnp.int32),
            pltpu.SemaphoreType.DMA((8,)),
        ],
        compiler_params=params(),
        cost_estimate=cost(),
        name="first",
    )(*[hbm(source) for source in sources])


def ready_kernel(
    col_bits, gates_hbm, phases_ref, angles_ref, bits_ref, coupled_ref, pair_ref, *refs
):
    (
        gate_high_ref,
        gate_low_ref,
        phase_real_ref,
        phase_imag_ref,
        coefficients_ref,
        gates_ref,
        sem,
    ) = refs
    copy = pltpu.make_async_copy(gates_hbm.at[1], gates_ref, sem)
    copy.start()
    rows = gates_ref.shape[1]
    cols = coefficients_ref.shape[1]
    row_bits = rows.bit_length() - 1
    bit = lax.axis_index("lo") & 1
    before = qubit_factors(0, phases_ref, bits_ref, coupled_ref)
    after = qubit_factors(1, phases_ref, bits_ref, coupled_ref)
    base_real, base_imag = sincos(angles_ref[0:1, 1:2])
    phase_real_ref[...], phase_imag_ref[...] = row_phases(
        *after, col_bits, row_bits, base_real, base_imag
    )
    phase_real, phase_imag = turn(
        *col_phases(*before, col_bits, cols), *col_phases(*after, col_bits, cols)
    )
    c = pair_coefficients(pair_ref, 1, bit)
    c = turn(phase_real, phase_imag, c[0], c[1]) + turn(phase_real, phase_imag, c[2], c[3])
    for i in range(4):
        coefficients_ref[i : i + 1, :] = c[i]
    coefficients_ref[4:8, :] = jnp.zeros((4, cols), F32)
    copy.wait()
    for i in range(2):
        high, low = split(gates_ref[i])
        gate_high_ref[:, i * rows : (i + 1) * rows] = high
        gate_low_ref[:, i * rows : (i + 1) * rows] = low


def ready(col_bits, gates, phases, angles, bits, coupled, pair):
    rows = gates.shape[2]
    cols = 1 << col_bits
    return pl.pallas_call(
        functools.partial(ready_kernel, col_bits),
        out_shape=[
            jax.ShapeDtypeStruct((rows, 2 * rows), BF16),
            jax.ShapeDtypeStruct((rows, 2 * rows), BF16),
            jax.ShapeDtypeStruct((rows, 128), F32),
            jax.ShapeDtypeStruct((rows, 128), F32),
            jax.ShapeDtypeStruct((8, cols), F32),
        ],
        in_specs=[any_space(), vmem(), vmem(), smem(), smem(), smem()],
        out_specs=[vmem()] * 5,
        scratch_shapes=[pltpu.VMEM(gates.shape[1:], F32), pltpu.SemaphoreType.DMA],
        compiler_params=params(),
        cost_estimate=cost(READY_COST),
        name="ready",
    )(hbm(gates), phases, angles, bits, coupled, pair)


def pair_coefficients(pair_ref, layer, bit):
    own = bit
    other = 1 - bit
    return (
        pair_ref[layer, 0, own, own],
        pair_ref[layer, 1, own, own],
        pair_ref[layer, 0, own, other],
        pair_ref[layer, 1, own, other],
    )


def combined(own, other, c):
    own_real, own_imag = turn(own[0], own[1], c[0], c[1])
    other_real, other_imag = turn(other[0], other[1], c[2], c[3])
    return own_real + other_real, own_imag + other_imag


def combine_kernel(top_bit, own_ref, other_ref, pair_ref, *out_refs):
    bit = (lax.axis_index("lo") >> top_bit) & 1
    c = pair_coefficients(pair_ref, 0, bit)
    size = out_refs[0].shape[1]
    for i, out_ref in enumerate(out_refs):
        rows = slice(i * size, (i + 1) * size)
        out_ref[0], out_ref[1] = combined(
            (own_ref[0, rows], own_ref[1, rows]), (other_ref[0, rows], other_ref[1, rows]), c
        )


def combine(top_bit, count, own, other, pair_gates):
    shape = (2, own.shape[1] // count, own.shape[2])
    return pl.pallas_call(
        functools.partial(combine_kernel, top_bit),
        out_shape=[jax.ShapeDtypeStruct(shape, F32)] * count,
        in_specs=[vmem(), vmem(), smem()],
        out_specs=[vmem()] * count,
        compiler_params=params(),
        cost_estimate=cost(),
        name="combine",
    )(own, other, pair_gates)


def partial_product(quarters, pieces, piece_rows, parts_refs, scratch_refs):
    gate_high_ref, gate_low_ref, phase_real_ref, phase_imag_ref = parts_refs
    real_ref, imag_ref = scratch_refs
    rows = gate_high_ref.shape[0]
    size = rows // 4
    quarter = size // piece_rows
    me = lax.axis_index("hi")
    for step, (real, imag) in pieces.items():
        offset = quarters.index(step // quarter) * size
        start = offset + ((me ^ step) & (quarter - 1)) * piece_rows
        start = pl.multiple_of(start, piece_rows)
        real_ref[pl.ds(start, piece_rows), :] = real
        imag_ref[pl.ds(start, piece_rows), :] = imag
    starts = [pl.multiple_of(((me // quarter) ^ q) * size, size) for q in quarters]

    def some_rows(ref):
        return jnp.concatenate([ref[pl.ds(start, size), :] for start in starts], axis=0)

    def some_cols(ref):
        shift = (0, rows)
        return jnp.concatenate(
            [
                ref[:, pl.ds(pl.multiple_of(start + extra, size), size)]
                for extra in shift
                for start in starts
            ],
            axis=1,
        )

    right_high, right_low = turned_rows(
        real_ref[...], imag_ref[...], some_rows(phase_real_ref), some_rows(phase_imag_ref)
    )
    out = product(some_cols(gate_high_ref), some_cols(gate_low_ref), right_high, right_low)
    cols = real_ref.shape[1]
    return out[:, :cols], out[:, cols:]


def late_kernel(*refs):
    *part_refs, out_ref = refs
    size = part_refs[0].shape[1]
    for i, part_ref in enumerate(part_refs):
        out_ref[:, i * size : (i + 1) * size, :] = part_ref[...]


def joined(arrays, flops):
    _, size, cols = arrays[0].shape
    return pl.pallas_call(
        late_kernel,
        out_shape=jax.ShapeDtypeStruct((2, size * len(arrays), cols), F32),
        in_specs=[vmem()] * len(arrays),
        out_specs=vmem(),
        compiler_params=params(),
        cost_estimate=cost(flops),
        name="joined",
    )(*arrays)


def split_pieces(ref, steps, piece_rows):
    pieces = {}
    for i, step in enumerate(steps):
        part = slice(i * piece_rows, (i + 1) * piece_rows)
        pieces[step] = (ref[0, part], ref[1, part])
    return pieces


def middle_kernel(quarters, landed, piece_rows, *refs):
    landed_refs = refs[4:-3]
    out_ref = refs[-3]
    pieces = {step: (ref[0], ref[1]) for step, ref in zip(landed, landed_refs, strict=True)}
    out_ref[0], out_ref[1] = partial_product(quarters, pieces, piece_rows, refs[:4], refs[-2:])


def middle(quarters, landed, piece_rows, parts, arrays):
    rows = parts[0].shape[0]
    cols = arrays[0].shape[2]
    return pl.pallas_call(
        functools.partial(middle_kernel, quarters, landed, piece_rows),
        out_shape=jax.ShapeDtypeStruct((2, rows, cols), F32),
        in_specs=[vmem()] * (4 + len(arrays)),
        out_specs=vmem(),
        scratch_shapes=[pltpu.VMEM((len(quarters) * rows // 4, cols), F32)] * 2,
        compiler_params=params(),
        cost_estimate=cost(MIDDLE_COST),
        name="middle",
    )(*parts, *arrays)


def second_kernel(quarters, exchanged, grouped, landed, piece_rows, top_bit, *refs):
    sum_ref, pair_ref, own_ref, other_ref, group_ref = refs[4:9]
    landed_refs = refs[9 : 9 + len(landed)]
    out_ref = refs[-3]
    bit = (lax.axis_index("lo") >> top_bit) & 1
    c = pair_coefficients(pair_ref, 0, bit)
    pieces = {step: (ref[0], ref[1]) for step, ref in zip(landed, landed_refs, strict=True)}
    pieces.update(split_pieces(group_ref, grouped, piece_rows))
    others = split_pieces(other_ref, exchanged, piece_rows)
    for step, own in split_pieces(own_ref, exchanged, piece_rows).items():
        pieces[step] = combined(own, others[step], c)
    real, imag = partial_product(quarters, pieces, piece_rows, refs[:4], refs[-2:])
    out_ref[0] = sum_ref[0] + real
    out_ref[1] = sum_ref[1] + imag


def second(
    quarters, exchanged, grouped, landed, piece_rows, top_bit, parts, total, pair, own, other, arrays
):
    rows = parts[0].shape[0]
    cols = own.shape[2]
    return pl.pallas_call(
        functools.partial(
            second_kernel, quarters, exchanged, grouped, landed, piece_rows, top_bit
        ),
        out_shape=jax.ShapeDtypeStruct((2, rows, cols), F32),
        in_specs=[vmem()] * 5 + [smem()] + [vmem()] * (2 + len(arrays)),
        out_specs=vmem(),
        scratch_shapes=[pltpu.VMEM((len(quarters) * rows // 4, cols), F32)] * 2,
        compiler_params=params(),
        cost_estimate=cost(),
        name="second",
    )(*parts, total, pair, own, other, *arrays)


def last_kernel(own_ref, other_ref, coefficients_ref, out_ref):
    c = [coefficients_ref[i : i + 1, :] for i in range(4)]
    out_ref[0, 0], out_ref[1, 0] = combined(own_ref, other_ref, c)


def last(own, other, coefficients):
    _, rows, cols = own.shape
    step = rows // 4
    block = pl.BlockSpec((2, step, cols), lambda i: (0, i, 0))
    return pl.pallas_call(
        last_kernel,
        grid=(rows // step,),
        out_shape=jax.ShapeDtypeStruct((2, 1, rows, cols), F32),
        in_specs=[block, block, pl.BlockSpec((8, cols), lambda i: (0, 0))],
        out_specs=pl.BlockSpec((2, 1, step, cols), lambda i: (0, 0, i, 0)),
        compiler_params=params(),
        cost_estimate=cost(),
        name="last",
    )(own, other, coefficients)


def swap(value, axis, mask):
    return lax.ppermute(value, axis, [(i, i ^ mask) for i in range(lax.axis_size(axis))])


def after(value, earlier):
    return lax.optimization_barrier((value, earlier))[0]


def shards(amplitudes, gates, pair, angles, phases, bits, coupled, layout):
    rows = amplitudes.shape[2]
    cols = amplitudes.shape[3]
    col_bits = cols.bit_length() - 1
    count = lax.axis_size("hi")
    piece_rows = rows // count
    top_bit = lax.axis_size("lo").bit_length() - 2
    quarter = count // 4
    angles = angles.T
    beside = tuple(range(1, quarter))
    near = tuple(range(quarter, 2 * quarter))
    far = tuple(range(2 * quarter, 3 * quarter))
    early = tuple(range(3 * quarter, count))
    late = beside + far
    cross = functools.partial(swap, axis="lo", mask=1 << top_bit)

    made = first(
        (early, (0,) + near) + tuple((d,) for d in late),
        piece_rows,
        col_bits,
        amplitudes,
        gates,
        phases,
        angles,
        bits,
        coupled,
        layout,
    )
    early_part, near_part, *late_parts = made
    early_other = cross(early_part)
    late_parts = [swap(part, "hi", d) for part, d in zip(late_parts, late, strict=True)]
    near_other = cross(near_part)
    early_parts = combine(top_bit, len(early), early_part, early_other, pair)
    *parts, coefficients = ready(
        col_bits, after(gates, early_parts[0]), phases, angles, bits, coupled, pair
    )
    early_parts = [swap(part, "hi", d) for part, d in zip(early_parts, early, strict=True)]
    for part in late_parts[: len(beside)]:
        near_other = after(near_other, part)
    own_part, *near_parts = combine(
        top_bit, 1 + len(near), near_part, after(near_other, coefficients), pair
    )
    late_part = joined([after(part, own_part) for part in late_parts], LATE_COST)
    late_other = cross(late_part)
    near_parts = [swap(part, "hi", d) for part, d in zip(near_parts, near, strict=True)]
    half = len(early) // 2
    half_part = joined(early_parts[:half], HALF_COST)
    total = middle((1,), near, piece_rows, parts, [after(part, half_part) for part in near_parts])
    gated = second(
        (0, 2, 3),
        late,
        early[:half],
        (0,) + early[half:],
        piece_rows,
        top_bit,
        parts,
        total,
        pair,
        late_part,
        after(late_other, total),
        [half_part, own_part] + early_parts[half:],
    )
    return last(gated, swap(gated, "lo", 1), coefficients)


def solution(mesh):
    placed = (
        P(None, ("hi", "lo"), None, None),
        P(),
        P(),
        P(None, ("hi", "lo")),
        P(),
        P(),
        P(),
        P(),
    )
    return jax.shard_map(
        shards,
        mesh=mesh,
        in_specs=placed,
        out_specs=P(None, ("hi", "lo"), None, None),
        check_vma=False,
    )
```

time: 53.6 us -> 43.7 us (0.82)
  waiting for transfers between devices: 18.6 us -> 9.55 us
  local copies, waits for them, and re-layouts: 6.88 us -> 0.02 us
  starting transfers between devices: 17.1 us -> 20.4 us
  Pallas kernels: 10.6 us -> 13.5 us
    ppermute x12 -> x11, waiting for transfers between devices: 18.6 us -> 9.55 us  [swap(): lax.ppermute(value, axis, [(i, i ^ mask) for i in range(lax.axis_size(axi...]
    unnamed x20 -> x10, local copies, waits for them, and re-layouts: 6.86 us -> 0.02 us
    ppermute x12 -> x11, starting transfers between devices: 17.1 us -> 20.4 us  [swap(): lax.ppermute(value, axis, [(i, i ^ mask) for i in range(lax.axis_size(axi...]
    pallas_call x4 -> x7, Pallas kernels: 9.92 us -> 12.1 us  [the longest x1 4.86 us: first(): pl.pallas_call(functools.partial(first_kernel, groups, piece_rows, col_bi...]
    pallas_call x1 -> x2, Pallas kernels: 0.68 us -> 1.39 us  [combine(): pl.pallas_call(functools.partial(combine_kernel, top_bit), out_shape=[jax...]
  transfers between devices with their start and end apart: 12 -> 11, of which waited for: 5 -> 6; matrix products, arithmetic and copies ran while one was open for 0% -> 0% of each run, Pallas kernels for 6% -> 11%
where the time goes in v2:
time: 43.7 us; the launch traced here: 43.5 us
  starting transfers between devices  20.4 us (47%)
  Pallas kernels  13.5 us (31%)
  waiting for transfers between devices  9.55 us (22%)
    ppermute x11, starting transfers between devices, swap(): lax.ppermute(value, axis, [(i, i ^ mask) for i in range(lax.axis_size(axi...  20.4 us
    ppermute x11, waiting for transfers between devices, swap(): lax.ppermute(value, axis, [(i, i ^ mask) for i in range(lax.axis_size(axi...  9.55 us
    pallas_call x1, Pallas kernels, first(): pl.pallas_call(functools.partial(first_kernel, groups, piece_rows, col_bi...  4.86 us
    pallas_call x1, Pallas kernels, ready(): pl.pallas_call(functools.partial(ready_kernel, col_bits), out_shape=[jax....  2.56 us
    pallas_call x1, Pallas kernels, second(): pl.pallas_call(functools.partial(second_kernel, quarters, exchanged, grou...  2.2 us
    pallas_call x1, Pallas kernels, last(): pl.pallas_call(last_kernel, grid=(rows // step,), out_shape=jax.ShapeDtyp...  1.77 us
    pallas_call x2, Pallas kernels, combine(): pl.pallas_call(functools.partial(combine_kernel, top_bit), out_shape=[jax...  1.39 us
  transfers between devices with their start and end apart: 11, of which 6 were waited for; matrix products, arithmetic and copies ran while one was open for 0% of the time, Pallas kernels for 11%

profile of v2, /device:TPU:0, one launch (start us, length us, event | category | flops | bytes accessed | tf_op | source)
XLA Modules:
  0.0 43.5 jit_solution(895170322516048379)
XLA Ops:
  0.0 0.0 copy-start.2
  0.0 0.0 copy-start.4
  0.0 0.0 copy-start.1
  0.0 0.0 copy-start.3
  0.0 0.0 copy-start
  0.0 4.9 %first.1 = (f32[2,128,256]{2,1,0:T(8,128)S(1)}, f32[2,192,256]{2,1,0:T(8,128)S(1)}, f32[2,64,256]{2,1,0:T(8,128)S(1)}, f32[2,64,256]{2,1,0:T(8,128)S(1)}, f32[2,64,256]{2,1,0:T(8,128)S(1)}) custom-call(f32[2,1,512,256]{3,2,1,0:T(8,128)} %amplitudes_hbm.1, f32[2,2,512,512]{3,2,1,0:T(8,128)} %gates_hbm.2, f32[2,17]{1,0:T(2,128)} %phases_ref.1, ...), custom_call_target="tpu_custom_call" | custom-call | flops 1000 | bytes 1000 | tf_op jit(solution)/shard_map/first/pallas_call | solution.py:254
  4.9 3.0 %collective-permute-start = (f32[2,128,256]{2,1,0:T(8,128)S(1)}, f32[2,128,256]{2,1,0:T(8,128)S(1)}, u32[]{:S(2)}, u32[]{:S(2)}) collective-permute-start(f32[2,128,256]{2,1,0:T(8,128)S(1)} %get-tuple-element.29.own_ref), channel_id=1, source_target_pairs={{0,2},{1,3},{2,0},{3,1},{4,6},{5,7},{6,4},{7,5},{8,10},{9,11},{10,... | collective-permute-start | bytes 786440 | tf_op jit(solution)/shard_map/ppermute | solution.py:520
  7.9 0.1 collective-permute-start.1
  8.0 2.0 %collective-permute-start.2 = (f32[2,64,256]{2,1,0:T(8,128)S(1)}, f32[2,64,256]{2,1,0:T(8,128)S(1)}, u32[]{:S(2)}, u32[]{:S(2)}) collective-permute-start(f32[2,64,256]{2,1,0:T(8,128)S(1)} %get-tuple-element.37), channel_id=1, source_target_pairs={{0,4},{4,0},{8,12},{12,8},{16,20},{20,16},{24,28},{28,24},{1,5},{5... | collective-permute-start | bytes 393224 | tf_op jit(solution)/shard_map/ppermute | solution.py:520
  10.0 2.6 %collective-permute-start.6 = (f32[2,64,256]{2,1,0:T(8,128)S(1)}, f32[2,64,256]{2,1,0:T(8,128)S(1)}, u32[]{:S(2)}, u32[]{:S(2)}) collective-permute-start(f32[2,64,256]{2,1,0:T(8,128)S(1)} %get-tuple-element.47), channel_id=1, source_target_pairs={{0,16},{4,20},{8,24},{12,28},{16,0},{20,4},{24,8},{28,12},{1,17},{... | collective-permute-start | bytes 393224 | tf_op jit(solution)/shard_map/ppermute | solution.py:520
  12.6 0.0 collective-permute-start.7
  12.6 2.5 %collective-permute-done.other_ref = f32[2,128,256]{2,1,0:T(8,128)S(1)} collective-permute-done((f32[2,128,256]{2,1,0:T(8,128)S(1)}, f32[2,128,256]{2,1,0:T(8,128)S(1)}, u32[]{:S(2)}, u32[]{:S(2)}) %collective-permute-start) | collective-permute-done | bytes 262176 | tf_op jit(solution)/shard_map/ppermute | solution.py:520
  15.0 0.0 copy-done
  15.0 0.7 %combine.2 = (f32[2,64,256]{2,1,0:T(8,128)S(1)}, f32[2,64,256]{2,1,0:T(8,128)S(1)}) custom-call(f32[2,128,256]{2,1,0:T(8,128)S(1)} %get-tuple-element.29.own_ref, f32[2,128,256]{2,1,0:T(8,128)S(1)} %collective-permute-done.other_ref, f32[2,2,2,2]{3,2,1,0:T(2,128)S(1)} %copy-done), custom_call_target="tpu_custom_call" | custom-call | flops 1000 | bytes 1000 | tf_op jit(solution)/shard_map/combine/pallas_call | solution.py:365
  15.7 4.2 %collective-permute-start.4 = (f32[2,64,256]{2,1,0:T(8,128)S(1)}, f32[2,64,256]{2,1,0:T(8,128)S(1)}, u32[]{:S(2)}, u32[]{:S(2)}) collective-permute-start(f32[2,64,256]{2,1,0:T(8,128)S(1)} %get-tuple-element.30), channel_id=1, source_target_pairs={{0,24},{4,28},{8,16},{12,20},{16,8},{20,12},{24,0},{28,4},{1,25},{... | collective-permute-start | bytes 393224 | tf_op jit(solution)/shard_map/ppermute | solution.py:520
  20.0 0.0 copy-done.2
  20.0 0.0 copy-done.4
  20.0 0.0 copy-done.1
  20.0 0.0 copy-done.3
  20.0 2.6 %ready.1 = (bf16[512,1024]{1,0:T(8,128)(2,1)S(1)}, bf16[512,1024]{1,0:T(8,128)(2,1)S(1)}, f32[512,128]{1,0:T(8,128)S(1)}, f32[512,128]{1,0:T(8,128)S(1)}, f32[8,256]{1,0:T(8,128)S(1)}) custom-call(f32[2,2,512,512]{3,2,1,0:T(8,128)} %gates_hbm.2, f32[2,17]{1,0:T(2,128)S(1)} %copy-done.1, f32[1,2]{1,0:T(1,128)S(1)} %bitcast.2, s32[17]{0:T(128)S(1)} %copy-done.4, ...), custom_call_target="tpu_custom_call" | custom-call | flops 1500001024 | bytes 1000 | tf_op jit(solution)/shard_map/ready/pallas_call | solution.py:317
  22.5 0.0 collective-permute-done.2.refs_0_
  22.6 0.1 collective-permute-done.1.other_ref
  22.6 0.7 %combine.3 = (f32[2,64,256]{2,1,0:T(8,128)S(1)}, f32[2,64,256]{2,1,0:T(8,128)S(1)}, f32[2,64,256]{2,1,0:T(8,128)S(1)}) custom-call(f32[2,192,256]{2,1,0:T(8,128)S(1)} %get-tuple-element.36.own_ref, f32[2,192,256]{2,1,0:T(8,128)S(1)} %collective-permute-done.1.other_ref, f32[2,2,2,2]{3,2,1,0:T(2,128)S(1)} %copy-done), custom_call_target="tpu_custom_call" | custom-call | flops 1000 | bytes 1000 | tf_op jit(solution)/shard_map/combine/pallas_call | solution.py:365
  23.4 1.9 %collective-permute-start.3 = (f32[2,64,256]{2,1,0:T(8,128)S(1)}, f32[2,64,256]{2,1,0:T(8,128)S(1)}, u32[]{:S(2)}, u32[]{:S(2)}) collective-permute-start(f32[2,64,256]{2,1,0:T(8,128)S(1)} %get-tuple-element.41), channel_id=1, source_target_pairs={{0,8},{4,12},{8,0},{12,4},{16,24},{20,28},{24,16},{28,20},{1,9},{5... | collective-permute-start | bytes 393224 | tf_op jit(solution)/shard_map/ppermute | solution.py:520
  25.2 1.4 %collective-permute-start.5 = (f32[2,64,256]{2,1,0:T(8,128)S(1)}, f32[2,64,256]{2,1,0:T(8,128)S(1)}, u32[]{:S(2)}, u32[]{:S(2)}) collective-permute-start(f32[2,64,256]{2,1,0:T(8,128)S(1)} %get-tuple-element.43), channel_id=1, source_target_pairs={{0,12},{4,8},{8,4},{12,0},{16,28},{20,24},{24,20},{28,16},{1,13},{... | collective-permute-start | bytes 393224 | tf_op jit(solution)/shard_map/ppermute | solution.py:520
  26.7 0.8 %collective-permute-done.7.refs_2_ = f32[2,64,256]{2,1,0:T(8,128)S(1)} collective-permute-done((f32[2,64,256]{2,1,0:T(8,128)S(1)}, f32[2,64,256]{2,1,0:T(8,128)S(1)}, u32[]{:S(2)}, u32[]{:S(2)}) %collective-permute-start.7) | collective-permute-done | bytes 131104 | tf_op jit(solution)/shard_map/ppermute | solution.py:520
  27.4 0.0 collective-permute-done.6.refs_1_
  27.5 1.7 %collective-permute-start.8 = (f32[2,192,256]{2,1,0:T(8,128)S(1)}, f32[2,192,256]{2,1,0:T(8,128)S(1)}, u32[]{:S(2)}, u32[]{:S(2)}) collective-permute-start(f32[2,192,256]{2,1,0:T(8,128)S(1)} %joined.3.refs_6_), channel_id=1, source_target_pairs={{0,2},{1,3},{2,0},{3,1},{4,6},{5,7},{6,4},{7,5},{8,10},{9,11},{10,... | collective-permute-start | bytes 1179656 | tf_op jit(solution)/shard_map/ppermute | solution.py:520
  29.2 3.4 %collective-permute-start.9 = (f32[2,64,256]{2,1,0:T(8,128)S(1)}, f32[2,64,256]{2,1,0:T(8,128)S(1)}, u32[]{:S(2)}, u32[]{:S(2)}) collective-permute-start(f32[2,64,256]{2,1,0:T(8,128)S(1)} %get-tuple-element.52), channel_id=1, source_target_pairs={{0,28},{4,24},{8,20},{12,16},{16,12},{20,8},{24,4},{28,0},{1,29},{... | collective-permute-start | bytes 393224 | tf_op jit(solution)/shard_map/ppermute | solution.py:520
  32.6 0.0 collective-permute-done.4.refs_0_
  32.6 0.0 collective-permute-done.3.refs_4_
  32.6 0.0 collective-permute-done.5.refs_5_
  32.6 0.6 %middle.1.refs_4_ = f32[2,512,256]{2,1,0:T(8,128)S(1)} custom-call(bf16[512,1024]{1,0:T(8,128)(2,1)S(1)} %get-tuple-element.32.refs_0_, bf16[512,1024]{1,0:T(8,128)(2,1)S(1)} %get-tuple-element.33.refs_1_, f32[512,128]{1,0:T(8,128)S(1)} %get-tuple-element.34.refs_2_, f32[512,128]{1,0:T(8,128)S(1)} %get-tuple-element.35.refs_3_, ...), custom_call_target="tpu_custom_call" | custom-call | flops 3000000000 | bytes 1000 | tf_op jit(solution)/shard_map/middle/pallas_call | solution.py:451
  33.3 3.3 %collective-permute-done.8.refs_7_ = f32[2,192,256]{2,1,0:T(8,128)S(1)} collective-permute-done((f32[2,192,256]{2,1,0:T(8,128)S(1)}, f32[2,192,256]{2,1,0:T(8,128)S(1)}, u32[]{:S(2)}, u32[]{:S(2)}) %collective-permute-start.8) | collective-permute-done | bytes 393248 | tf_op jit(solution)/shard_map/ppermute | solution.py:520
  36.5 0.3 collective-permute-done.9.refs_10_
  36.8 2.2 %second.1.own_ref = f32[2,512,256]{2,1,0:T(8,128)S(1)} custom-call(bf16[512,1024]{1,0:T(8,128)(2,1)S(1)} %get-tuple-element.32.refs_0_, bf16[512,1024]{1,0:T(8,128)(2,1)S(1)} %get-tuple-element.33.refs_1_, f32[512,128]{1,0:T(8,128)S(1)} %get-tuple-element.34.refs_2_, f32[512,128]{1,0:T(8,128)S(1)} %get-tuple-element.35.refs_3_, ...), custom_call_target="tpu_custom_call" | custom-call | flops 1000 | bytes 1000 | tf_op jit(solution)/shard_map/second/pallas_call | solution.py:484
  39.0 0.1 collective-permute-start.10
  39.1 2.6 %collective-permute-done.10.other_ref = f32[2,512,256]{2,1,0:T(8,128)S(1)} collective-permute-done((f32[2,512,256]{2,1,0:T(8,128)S(1)}, f32[2,512,256]{2,1,0:T(8,128)S(1)}, u32[]{:S(2)}, u32[]{:S(2)}) %collective-permute-start.10) | collective-permute-done | bytes 1048608 | tf_op jit(solution)/shard_map/ppermute | solution.py:520
  41.8 1.8 %last.1 = f32[2,1,512,256]{3,2,1,0:T(8,128)} custom-call(f32[2,512,256]{2,1,0:T(8,128)S(1)} %second.1.own_ref, f32[2,512,256]{2,1,0:T(8,128)S(1)} %collective-permute-done.10.other_ref, f32[8,256]{1,0:T(8,128)S(1)} %get-tuple-element.39.coefficients_ref), custom_call_target="tpu_custom_call" | custom-call | flops 1000 | bytes 1000 | tf_op jit(solution)/shard_map/last/pallas_call | solution.py:507
  (2 shorter events, 0.0 us)
Async XLA Ops:
  0.0 20.0 %copy-start.2 = (s32[2,17]{1,0:T(2,128)S(1)}, s32[2,17]{1,0:T(2,128)}, u32[]{:S(2)}) copy-start(s32[2,17]{1,0:T(2,128)} %coupled_ref.1) | copy-start | bytes 412
  0.0 20.0 %copy-start.4 = (s32[17]{0:T(128)S(1)}, s32[17]{0:T(128)}, u32[]{:S(2)}) copy-start(s32[17]{0:T(128)} %bits_ref.1) | copy-start | bytes 208
  0.0 20.0 %copy-start.1 = (f32[2,17]{1,0:T(2,128)S(1)}, f32[2,17]{1,0:T(2,128)}, u32[]{:S(2)}) copy-start(f32[2,17]{1,0:T(2,128)} %phases_ref.1) | copy-start | bytes 412
  0.0 20.0 %copy-start.3 = (f32[2,1]{0,1:T(1,128)S(1)}, f32[2,1]{0,1:T(1,128)}, u32[]{:S(2)}) copy-start(f32[2,1]{0,1:T(1,128)} %param.11) | copy-start | bytes 28
  0.0 15.0 %copy-start = (f32[2,2,2,2]{3,2,1,0:T(2,128)S(1)}, f32[2,2,2,2]{3,2,1,0:T(2,128)}, u32[]{:S(2)}) copy-start(f32[2,2,2,2]{3,2,1,0:T(2,128)} %refs_5_.1) | copy-start | bytes 196
  4.9 10.2 %collective-permute-start = (f32[2,128,256]{2,1,0:T(8,128)S(1)}, f32[2,128,256]{2,1,0:T(8,128)S(1)}, u32[]{:S(2)}, u32[]{:S(2)}) collective-permute-start(f32[2,128,256]{2,1,0:T(8,128)S(1)} %get-tuple-element.29.own_ref), channel_id=1, source_target_pairs={{0,2},{1,3},{2,0},{3,1},{4,6},{5,7},{6,4},{7,5},{8,10},{9,11},{10,... | collective-permute-start | bytes 786440 | tf_op jit(solution)/shard_map/ppermute | solution.py:520
  7.9 14.7 %collective-permute-start.1 = (f32[2,192,256]{2,1,0:T(8,128)S(1)}, f32[2,192,256]{2,1,0:T(8,128)S(1)}, u32[]{:S(2)}, u32[]{:S(2)}) collective-permute-start(f32[2,192,256]{2,1,0:T(8,128)S(1)} %get-tuple-element.36.own_ref), channel_id=1, source_target_pairs={{0,2},{1,3},{2,0},{3,1},{4,6},{5,7},{6,4},{7,5},{8,10},{9,11},{10,... | collective-permute-start | bytes 1179656 | tf_op jit(solution)/shard_map/ppermute | solution.py:520
  8.0 14.6 %collective-permute-start.2 = (f32[2,64,256]{2,1,0:T(8,128)S(1)}, f32[2,64,256]{2,1,0:T(8,128)S(1)}, u32[]{:S(2)}, u32[]{:S(2)}) collective-permute-start(f32[2,64,256]{2,1,0:T(8,128)S(1)} %get-tuple-element.37), channel_id=1, source_target_pairs={{0,4},{4,0},{8,12},{12,8},{16,20},{20,16},{24,28},{28,24},{1,5},{5... | collective-permute-start | bytes 393224 | tf_op jit(solution)/shard_map/ppermute | solution.py:520
  10.0 17.5 %collective-permute-start.6 = (f32[2,64,256]{2,1,0:T(8,128)S(1)}, f32[2,64,256]{2,1,0:T(8,128)S(1)}, u32[]{:S(2)}, u32[]{:S(2)}) collective-permute-start(f32[2,64,256]{2,1,0:T(8,128)S(1)} %get-tuple-element.47), channel_id=1, source_target_pairs={{0,16},{4,20},{8,24},{12,28},{16,0},{20,4},{24,8},{28,12},{1,17},{... | collective-permute-start | bytes 393224 | tf_op jit(solution)/shard_map/ppermute | solution.py:520
  12.6 14.9 %collective-permute-start.7 = (f32[2,64,256]{2,1,0:T(8,128)S(1)}, f32[2,64,256]{2,1,0:T(8,128)S(1)}, u32[]{:S(2)}, u32[]{:S(2)}) collective-permute-start(f32[2,64,256]{2,1,0:T(8,128)S(1)} %get-tuple-element.49), channel_id=1, source_target_pairs={{0,20},{4,16},{8,28},{12,24},{16,4},{20,0},{24,12},{28,8},{1,21},{... | collective-permute-start | bytes 393224 | tf_op jit(solution)/shard_map/ppermute | solution.py:520
  15.7 16.9 %collective-permute-start.4 = (f32[2,64,256]{2,1,0:T(8,128)S(1)}, f32[2,64,256]{2,1,0:T(8,128)S(1)}, u32[]{:S(2)}, u32[]{:S(2)}) collective-permute-start(f32[2,64,256]{2,1,0:T(8,128)S(1)} %get-tuple-element.30), channel_id=1, source_target_pairs={{0,24},{4,28},{8,16},{12,20},{16,8},{20,12},{24,0},{28,4},{1,25},{... | collective-permute-start | bytes 393224 | tf_op jit(solution)/shard_map/ppermute | solution.py:520
  23.4 9.3 %collective-permute-start.3 = (f32[2,64,256]{2,1,0:T(8,128)S(1)}, f32[2,64,256]{2,1,0:T(8,128)S(1)}, u32[]{:S(2)}, u32[]{:S(2)}) collective-permute-start(f32[2,64,256]{2,1,0:T(8,128)S(1)} %get-tuple-element.41), channel_id=1, source_target_pairs={{0,8},{4,12},{8,0},{12,4},{16,24},{20,28},{24,16},{28,20},{1,9},{5... | collective-permute-start | bytes 393224 | tf_op jit(solution)/shard_map/ppermute | solution.py:520
  25.2 7.4 %collective-permute-start.5 = (f32[2,64,256]{2,1,0:T(8,128)S(1)}, f32[2,64,256]{2,1,0:T(8,128)S(1)}, u32[]{:S(2)}, u32[]{:S(2)}) collective-permute-start(f32[2,64,256]{2,1,0:T(8,128)S(1)} %get-tuple-element.43), channel_id=1, source_target_pairs={{0,12},{4,8},{8,4},{12,0},{16,28},{20,24},{24,20},{28,16},{1,13},{... | collective-permute-start | bytes 393224 | tf_op jit(solution)/shard_map/ppermute | solution.py:520
  27.5 9.1 %collective-permute-start.8 = (f32[2,192,256]{2,1,0:T(8,128)S(1)}, f32[2,192,256]{2,1,0:T(8,128)S(1)}, u32[]{:S(2)}, u32[]{:S(2)}) collective-permute-start(f32[2,192,256]{2,1,0:T(8,128)S(1)} %joined.3.refs_6_), channel_id=1, source_target_pairs={{0,2},{1,3},{2,0},{3,1},{4,6},{5,7},{6,4},{7,5},{8,10},{9,11},{10,... | collective-permute-start | bytes 1179656 | tf_op jit(solution)/shard_map/ppermute | solution.py:520
  29.2 7.7 %collective-permute-start.9 = (f32[2,64,256]{2,1,0:T(8,128)S(1)}, f32[2,64,256]{2,1,0:T(8,128)S(1)}, u32[]{:S(2)}, u32[]{:S(2)}) collective-permute-start(f32[2,64,256]{2,1,0:T(8,128)S(1)} %get-tuple-element.52), channel_id=1, source_target_pairs={{0,28},{4,24},{8,20},{12,16},{16,12},{20,8},{24,4},{28,0},{1,29},{... | collective-permute-start | bytes 393224 | tf_op jit(solution)/shard_map/ppermute | solution.py:520
  39.0 2.7 %collective-permute-start.10 = (f32[2,512,256]{2,1,0:T(8,128)S(1)}, f32[2,512,256]{2,1,0:T(8,128)S(1)}, u32[]{:S(2)}, u32[]{:S(2)}) collective-permute-start(f32[2,512,256]{2,1,0:T(8,128)S(1)} %second.1.own_ref), channel_id=1, source_target_pairs={{0,1},{1,0},{2,3},{3,2},{4,5},{5,4},{6,7},{7,6},{8,9},{9,8},{10,11... | collective-permute-start | bytes 3145736 | tf_op jit(solution)/shard_map/ppermute | solution.py:520

commit v3 on v2

--- a/solution.py
+++ b/solution.py
@@ -89,6 +89,12 @@
     return jnp.dot(a, b, preferred_element_type=F32)
 
 
+def signed_block(r, i):
+    return jnp.concatenate(
+        [jnp.concatenate([r, i], axis=1), jnp.concatenate([-i, r], axis=1)], axis=0
+    )
+
+
 def turned_rows(real, imag, phase_real, phase_imag):
     reps = real.shape[1] // phase_real.shape[1]
     phase_real = jnp.concatenate([phase_real] * reps, axis=1)
@@ -96,13 +102,7 @@
     real, imag = turn(real, imag, phase_real, phase_imag)
     real_high, real_low = split(real)
     imag_high, imag_low = split(imag)
-
-    def block(r, i):
-        return jnp.concatenate(
-            [jnp.concatenate([r, i], axis=1), jnp.concatenate([-i, r], axis=1)], axis=0
-        )
-
-    return block(real_high, imag_high), block(real_low, imag_low)
+    return signed_block(real_high, imag_high), signed_block(real_low, imag_low)
 
 
 def product(left_high, left_low, right_high, right_low):
@@ -163,13 +163,13 @@
     )
 
 
-def gate_pieces(groups, piece_rows, layout_ref, gate_high, gate_low, right_high, right_low, out_refs):
-    rows = gate_high.shape[0]
+def gate_pieces(groups, piece_rows, layout_ref, left_high, left_low, right_high, right_low, out_refs):
+    rows = left_high.shape[0]
     cols = right_high.shape[1] // 2
+    gated = product(left_high, left_low, right_high, right_low)
     chosen = chosen_rows([d for group in groups for d in group], piece_rows, rows, layout_ref)
-    left_high = dot(chosen, gate_high).astype(BF16)
-    left_low = dot(chosen, gate_low).astype(BF16)
-    out = product(left_high, left_low, right_high, right_low)
+    gated_high, gated_low = split(gated)
+    out = dot(chosen, gated_high) + dot(chosen, gated_low)
     start = 0
     for group, out_ref in zip(groups, out_refs, strict=True):
         size = len(group) * piece_rows
@@ -272,20 +272,29 @@
     )(*[hbm(source) for source in sources])
 
 
+def own_order(tile, piece_rows, me):
+    lane = lax.broadcasted_iota(jnp.int32, tile.shape, 1)
+    width = tile.shape[1]
+    size = piece_rows
+    bit = 0
+    while size < width:
+        upper = (lane & size) != 0
+        swapped = jnp.where(
+            upper, pltpu.roll(tile, size, 1), pltpu.roll(tile, width - size, 1)
+        )
+        tile = jnp.where(((me >> bit) & 1) == 1, swapped, tile)
+        size *= 2
+        bit += 1
+    return tile
+
+
 def ready_kernel(
-    col_bits, gates_hbm, phases_ref, angles_ref, bits_ref, coupled_ref, pair_ref, *refs
+    sets, piece_rows, col_bits, gates_hbm, phases_ref, angles_ref, bits_ref, coupled_ref, pair_ref, *refs
 ):
-    (
-        gate_high_ref,
-        gate_low_ref,
-        phase_real_ref,
-        phase_imag_ref,
-        coefficients_ref,
-        gates_ref,
-        sem,
-    ) = refs
+    *out_refs, coefficients_ref, gates_ref, phase_real_ref, phase_imag_ref, sem = refs
     copy = pltpu.make_async_copy(gates_hbm.at[1], gates_ref, sem)
     copy.start()
+    me = lax.axis_index("hi")
     rows = gates_ref.shape[1]
     cols = coefficients_ref.shape[1]
     row_bits = rows.bit_length() - 1
@@ -305,27 +314,55 @@
         coefficients_ref[i : i + 1, :] = c[i]
     coefficients_ref[4:8, :] = jnp.zeros((4, cols), F32)
     copy.wait()
+    size = rows // 4
+    quarter = size // piece_rows
+    high, low = [], []
     for i in range(2):
-        high, low = split(gates_ref[i])
-        gate_high_ref[:, i * rows : (i + 1) * rows] = high
-        gate_low_ref[:, i * rows : (i + 1) * rows] = low
-
-
-def ready(col_bits, gates, phases, angles, bits, coupled, pair):
+        high_tiles, low_tiles = [], []
+        for q in range(4):
+            start = pl.multiple_of(((me // quarter) ^ q) * size, size)
+            tile = own_order(gates_ref[i, :, pl.ds(start, size)], piece_rows, me)
+            for tiles, part in zip((high_tiles, low_tiles), split(tile), strict=True):
+                tiles.append(part)
+        high.append(jnp.concatenate(high_tiles, axis=1))
+        low.append(jnp.concatenate(low_tiles, axis=1))
+    for k, steps in enumerate(sets):
+        for part, out_ref in zip((high, low), out_refs[4 * k : 4 * k + 2], strict=True):
+            out_ref[...] = jnp.concatenate(
+                [
+                    part[i][:, d * piece_rows : (d + 1) * piece_rows]
+                    for i in range(2)
+                    for d in steps
+                ],
+                axis=1,
+            )
+        for j, d in enumerate(steps):
+            start = pl.multiple_of((me ^ d) * piece_rows, piece_rows)
+            target = slice(j * piece_rows, (j + 1) * piece_rows)
+            out_refs[4 * k + 2][target, :] = phase_real_ref[pl.ds(start, piece_rows), :]
+            out_refs[4 * k + 3][target, :] = phase_imag_ref[pl.ds(start, piece_rows), :]
+
+
+def ready(sets, piece_rows, col_bits, gates, phases, angles, bits, coupled, pair):
     rows = gates.shape[2]
     cols = 1 << col_bits
-    return pl.pallas_call(
-        functools.partial(ready_kernel, col_bits),
-        out_shape=[
-            jax.ShapeDtypeStruct((rows, 2 * rows), BF16),
-            jax.ShapeDtypeStruct((rows, 2 * rows), BF16),
-            jax.ShapeDtypeStruct((rows, 128), F32),
-            jax.ShapeDtypeStruct((rows, 128), F32),
-            jax.ShapeDtypeStruct((8, cols), F32),
+    shapes = []
+    for steps in sets:
+        depth = len(steps) * piece_rows
+        shapes += [jax.ShapeDtypeStruct((rows, 2 * depth), BF16)] * 2
+        shapes += [jax.ShapeDtypeStruct((depth, 128), F32)] * 2
+    shapes.append(jax.ShapeDtypeStruct((8, cols), F32))
+    return pl.pallas_call(
+        functools.partial(ready_kernel, sets, piece_rows, col_bits),
+        out_shape=shapes,
+        in_specs=[any_space(), vmem(), vmem(), smem(), smem(), smem()],
+        out_specs=[vmem()] * len(shapes),
+        scratch_shapes=[
+            pltpu.VMEM(gates.shape[1:], F32),
+            pltpu.VMEM((rows, 128), F32),
+            pltpu.VMEM((rows, 128), F32),
+            pltpu.SemaphoreType.DMA,
         ],
-        in_specs=[any_space(), vmem(), vmem(), smem(), smem(), smem()],
-        out_specs=[vmem()] * 5,
-        scratch_shapes=[pltpu.VMEM(gates.shape[1:], F32), pltpu.SemaphoreType.DMA],
         compiler_params=params(),
         cost_estimate=cost(READY_COST),
         name="ready",
@@ -373,43 +410,6 @@
     )(own, other, pair_gates)
 
 
-def partial_product(quarters, pieces, piece_rows, parts_refs, scratch_refs):
-    gate_high_ref, gate_low_ref, phase_real_ref, phase_imag_ref = parts_refs
-    real_ref, imag_ref = scratch_refs
-    rows = gate_high_ref.shape[0]
-    size = rows // 4
-    quarter = size // piece_rows
-    me = lax.axis_index("hi")
-    for step, (real, imag) in pieces.items():
-        offset = quarters.index(step // quarter) * size
-        start = offset + ((me ^ step) & (quarter - 1)) * piece_rows
-        start = pl.multiple_of(start, piece_rows)
-        real_ref[pl.ds(start, piece_rows), :] = real
-        imag_ref[pl.ds(start, piece_rows), :] = imag
-    starts = [pl.multiple_of(((me // quarter) ^ q) * size, size) for q in quarters]
-
-    def some_rows(ref):
-        return jnp.concatenate([ref[pl.ds(start, size), :] for start in starts], axis=0)
-
-    def some_cols(ref):
-        shift = (0, rows)
-        return jnp.concatenate(
-            [
-                ref[:, pl.ds(pl.multiple_of(start + extra, size), size)]
-                for extra in shift
-                for start in starts
-            ],
-            axis=1,
-        )
-
-    right_high, right_low = turned_rows(
-        real_ref[...], imag_ref[...], some_rows(phase_real_ref), some_rows(phase_imag_ref)
-    )
-    out = product(some_cols(gate_high_ref), some_cols(gate_low_ref), right_high, right_low)
-    cols = real_ref.shape[1]
-    return out[:, :cols], out[:, cols:]
-
-
 def late_kernel(*refs):
     *part_refs, out_ref = refs
     size = part_refs[0].shape[1]
@@ -430,90 +430,124 @@
     )(*arrays)
 
 
-def split_pieces(ref, steps, piece_rows):
-    pieces = {}
-    for i, step in enumerate(steps):
-        part = slice(i * piece_rows, (i + 1) * piece_rows)
-        pieces[step] = (ref[0, part], ref[1, part])
-    return pieces
-
-
-def middle_kernel(quarters, landed, piece_rows, *refs):
-    landed_refs = refs[4:-3]
-    out_ref = refs[-3]
-    pieces = {step: (ref[0], ref[1]) for step, ref in zip(landed, landed_refs, strict=True)}
-    out_ref[0], out_ref[1] = partial_product(quarters, pieces, piece_rows, refs[:4], refs[-2:])
-
-
-def middle(quarters, landed, piece_rows, parts, arrays):
-    rows = parts[0].shape[0]
-    cols = arrays[0].shape[2]
-    return pl.pallas_call(
-        functools.partial(middle_kernel, quarters, landed, piece_rows),
-        out_shape=jax.ShapeDtypeStruct((2, rows, cols), F32),
-        in_specs=[vmem()] * (4 + len(arrays)),
+def turned_pieces_kernel(phase_real_ref, phase_imag_ref, *refs):
+    *piece_refs, out_ref = refs
+    reps = out_ref.shape[2] // phase_real_ref.shape[1]
+    start = 0
+    for ref in piece_refs:
+        part = slice(start, start + ref.shape[1])
+        cosine = jnp.concatenate([phase_real_ref[part, :]] * reps, axis=1)
+        sine = jnp.concatenate([phase_imag_ref[part, :]] * reps, axis=1)
+        out_ref[0, part], out_ref[1, part] = turn(ref[0], ref[1], cosine, sine)
+        start += ref.shape[1]
+
+
+def turned_pieces(phase_parts, arrays):
+    shape = (2, sum(a.shape[1] for a in arrays), arrays[0].shape[2])
+    return pl.pallas_call(
+        turned_pieces_kernel,
+        out_shape=jax.ShapeDtypeStruct(shape, F32),
+        in_specs=[vmem()] * (2 + len(arrays)),
         out_specs=vmem(),
-        scratch_shapes=[pltpu.VMEM((len(quarters) * rows // 4, cols), F32)] * 2,
         compiler_params=params(),
         cost_estimate=cost(MIDDLE_COST),
+        name="turned_pieces",
+    )(*phase_parts, *arrays)
+
+
+def mixed_parts(coefficients_ref, own_ref, other_ref):
+    c = [coefficients_ref[i : i + 1, :] for i in range(4)]
+    real, imag = combined(own_ref, other_ref, c)
+    real_high, real_low = split(real)
+    imag_high, imag_low = split(imag)
+    return signed_block(real_high, imag_high), signed_block(real_low, imag_low)
+
+
+def middle_kernel(high_ref, low_ref, coefficients_ref, own_ref, other_ref, out_ref):
+    cols = out_ref.shape[2]
+    right_high, right_low = mixed_parts(coefficients_ref, own_ref, other_ref)
+    out = product(high_ref[...], low_ref[...], right_high, right_low)
+    out_ref[0] = out[:, :cols]
+    out_ref[1] = out[:, cols:]
+
+
+def middle(parts, coefficients, own, other):
+    return pl.pallas_call(
+        middle_kernel,
+        out_shape=jax.ShapeDtypeStruct((2, parts[0].shape[0], own.shape[2]), F32),
+        in_specs=[vmem()] * 5,
+        out_specs=vmem(),
+        compiler_params=params(),
+        cost_estimate=cost(),
         name="middle",
-    )(*parts, *arrays)
-
-
-def second_kernel(quarters, exchanged, grouped, landed, piece_rows, top_bit, *refs):
-    sum_ref, pair_ref, own_ref, other_ref, group_ref = refs[4:9]
-    landed_refs = refs[9 : 9 + len(landed)]
-    out_ref = refs[-3]
+    )(*parts, coefficients, own, other)
+
+
+def turned_kernel(
+    top_bit, phase_real_ref, phase_imag_ref, pair_ref, own_ref, other_ref, last_ref, out_ref
+):
     bit = (lax.axis_index("lo") >> top_bit) & 1
-    c = pair_coefficients(pair_ref, 0, bit)
-    pieces = {step: (ref[0], ref[1]) for step, ref in zip(landed, landed_refs, strict=True)}
-    pieces.update(split_pieces(group_ref, grouped, piece_rows))
-    others = split_pieces(other_ref, exchanged, piece_rows)
-    for step, own in split_pieces(own_ref, exchanged, piece_rows).items():
-        pieces[step] = combined(own, others[step], c)
-    real, imag = partial_product(quarters, pieces, piece_rows, refs[:4], refs[-2:])
-    out_ref[0] = sum_ref[0] + real
-    out_ref[1] = sum_ref[1] + imag
-
-
-def second(
-    quarters, exchanged, grouped, landed, piece_rows, top_bit, parts, total, pair, own, other, arrays
+    size = own_ref.shape[1]
+    parts = (
+        (slice(0, size), combined(own_ref, other_ref, pair_coefficients(pair_ref, 0, bit))),
+        (slice(size, out_ref.shape[1]), (last_ref[0], last_ref[1])),
+    )
+    reps = out_ref.shape[2] // phase_real_ref.shape[1]
+    for part, (real, imag) in parts:
+        cosine = jnp.concatenate([phase_real_ref[part, :]] * reps, axis=1)
+        sine = jnp.concatenate([phase_imag_ref[part, :]] * reps, axis=1)
+        out_ref[0, part], out_ref[1, part] = turn(real, imag, cosine, sine)
+
+
+def turned(top_bit, phase_parts, pair, own, other, last):
+    shape = (2, own.shape[1] + last.shape[1], own.shape[2])
+    return pl.pallas_call(
+        functools.partial(turned_kernel, top_bit),
+        out_shape=jax.ShapeDtypeStruct(shape, F32),
+        in_specs=[vmem(), vmem(), smem(), vmem(), vmem(), vmem()],
+        out_specs=vmem(),
+        compiler_params=params(),
+        cost_estimate=cost(),
+        name="turned",
+    )(*phase_parts, pair, own, other, last)
+
+
+def last_kernel(
+    high_ref, low_ref, coefficients_ref, own_ref, other_ref, sum_ref, out_hbm, out_ref, sems
 ):
-    rows = parts[0].shape[0]
-    cols = own.shape[2]
-    return pl.pallas_call(
-        functools.partial(
-            second_kernel, quarters, exchanged, grouped, landed, piece_rows, top_bit
-        ),
-        out_shape=jax.ShapeDtypeStruct((2, rows, cols), F32),
-        in_specs=[vmem()] * 5 + [smem()] + [vmem()] * (2 + len(arrays)),
-        out_specs=vmem(),
-        scratch_shapes=[pltpu.VMEM((len(quarters) * rows // 4, cols), F32)] * 2,
-        compiler_params=params(),
-        cost_estimate=cost(),
-        name="second",
-    )(*parts, total, pair, own, other, *arrays)
-
-
-def last_kernel(own_ref, other_ref, coefficients_ref, out_ref):
-    c = [coefficients_ref[i : i + 1, :] for i in range(4)]
-    out_ref[0, 0], out_ref[1, 0] = combined(own_ref, other_ref, c)
-
-
-def last(own, other, coefficients):
-    _, rows, cols = own.shape
-    step = rows // 4
-    block = pl.BlockSpec((2, step, cols), lambda i: (0, i, 0))
+    cols = own_ref.shape[2]
+    right_high, right_low = mixed_parts(coefficients_ref, own_ref, other_ref)
+    count = sems.shape[0]
+    step = out_ref.shape[2] // count
+    copies = []
+    for i in range(count):
+        part = pl.ds(i * step, step)
+        out = product(high_ref[part, :], low_ref[part, :], right_high, right_low)
+        out_ref[0, 0, part] = sum_ref[0, part] + out[:, :cols]
+        out_ref[1, 0, part] = sum_ref[1, part] + out[:, cols:]
+        copies.append(
+            pltpu.make_async_copy(
+                out_ref.at[:, :, part], out_hbm.at[:, :, part], sems.at[i]
+            )
+        )
+        copies[-1].start()
+    for copy in copies:
+        copy.wait()
+
+
+def last(parts, coefficients, own, other, total):
+    _, rows, cols = total.shape
+    shape = (2, 1, rows, cols)
     return pl.pallas_call(
         last_kernel,
-        grid=(rows // step,),
-        out_shape=jax.ShapeDtypeStruct((2, 1, rows, cols), F32),
-        in_specs=[block, block, pl.BlockSpec((8, cols), lambda i: (0, 0))],
-        out_specs=pl.BlockSpec((2, 1, step, cols), lambda i: (0, 0, i, 0)),
+        out_shape=jax.ShapeDtypeStruct(shape, F32),
+        in_specs=[vmem()] * 6,
+        out_specs=any_space(),
+        scratch_shapes=[pltpu.VMEM(shape, F32), pltpu.SemaphoreType.DMA((2,))],
         compiler_params=params(),
         cost_estimate=cost(),
         name="last",
-    )(own, other, coefficients)
+    )(*parts, coefficients, own, other, total)
 
 
 def swap(value, axis, mask):
@@ -557,36 +591,28 @@
     late_parts = [swap(part, "hi", d) for part, d in zip(late_parts, late, strict=True)]
     near_other = cross(near_part)
     early_parts = combine(top_bit, len(early), early_part, early_other, pair)
+    sets = ((0,) + near + early[:-1], late + early[-1:])
     *parts, coefficients = ready(
-        col_bits, after(gates, early_parts[0]), phases, angles, bits, coupled, pair
+        sets, piece_rows, col_bits, after(gates, early_parts[0]), phases, angles, bits, coupled, pair
     )
     early_parts = [swap(part, "hi", d) for part, d in zip(early_parts, early, strict=True)]
-    for part in late_parts[: len(beside)]:
-        near_other = after(near_other, part)
     own_part, *near_parts = combine(
         top_bit, 1 + len(near), near_part, after(near_other, coefficients), pair
     )
     late_part = joined([after(part, own_part) for part in late_parts], LATE_COST)
     late_other = cross(late_part)
     near_parts = [swap(part, "hi", d) for part, d in zip(near_parts, near, strict=True)]
-    half = len(early) // 2
-    half_part = joined(early_parts[:half], HALF_COST)
-    total = middle((1,), near, piece_rows, parts, [after(part, half_part) for part in near_parts])
-    gated = second(
-        (0, 2, 3),
-        late,
-        early[:half],
-        (0,) + early[half:],
-        piece_rows,
-        top_bit,
-        parts,
-        total,
-        pair,
-        late_part,
-        after(late_other, total),
-        [half_part, own_part] + early_parts[half:],
-    )
-    return last(gated, swap(gated, "lo", 1), coefficients)
+    half_part = joined(early_parts[:-1], HALF_COST)
+    near_turned = turned_pieces(
+        parts[2:4], [own_part] + [after(part, half_part) for part in near_parts] + [half_part]
+    )
+    near_turned_other = swap(near_turned, "lo", 1)
+    late_turned = turned(
+        top_bit, parts[6:], pair, late_part, after(late_other, near_turned), early_parts[-1]
+    )
+    late_turned_other = swap(late_turned, "lo", 1)
+    total = middle(parts[:2], coefficients, near_turned, near_turned_other)
+    return last(parts[4:6], coefficients, late_turned, late_turned_other, total)
 
 
 def solution(mesh):

time: 43.7 us -> 41.2 us (0.943)
  waiting for transfers between devices: 9.55 us -> 8.08 us
  starting transfers between devices: 20.4 us -> 19.5 us
    ppermute x11 -> x12, waiting for transfers between devices: 9.55 us -> 8.08 us  [swap(): lax.ppermute(value, axis, [(i, i ^ mask) for i in range(lax.axis_size(axi...]
    ppermute x11 -> x12, starting transfers between devices: 20.4 us -> 19.5 us  [swap(): lax.ppermute(value, axis, [(i, i ^ mask) for i in range(lax.axis_size(axi...]
    pallas_call x4 -> x5, Pallas kernels: 7.18 us -> 7.48 us  [the longest x1 3.55 us: ready(): pl.pallas_call(functools.partial(ready_kernel, sets, piece_rows, col_bits...]
  transfers between devices with their start and end apart: 11 -> 12, of which waited for: 6 -> 6; matrix products, arithmetic and copies ran while one was open for 0% -> 0% of each run, Pallas kernels for 11% -> 17%
where the time goes in v3:
time: 41.2 us; the launch traced here: 41.1 us
  starting transfers between devices  19.5 us (47%)
  Pallas kernels  13.4 us (33%)
  waiting for transfers between devices  8.08 us (20%)
    ppermute x12, starting transfers between devices, swap(): lax.ppermute(value, axis, [(i, i ^ mask) for i in range(lax.axis_size(axi...  19.5 us
    ppermute x12, waiting for transfers between devices, swap(): lax.ppermute(value, axis, [(i, i ^ mask) for i in range(lax.axis_size(axi...  8.08 us
    pallas_call x1, Pallas kernels, first(): pl.pallas_call(functools.partial(first_kernel, groups, piece_rows, col_bi...  4.46 us
    pallas_call x1, Pallas kernels, ready(): pl.pallas_call(functools.partial(ready_kernel, sets, piece_rows, col_bits...  3.55 us
    pallas_call x1, Pallas kernels, last(): pl.pallas_call(last_kernel, out_shape=jax.ShapeDtypeStruct(shape, F32), i...  1.96 us
    pallas_call x2, Pallas kernels, combine(): pl.pallas_call(functools.partial(combine_kernel, top_bit), out_shape=[jax...  1.41 us
    pallas_call x1, Pallas kernels, middle(): pl.pallas_call(middle_kernel, out_shape=jax.ShapeDtypeStruct((2, parts[0]...  1.13 us
  transfers between devices with their start and end apart: 12, of which 6 were waited for; matrix products, arithmetic and copies ran while one was open for 0% of the time, Pallas kernels for 17%

profile of v3, /device:TPU:0, one launch (start us, length us, event | category | flops | bytes accessed | tf_op | source)
XLA Modules:
  0.0 41.1 jit_solution(17526628441272082130)
XLA Ops:
  0.0 0.0 copy-start.3
  0.0 0.0 copy-start.1
  0.0 0.0 copy-start.4
  0.0 0.0 copy-start.2
  0.0 0.0 copy-start
  0.0 4.5 %first.1 = (f32[2,128,256]{2,1,0:T(8,128)S(1)}, f32[2,192,256]{2,1,0:T(8,128)S(1)}, f32[2,64,256]{2,1,0:T(8,128)S(1)}, f32[2,64,256]{2,1,0:T(8,128)S(1)}, f32[2,64,256]{2,1,0:T(8,128)S(1)}) custom-call(f32[2,1,512,256]{3,2,1,0:T(8,128)} %amplitudes_hbm.1, f32[2,2,512,512]{3,2,1,0:T(8,128)} %gates_hbm.2, f32[2,17]{1,0:T(2,128)} %phases_ref.1, ...), custom_call_target="tpu_custom_call" | custom-call | flops 1000 | bytes 1000 | tf_op jit(solution)/shard_map/first/pallas_call | solution.py:254
  4.5 3.0 %collective-permute-start = (f32[2,128,256]{2,1,0:T(8,128)S(1)}, f32[2,128,256]{2,1,0:T(8,128)S(1)}, u32[]{:S(2)}, u32[]{:S(2)}) collective-permute-start(f32[2,128,256]{2,1,0:T(8,128)S(1)} %get-tuple-element.32.own_ref), channel_id=1, source_target_pairs={{0,2},{1,3},{2,0},{3,1},{4,6},{5,7},{6,4},{7,5},{8,10},{9,11},{10,... | collective-permute-start | bytes 786440 | tf_op jit(solution)/shard_map/ppermute | solution.py:554
  7.5 0.1 collective-permute-start.2
  7.6 4.0 %collective-permute-start.4 = (f32[2,64,256]{2,1,0:T(8,128)S(1)}, f32[2,64,256]{2,1,0:T(8,128)S(1)}, u32[]{:S(2)}, u32[]{:S(2)}) collective-permute-start(f32[2,64,256]{2,1,0:T(8,128)S(1)} %get-tuple-element.47), channel_id=1, source_target_pairs={{0,20},{4,16},{8,28},{12,24},{16,4},{20,0},{24,12},{28,8},{1,21},{... | collective-permute-start | bytes 393224 | tf_op jit(solution)/shard_map/ppermute | solution.py:554
  11.6 0.3 collective-permute-start.3
  11.9 0.2 collective-permute-start.1
  12.1 2.5 %collective-permute-done.other_ref = f32[2,128,256]{2,1,0:T(8,128)S(1)} collective-permute-done((f32[2,128,256]{2,1,0:T(8,128)S(1)}, f32[2,128,256]{2,1,0:T(8,128)S(1)}, u32[]{:S(2)}, u32[]{:S(2)}) %collective-permute-start) | collective-permute-done | bytes 262176 | tf_op jit(solution)/shard_map/ppermute | solution.py:554
  14.6 0.0 copy-done
  14.6 0.7 %combine.2 = (f32[2,64,256]{2,1,0:T(8,128)S(1)}, f32[2,64,256]{2,1,0:T(8,128)S(1)}) custom-call(f32[2,128,256]{2,1,0:T(8,128)S(1)} %get-tuple-element.32.own_ref, f32[2,128,256]{2,1,0:T(8,128)S(1)} %collective-permute-done.other_ref, f32[2,2,2,2]{3,2,1,0:T(2,128)S(1)} %copy-done), custom_call_target="tpu_custom_call" | custom-call | flops 1000 | bytes 1000 | tf_op jit(solution)/shard_map/combine/pallas_call | solution.py:402
  15.3 4.2 %collective-permute-start.7 = (f32[2,64,256]{2,1,0:T(8,128)S(1)}, f32[2,64,256]{2,1,0:T(8,128)S(1)}, u32[]{:S(2)}, u32[]{:S(2)}) collective-permute-start(f32[2,64,256]{2,1,0:T(8,128)S(1)} %get-tuple-element.33), channel_id=1, source_target_pairs={{0,24},{4,28},{8,16},{12,20},{16,8},{20,12},{24,0},{28,4},{1,25},{... | collective-permute-start | bytes 393224 | tf_op jit(solution)/shard_map/ppermute | solution.py:554
  19.6 0.0 copy-done.3
  19.6 0.0 copy-done.1
  19.6 0.0 copy-done.4
  19.6 0.0 copy-done.2
  19.6 3.6 %ready.1 = (bf16[512,512]{1,0:T(8,128)(2,1)S(1)}, bf16[512,512]{1,0:T(8,128)(2,1)S(1)}, f32[256,128]{1,0:T(8,128)S(1)}, f32[256,128]{1,0:T(8,128)S(1)}, bf16[512...) custom-call(f32[2,2,512,512]{3,2,1,0:T(8,128)} %gates_hbm.2, ...), custom_call_target="tpu_custom_call" | custom-call | flops 1500001024 | bytes 1000 | tf_op jit(solution)/shard_map/ready/pallas_call | solution.py:355
  23.1 0.0 collective-permute-done.2.other_ref
  23.2 0.7 %combine.3 = (f32[2,64,256]{2,1,0:T(8,128)S(1)}, f32[2,64,256]{2,1,0:T(8,128)S(1)}, f32[2,64,256]{2,1,0:T(8,128)S(1)}) custom-call(f32[2,192,256]{2,1,0:T(8,128)S(1)} %get-tuple-element.41.own_ref, f32[2,192,256]{2,1,0:T(8,128)S(1)} %collective-permute-done.2.other_ref, f32[2,2,2,2]{3,2,1,0:T(2,128)S(1)} %copy-done), custom_call_target="tpu_custom_call" | custom-call | flops 1000 | bytes 1000 | tf_op jit(solution)/shard_map/combine/pallas_call | solution.py:402
  23.9 1.9 %collective-permute-start.8 = (f32[2,64,256]{2,1,0:T(8,128)S(1)}, f32[2,64,256]{2,1,0:T(8,128)S(1)}, u32[]{:S(2)}, u32[]{:S(2)}) collective-permute-start(f32[2,64,256]{2,1,0:T(8,128)S(1)} %get-tuple-element.53), channel_id=1, source_target_pairs={{0,12},{4,8},{8,4},{12,0},{16,28},{20,24},{24,20},{28,16},{1,13},{... | collective-permute-start | bytes 393224 | tf_op jit(solution)/shard_map/ppermute | solution.py:554
  25.8 0.0 collective-permute-done.4.refs_2_
  25.8 1.1 %collective-permute-start.6 = (f32[2,64,256]{2,1,0:T(8,128)S(1)}, f32[2,64,256]{2,1,0:T(8,128)S(1)}, u32[]{:S(2)}, u32[]{:S(2)}) collective-permute-start(f32[2,64,256]{2,1,0:T(8,128)S(1)} %get-tuple-element.51), channel_id=1, source_target_pairs={{0,8},{4,12},{8,0},{12,4},{16,24},{20,28},{24,16},{28,20},{1,9},{5... | collective-permute-start | bytes 393224 | tf_op jit(solution)/shard_map/ppermute | solution.py:554
  26.9 0.1 collective-permute-done.3.refs_1_
  27.0 0.0 collective-permute-done.1.refs_0_
  27.0 1.6 %collective-permute-start.5 = (f32[2,192,256]{2,1,0:T(8,128)S(1)}, f32[2,192,256]{2,1,0:T(8,128)S(1)}, u32[]{:S(2)}, u32[]{:S(2)}) collective-permute-start(f32[2,192,256]{2,1,0:T(8,128)S(1)} %joined.2.own_ref), channel_id=1, source_target_pairs={{0,2},{1,3},{2,0},{3,1},{4,6},{5,7},{6,4},{7,5},{8,10},{9,11},{10,... | collective-permute-start | bytes 1179656 | tf_op jit(solution)/shard_map/ppermute | solution.py:554
  28.6 2.8 %collective-permute-start.9 = (f32[2,64,256]{2,1,0:T(8,128)S(1)}, f32[2,64,256]{2,1,0:T(8,128)S(1)}, u32[]{:S(2)}, u32[]{:S(2)}) collective-permute-start(f32[2,64,256]{2,1,0:T(8,128)S(1)} %get-tuple-element.56), channel_id=1, source_target_pairs={{0,28},{4,24},{8,20},{12,16},{16,12},{20,8},{24,4},{28,0},{1,29},{... | collective-permute-start | bytes 393224 | tf_op jit(solution)/shard_map/ppermute | solution.py:554
  31.4 0.0 collective-permute-done.7.refs_0_
  31.4 0.0 collective-permute-done.8.refs_2_
  31.4 1.0 %collective-permute-done.6.refs_1_ = f32[2,64,256]{2,1,0:T(8,128)S(1)} collective-permute-done((f32[2,64,256]{2,1,0:T(8,128)S(1)}, f32[2,64,256]{2,1,0:T(8,128)S(1)}, u32[]{:S(2)}, u32[]{:S(2)}) %collective-permute-start.6) | collective-permute-done | bytes 131104 | tf_op jit(solution)/shard_map/ppermute | solution.py:554
  32.5 0.1 turned_pieces.1.own_ref
  32.5 0.1 collective-permute-start.11
  32.6 3.3 %collective-permute-done.5.other_ref = f32[2,192,256]{2,1,0:T(8,128)S(1)} collective-permute-done((f32[2,192,256]{2,1,0:T(8,128)S(1)}, f32[2,192,256]{2,1,0:T(8,128)S(1)}, u32[]{:S(2)}, u32[]{:S(2)}) %collective-permute-start.5) | collective-permute-done | bytes 393248 | tf_op jit(solution)/shard_map/ppermute | solution.py:554
  35.9 0.5 %collective-permute-done.9.last_ref = f32[2,64,256]{2,1,0:T(8,128)S(1)} collective-permute-done((f32[2,64,256]{2,1,0:T(8,128)S(1)}, f32[2,64,256]{2,1,0:T(8,128)S(1)}, u32[]{:S(2)}, u32[]{:S(2)}) %collective-permute-start.9) | collective-permute-done | bytes 131104 | tf_op jit(solution)/shard_map/ppermute | solution.py:554
  36.3 0.8 %turned.1.own_ref = f32[2,256,256]{2,1,0:T(8,128)S(1)} custom-call(f32[256,128]{1,0:T(8,128)S(1)} %get-tuple-element.38.phase_real_ref, f32[256,128]{1,0:T(8,128)S(1)} %get-tuple-element.39.phase_imag_ref, f32[2,2,2,2]{3,2,1,0:T(2,128)S(1)} %copy-done, f32[2,192,256]{2,1,0:T(8,128)S(1)} %joined.2.own_ref, ...), custom_call_target="tpu_custom_call" | custom-call | flops 1000 | bytes 1000 | tf_op jit(solution)/shard_map/turned/pallas_call | solution.py:504
  37.1 0.1 collective-permute-start.10
  37.2 0.0 collective-permute-done.11.other_ref
  37.2 1.1 %middle.1.sum_ref = f32[2,512,256]{2,1,0:T(8,128)S(1)} custom-call(bf16[512,512]{1,0:T(8,128)(2,1)S(1)} %get-tuple-element.57.high_ref, bf16[512,512]{1,0:T(8,128)(2,1)S(1)} %get-tuple-element.58.low_ref, f32[8,256]{1,0:T(8,128)S(1)} %get-tuple-element.37.coefficients_ref, f32[2,256,256]{2,1,0:T(8,128)S(1)} %turned_pieces.1.own_ref, ...), custom_call_target="tpu_custom_call" | custom-call | flops 1000 | bytes 1000 | tf_op jit(solution)/shard_map/middle/pallas_call | solution.py:475
  38.3 0.8 %collective-permute-done.10.other_ref = f32[2,256,256]{2,1,0:T(8,128)S(1)} collective-permute-done((f32[2,256,256]{2,1,0:T(8,128)S(1)}, f32[2,256,256]{2,1,0:T(8,128)S(1)}, u32[]{:S(2)}, u32[]{:S(2)}) %collective-permute-start.10) | collective-permute-done | bytes 524320 | tf_op jit(solution)/shard_map/ppermute | solution.py:554
  39.1 2.0 %last.1 = f32[2,1,512,256]{3,2,1,0:T(8,128)} custom-call(bf16[512,512]{1,0:T(8,128)(2,1)S(1)} %get-tuple-element.35.high_ref, bf16[512,512]{1,0:T(8,128)(2,1)S(1)} %get-tuple-element.36.low_ref, f32[8,256]{1,0:T(8,128)S(1)} %get-tuple-element.37.coefficients_ref, f32[2,256,256]{2,1,0:T(8,128)S(1)} %turned.1.own_ref, ...), custom_call_target="tpu_custom_call" | custom-call | flops 1000 | bytes 1000 | tf_op jit(solution)/shard_map/last/pallas_call | solution.py:541
  (2 shorter events, 0.0 us)
Async XLA Ops:
  0.0 19.6 %copy-start.3 = (f32[2,1]{0,1:T(1,128)S(1)}, f32[2,1]{0,1:T(1,128)}, u32[]{:S(2)}) copy-start(f32[2,1]{0,1:T(1,128)} %param.11) | copy-start | bytes 28
  0.0 19.6 %copy-start.1 = (f32[2,17]{1,0:T(2,128)S(1)}, f32[2,17]{1,0:T(2,128)}, u32[]{:S(2)}) copy-start(f32[2,17]{1,0:T(2,128)} %phases_ref.1) | copy-start | bytes 412
  0.0 19.6 %copy-start.4 = (s32[17]{0:T(128)S(1)}, s32[17]{0:T(128)}, u32[]{:S(2)}) copy-start(s32[17]{0:T(128)} %bits_ref.1) | copy-start | bytes 208
  0.0 19.6 %copy-start.2 = (s32[2,17]{1,0:T(2,128)S(1)}, s32[2,17]{1,0:T(2,128)}, u32[]{:S(2)}) copy-start(s32[2,17]{1,0:T(2,128)} %coupled_ref.1) | copy-start | bytes 412
  0.0 14.6 %copy-start = (f32[2,2,2,2]{3,2,1,0:T(2,128)S(1)}, f32[2,2,2,2]{3,2,1,0:T(2,128)}, u32[]{:S(2)}) copy-start(f32[2,2,2,2]{3,2,1,0:T(2,128)} %pair_ref.7) | copy-start | bytes 196
  4.5 10.1 %collective-permute-start = (f32[2,128,256]{2,1,0:T(8,128)S(1)}, f32[2,128,256]{2,1,0:T(8,128)S(1)}, u32[]{:S(2)}, u32[]{:S(2)}) collective-permute-start(f32[2,128,256]{2,1,0:T(8,128)S(1)} %get-tuple-element.32.own_ref), channel_id=1, source_target_pairs={{0,2},{1,3},{2,0},{3,1},{4,6},{5,7},{6,4},{7,5},{8,10},{9,11},{10,... | collective-permute-start | bytes 786440 | tf_op jit(solution)/shard_map/ppermute | solution.py:554
  7.5 15.7 %collective-permute-start.2 = (f32[2,192,256]{2,1,0:T(8,128)S(1)}, f32[2,192,256]{2,1,0:T(8,128)S(1)}, u32[]{:S(2)}, u32[]{:S(2)}) collective-permute-start(f32[2,192,256]{2,1,0:T(8,128)S(1)} %get-tuple-element.41.own_ref), channel_id=1, source_target_pairs={{0,2},{1,3},{2,0},{3,1},{4,6},{5,7},{6,4},{7,5},{8,10},{9,11},{10,... | collective-permute-start | bytes 1179656 | tf_op jit(solution)/shard_map/ppermute | solution.py:554
  7.6 18.2 %collective-permute-start.4 = (f32[2,64,256]{2,1,0:T(8,128)S(1)}, f32[2,64,256]{2,1,0:T(8,128)S(1)}, u32[]{:S(2)}, u32[]{:S(2)}) collective-permute-start(f32[2,64,256]{2,1,0:T(8,128)S(1)} %get-tuple-element.47), channel_id=1, source_target_pairs={{0,20},{4,16},{8,28},{12,24},{16,4},{20,0},{24,12},{28,8},{1,21},{... | collective-permute-start | bytes 393224 | tf_op jit(solution)/shard_map/ppermute | solution.py:554
  11.6 15.4 %collective-permute-start.3 = (f32[2,64,256]{2,1,0:T(8,128)S(1)}, f32[2,64,256]{2,1,0:T(8,128)S(1)}, u32[]{:S(2)}, u32[]{:S(2)}) collective-permute-start(f32[2,64,256]{2,1,0:T(8,128)S(1)} %get-tuple-element.45), channel_id=1, source_target_pairs={{0,16},{4,20},{8,24},{12,28},{16,0},{20,4},{24,8},{28,12},{1,17},{... | collective-permute-start | bytes 393224 | tf_op jit(solution)/shard_map/ppermute | solution.py:554
  11.9 15.1 %collective-permute-start.1 = (f32[2,64,256]{2,1,0:T(8,128)S(1)}, f32[2,64,256]{2,1,0:T(8,128)S(1)}, u32[]{:S(2)}, u32[]{:S(2)}) collective-permute-start(f32[2,64,256]{2,1,0:T(8,128)S(1)} %get-tuple-element.40), channel_id=1, source_target_pairs={{0,4},{4,0},{8,12},{12,8},{16,20},{20,16},{24,28},{28,24},{1,5},{5... | collective-permute-start | bytes 393224 | tf_op jit(solution)/shard_map/ppermute | solution.py:554
  15.3 16.1 %collective-permute-start.7 = (f32[2,64,256]{2,1,0:T(8,128)S(1)}, f32[2,64,256]{2,1,0:T(8,128)S(1)}, u32[]{:S(2)}, u32[]{:S(2)}) collective-permute-start(f32[2,64,256]{2,1,0:T(8,128)S(1)} %get-tuple-element.33), channel_id=1, source_target_pairs={{0,24},{4,28},{8,16},{12,20},{16,8},{20,12},{24,0},{28,4},{1,25},{... | collective-permute-start | bytes 393224 | tf_op jit(solution)/shard_map/ppermute | solution.py:554
  23.9 7.5 %collective-permute-start.8 = (f32[2,64,256]{2,1,0:T(8,128)S(1)}, f32[2,64,256]{2,1,0:T(8,128)S(1)}, u32[]{:S(2)}, u32[]{:S(2)}) collective-permute-start(f32[2,64,256]{2,1,0:T(8,128)S(1)} %get-tuple-element.53), channel_id=1, source_target_pairs={{0,12},{4,8},{8,4},{12,0},{16,28},{20,24},{24,20},{28,16},{1,13},{... | collective-permute-start | bytes 393224 | tf_op jit(solution)/shard_map/ppermute | solution.py:554
  25.8 6.7 %collective-permute-start.6 = (f32[2,64,256]{2,1,0:T(8,128)S(1)}, f32[2,64,256]{2,1,0:T(8,128)S(1)}, u32[]{:S(2)}, u32[]{:S(2)}) collective-permute-start(f32[2,64,256]{2,1,0:T(8,128)S(1)} %get-tuple-element.51), channel_id=1, source_target_pairs={{0,8},{4,12},{8,0},{12,4},{16,24},{20,28},{24,16},{28,20},{1,9},{5... | collective-permute-start | bytes 393224 | tf_op jit(solution)/shard_map/ppermute | solution.py:554
  27.0 8.8 %collective-permute-start.5 = (f32[2,192,256]{2,1,0:T(8,128)S(1)}, f32[2,192,256]{2,1,0:T(8,128)S(1)}, u32[]{:S(2)}, u32[]{:S(2)}) collective-permute-start(f32[2,192,256]{2,1,0:T(8,128)S(1)} %joined.2.own_ref), channel_id=1, source_target_pairs={{0,2},{1,3},{2,0},{3,1},{4,6},{5,7},{6,4},{7,5},{8,10},{9,11},{10,... | collective-permute-start | bytes 1179656 | tf_op jit(solution)/shard_map/ppermute | solution.py:554
  28.6 7.8 %collective-permute-start.9 = (f32[2,64,256]{2,1,0:T(8,128)S(1)}, f32[2,64,256]{2,1,0:T(8,128)S(1)}, u32[]{:S(2)}, u32[]{:S(2)}) collective-permute-start(f32[2,64,256]{2,1,0:T(8,128)S(1)} %get-tuple-element.56), channel_id=1, source_target_pairs={{0,28},{4,24},{8,20},{12,16},{16,12},{20,8},{24,4},{28,0},{1,29},{... | collective-permute-start | bytes 393224 | tf_op jit(solution)/shard_map/ppermute | solution.py:554
  32.5 4.7 %collective-permute-start.11 = (f32[2,256,256]{2,1,0:T(8,128)S(1)}, f32[2,256,256]{2,1,0:T(8,128)S(1)}, u32[]{:S(2)}, u32[]{:S(2)}) collective-permute-start(f32[2,256,256]{2,1,0:T(8,128)S(1)} %turned_pieces.1.own_ref), channel_id=1, source_target_pairs={{0,1},{1,0},{2,3},{3,2},{4,5},{5,4},{6,7},{7,6},{8,9},{9,8},{10,11... | collective-permute-start | bytes 1572872 | tf_op jit(solution)/shard_map/ppermute | solution.py:554
  37.1 2.0 %collective-permute-start.10 = (f32[2,256,256]{2,1,0:T(8,128)S(1)}, f32[2,256,256]{2,1,0:T(8,128)S(1)}, u32[]{:S(2)}, u32[]{:S(2)}) collective-permute-start(f32[2,256,256]{2,1,0:T(8,128)S(1)} %turned.1.own_ref), channel_id=1, source_target_pairs={{0,1},{1,0},{2,3},{3,2},{4,5},{5,4},{6,7},{7,6},{8,9},{9,8},{10,11... | collective-permute-start | bytes 1572872 | tf_op jit(solution)/shard_map/ppermute | solution.py:554

commit v4 on v3

--- a/solution.py
+++ b/solution.py
@@ -12,7 +12,9 @@
 VMEM_BYTES = 32 * 1024 * 1024
 MIDDLE_COST = 3000000000
 HALF_COST = 1000
-READY_COST = 1500001000
+CHUNKS = 2
+LAST_CHUNKS = 4
+COMBINE_COST = 1500001000
 LATE_COST = 1000
 
 
@@ -163,11 +165,102 @@
     )
 
 
-def gate_pieces(groups, piece_rows, layout_ref, left_high, left_low, right_high, right_low, out_refs):
-    rows = left_high.shape[0]
-    cols = right_high.shape[1] // 2
-    gated = product(left_high, left_low, right_high, right_low)
-    chosen = chosen_rows([d for group in groups for d in group], piece_rows, rows, layout_ref)
+def first_kernel(
+    groups,
+    piece_rows,
+    col_bits,
+    top_bit,
+    amplitudes_hbm,
+    gates_hbm,
+    phases_hbm,
+    angles_hbm,
+    bits_hbm,
+    coupled_hbm,
+    layout_hbm,
+    pair_hbm,
+    *refs,
+):
+    (
+        pairs_ref,
+        *out_refs,
+        amplitudes_ref,
+        gates_ref,
+        phases_ref,
+        angles_ref,
+        bits_ref,
+        coupled_ref,
+        layout_ref,
+        pair_ref,
+        small_sems,
+        chunk_sems,
+    ) = refs
+    rows, cols = amplitudes_ref.shape[2:]
+    row_bits = rows.bit_length() - 1
+    small = [
+        pltpu.make_async_copy(source, target, small_sems.at[i])
+        for i, (source, target) in enumerate(
+            (
+                (phases_hbm, phases_ref),
+                (angles_hbm, angles_ref),
+                (bits_hbm, bits_ref),
+                (coupled_hbm, coupled_ref),
+                (layout_hbm, layout_ref),
+                (pair_hbm, pair_ref),
+            )
+        )
+    ]
+    count = chunk_sems.shape[0]
+    step = rows // count
+    chunks = []
+    for k in range(count):
+        part = pl.ds(k * step, step)
+        chunks.append(
+            [
+                pltpu.make_async_copy(
+                    gates_hbm.at[0, 0, :, part], gates_ref.at[0, :, part], chunk_sems.at[k, 0]
+                ),
+                pltpu.make_async_copy(
+                    gates_hbm.at[0, 1, :, part], gates_ref.at[1, :, part], chunk_sems.at[k, 1]
+                ),
+                pltpu.make_async_copy(
+                    amplitudes_hbm.at[:, :, part], amplitudes_ref.at[:, :, part], chunk_sems.at[k, 2]
+                ),
+            ]
+        )
+    for copy in small:
+        copy.start()
+    for chunk in chunks:
+        for copy in chunk:
+            copy.start()
+    for copy in small:
+        copy.wait()
+    bit = (lax.axis_index("lo") >> top_bit) & 1
+    c = pair_coefficients(pair_ref, 0, bit)
+    for i in range(4):
+        pairs_ref[i : i + 1, :] = jnp.full((1, cols), c[i], F32)
+    pairs_ref[4:8, :] = jnp.zeros((4, cols), F32)
+    cosine, sine = qubit_factors(0, phases_ref, bits_ref, coupled_ref)
+    base_real, base_imag = sincos(angles_ref[0:1, 0:1])
+    phase_real, phase_imag = row_phases(cosine, sine, col_bits, row_bits, base_real, base_imag)
+    steps = [d for group in groups for d in group]
+    chosen = chosen_rows(steps, piece_rows, rows, layout_ref)
+    gated = None
+    for k in range(count):
+        for copy in chunks[k]:
+            copy.wait()
+        part = slice(k * step, (k + 1) * step)
+        real_high, real_low = split(gates_ref[0, :, part])
+        imag_high, imag_low = split(gates_ref[1, :, part])
+        right_high, right_low = turned_rows(
+            amplitudes_ref[0, 0, part], amplitudes_ref[1, 0, part], phase_real[part], phase_imag[part]
+        )
+        term = product(
+            jnp.concatenate([real_high, imag_high], axis=1),
+            jnp.concatenate([real_low, imag_low], axis=1),
+            right_high,
+            right_low,
+        )
+        gated = term if gated is None else gated + term
     gated_high, gated_low = split(gated)
     out = dot(chosen, gated_high) + dot(chosen, gated_low)
     start = 0
@@ -178,81 +271,15 @@
         start += size
 
 
-def first_kernel(
-    groups,
-    piece_rows,
-    col_bits,
-    amplitudes_hbm,
-    gates_hbm,
-    phases_hbm,
-    angles_hbm,
-    bits_hbm,
-    coupled_hbm,
-    layout_hbm,
-    *refs,
+def first(
+    groups, piece_rows, col_bits, top_bit, amplitudes, gates, phases, angles, bits, coupled, layout, pair
 ):
-    (
-        *out_refs,
-        amplitudes_ref,
-        gates_ref,
-        phases_ref,
-        angles_ref,
-        bits_ref,
-        coupled_ref,
-        layout_ref,
-        sems,
-    ) = refs
-    copies = [
-        pltpu.make_async_copy(source, target, sems.at[i])
-        for i, (source, target) in enumerate(
-            (
-                (phases_hbm, phases_ref),
-                (angles_hbm, angles_ref),
-                (bits_hbm, bits_ref),
-                (coupled_hbm, coupled_ref),
-                (layout_hbm, layout_ref),
-                (gates_hbm.at[0, 0], gates_ref.at[0]),
-                (gates_hbm.at[0, 1], gates_ref.at[1]),
-                (amplitudes_hbm, amplitudes_ref),
-            )
-        )
-    ]
-    for copy in copies:
-        copy.start()
-    for copy in copies[:5]:
-        copy.wait()
-    rows = amplitudes_ref.shape[2]
-    row_bits = rows.bit_length() - 1
-    cosine, sine = qubit_factors(0, phases_ref, bits_ref, coupled_ref)
-    base_real, base_imag = sincos(angles_ref[0:1, 0:1])
-    phase_real, phase_imag = row_phases(cosine, sine, col_bits, row_bits, base_real, base_imag)
-    high, low = [], []
-    for i in range(2):
-        copies[5 + i].wait()
-        for parts, part in zip((high, low), split(gates_ref[i]), strict=True):
-            parts.append(part)
-    copies[7].wait()
-    right_high, right_low = turned_rows(
-        amplitudes_ref[0, 0], amplitudes_ref[1, 0], phase_real, phase_imag
-    )
-    gate_pieces(
-        groups,
-        piece_rows,
-        layout_ref,
-        jnp.concatenate(high, axis=1),
-        jnp.concatenate(low, axis=1),
-        right_high,
-        right_low,
-        out_refs,
-    )
-
-
-def first(groups, piece_rows, col_bits, amplitudes, gates, phases, angles, bits, coupled, layout):
     rows, cols = amplitudes.shape[2:]
-    shapes = [jax.ShapeDtypeStruct((2, len(group) * piece_rows, cols), F32) for group in groups]
-    sources = (amplitudes, gates, phases, angles, bits, coupled, layout)
-    return pl.pallas_call(
-        functools.partial(first_kernel, groups, piece_rows, col_bits),
+    shapes = [jax.ShapeDtypeStruct((8, cols), F32)]
+    shapes += [jax.ShapeDtypeStruct((2, len(group) * piece_rows, cols), F32) for group in groups]
+    sources = (amplitudes, gates, phases, angles, bits, coupled, layout, pair)
+    return pl.pallas_call(
+        functools.partial(first_kernel, groups, piece_rows, col_bits, top_bit),
         out_shape=shapes,
         in_specs=[any_space()] * len(sources),
         out_specs=[vmem()] * len(shapes),
@@ -264,7 +291,9 @@
             pltpu.SMEM(bits.shape, jnp.int32),
             pltpu.SMEM(coupled.shape, jnp.int32),
             pltpu.SMEM(layout.shape, jnp.int32),
-            pltpu.SemaphoreType.DMA((8,)),
+            pltpu.SMEM(pair.shape, F32),
+            pltpu.SemaphoreType.DMA((6,)),
+            pltpu.SemaphoreType.DMA((CHUNKS, 3)),
         ],
         compiler_params=params(),
         cost_estimate=cost(),
@@ -288,14 +317,12 @@
     return tile
 
 
-def ready_kernel(
-    sets, piece_rows, col_bits, gates_hbm, phases_ref, angles_ref, bits_ref, coupled_ref, pair_ref, *refs
+def phases_kernel(
+    sets, piece_rows, col_bits, phases_ref, angles_ref, bits_ref, coupled_ref, pair_ref, *refs
 ):
-    *out_refs, coefficients_ref, gates_ref, phase_real_ref, phase_imag_ref, sem = refs
-    copy = pltpu.make_async_copy(gates_hbm.at[1], gates_ref, sem)
-    copy.start()
+    *out_refs, coefficients_ref, phase_real_ref, phase_imag_ref = refs
     me = lax.axis_index("hi")
-    rows = gates_ref.shape[1]
+    rows = phase_real_ref.shape[0]
     cols = coefficients_ref.shape[1]
     row_bits = rows.bit_length() - 1
     bit = lax.axis_index("lo") & 1
@@ -313,9 +340,40 @@
     for i in range(4):
         coefficients_ref[i : i + 1, :] = c[i]
     coefficients_ref[4:8, :] = jnp.zeros((4, cols), F32)
+    for k, steps in enumerate(sets):
+        for j, d in enumerate(steps):
+            start = pl.multiple_of((me ^ d) * piece_rows, piece_rows)
+            target = slice(j * piece_rows, (j + 1) * piece_rows)
+            out_refs[2 * k][target, :] = phase_real_ref[pl.ds(start, piece_rows), :]
+            out_refs[2 * k + 1][target, :] = phase_imag_ref[pl.ds(start, piece_rows), :]
+
+
+def second_phases(sets, piece_rows, rows, col_bits, phases, angles, bits, coupled, pair):
+    cols = 1 << col_bits
+    shapes = []
+    for steps in sets:
+        shapes += [jax.ShapeDtypeStruct((len(steps) * piece_rows, 128), F32)] * 2
+    shapes.append(jax.ShapeDtypeStruct((8, cols), F32))
+    return pl.pallas_call(
+        functools.partial(phases_kernel, sets, piece_rows, col_bits),
+        out_shape=shapes,
+        in_specs=[vmem(), vmem(), smem(), smem(), smem()],
+        out_specs=[vmem()] * len(shapes),
+        scratch_shapes=[pltpu.VMEM((rows, 128), F32)] * 2,
+        compiler_params=params(),
+        cost_estimate=cost(),
+        name="second_phases",
+    )(phases, angles, bits, coupled, pair)
+
+
+def gates_kernel(sets, piece_rows, gates_hbm, *refs):
+    *out_refs, gates_ref, sem = refs
+    copy = pltpu.make_async_copy(gates_hbm.at[1], gates_ref, sem)
+    copy.start()
+    me = lax.axis_index("hi")
+    size = gates_ref.shape[1] // 4
+    quarter = size // piece_rows
     copy.wait()
-    size = rows // 4
-    quarter = size // piece_rows
     high, low = [], []
     for i in range(2):
         high_tiles, low_tiles = [], []
@@ -327,7 +385,7 @@
         high.append(jnp.concatenate(high_tiles, axis=1))
         low.append(jnp.concatenate(low_tiles, axis=1))
     for k, steps in enumerate(sets):
-        for part, out_ref in zip((high, low), out_refs[4 * k : 4 * k + 2], strict=True):
+        for part, out_ref in zip((high, low), out_refs[2 * k : 2 * k + 2], strict=True):
             out_ref[...] = jnp.concatenate(
                 [
                     part[i][:, d * piece_rows : (d + 1) * piece_rows]
@@ -336,37 +394,23 @@
                 ],
                 axis=1,
             )
-        for j, d in enumerate(steps):
-            start = pl.multiple_of((me ^ d) * piece_rows, piece_rows)
-            target = slice(j * piece_rows, (j + 1) * piece_rows)
-            out_refs[4 * k + 2][target, :] = phase_real_ref[pl.ds(start, piece_rows), :]
-            out_refs[4 * k + 3][target, :] = phase_imag_ref[pl.ds(start, piece_rows), :]
-
-
-def ready(sets, piece_rows, col_bits, gates, phases, angles, bits, coupled, pair):
+
+
+def second_gates(sets, piece_rows, gates):
     rows = gates.shape[2]
-    cols = 1 << col_bits
     shapes = []
     for steps in sets:
-        depth = len(steps) * piece_rows
-        shapes += [jax.ShapeDtypeStruct((rows, 2 * depth), BF16)] * 2
-        shapes += [jax.ShapeDtypeStruct((depth, 128), F32)] * 2
-    shapes.append(jax.ShapeDtypeStruct((8, cols), F32))
-    return pl.pallas_call(
-        functools.partial(ready_kernel, sets, piece_rows, col_bits),
+        shapes += [jax.ShapeDtypeStruct((rows, 2 * len(steps) * piece_rows), BF16)] * 2
+    return pl.pallas_call(
+        functools.partial(gates_kernel, sets, piece_rows),
         out_shape=shapes,
-        in_specs=[any_space(), vmem(), vmem(), smem(), smem(), smem()],
+        in_specs=[any_space()],
         out_specs=[vmem()] * len(shapes),
-        scratch_shapes=[
-            pltpu.VMEM(gates.shape[1:], F32),
-            pltpu.VMEM((rows, 128), F32),
-            pltpu.VMEM((rows, 128), F32),
-            pltpu.SemaphoreType.DMA,
-        ],
-        compiler_params=params(),
-        cost_estimate=cost(READY_COST),
-        name="ready",
-    )(hbm(gates), phases, angles, bits, coupled, pair)
+        scratch_shapes=[pltpu.VMEM(gates.shape[1:], F32), pltpu.SemaphoreType.DMA],
+        compiler_params=params(),
+        cost_estimate=cost(),
+        name="second_gates",
+    )(hbm(gates))
 
 
 def pair_coefficients(pair_ref, layer, bit):
@@ -386,9 +430,12 @@
     return own_real + other_real, own_imag + other_imag
 
 
-def combine_kernel(top_bit, own_ref, other_ref, pair_ref, *out_refs):
-    bit = (lax.axis_index("lo") >> top_bit) & 1
-    c = pair_coefficients(pair_ref, 0, bit)
+def vector_coefficients(ref):
+    return [ref[i : i + 1, :] for i in range(4)]
+
+
+def combine_kernel(pairs_ref, own_ref, other_ref, *out_refs):
+    c = vector_coefficients(pairs_ref)
     size = out_refs[0].shape[1]
     for i, out_ref in enumerate(out_refs):
         rows = slice(i * size, (i + 1) * size)
@@ -397,17 +444,17 @@
         )
 
 
-def combine(top_bit, count, own, other, pair_gates):
+def combine(count, own, other, pairs, flops):
     shape = (2, own.shape[1] // count, own.shape[2])
     return pl.pallas_call(
-        functools.partial(combine_kernel, top_bit),
+        combine_kernel,
         out_shape=[jax.ShapeDtypeStruct(shape, F32)] * count,
-        in_specs=[vmem(), vmem(), smem()],
+        in_specs=[vmem()] * 3,
         out_specs=[vmem()] * count,
         compiler_params=params(),
-        cost_estimate=cost(),
+        cost_estimate=cost(flops),
         name="combine",
-    )(own, other, pair_gates)
+    )(pairs, own, other)
 
 
 def late_kernel(*refs):
@@ -456,7 +503,7 @@
 
 
 def mixed_parts(coefficients_ref, own_ref, other_ref):
-    c = [coefficients_ref[i : i + 1, :] for i in range(4)]
+    c = vector_coefficients(coefficients_ref)
     real, imag = combined(own_ref, other_ref, c)
     real_high, real_low = split(real)
     imag_high, imag_low = split(imag)
@@ -484,12 +531,11 @@
 
 
 def turned_kernel(
-    top_bit, phase_real_ref, phase_imag_ref, pair_ref, own_ref, other_ref, last_ref, out_ref
+    phase_real_ref, phase_imag_ref, pairs_ref, own_ref, other_ref, last_ref, out_ref
 ):
-    bit = (lax.axis_index("lo") >> top_bit) & 1
     size = own_ref.shape[1]
     parts = (
-        (slice(0, size), combined(own_ref, other_ref, pair_coefficients(pair_ref, 0, bit))),
+        (slice(0, size), combined(own_ref, other_ref, vector_coefficients(pairs_ref))),
         (slice(size, out_ref.shape[1]), (last_ref[0], last_ref[1])),
     )
     reps = out_ref.shape[2] // phase_real_ref.shape[1]
@@ -499,17 +545,17 @@
         out_ref[0, part], out_ref[1, part] = turn(real, imag, cosine, sine)
 
 
-def turned(top_bit, phase_parts, pair, own, other, last):
+def turned(phase_parts, pairs, own, other, last):
     shape = (2, own.shape[1] + last.shape[1], own.shape[2])
     return pl.pallas_call(
-        functools.partial(turned_kernel, top_bit),
+        turned_kernel,
         out_shape=jax.ShapeDtypeStruct(shape, F32),
-        in_specs=[vmem(), vmem(), smem(), vmem(), vmem(), vmem()],
+        in_specs=[vmem()] * 6,
         out_specs=vmem(),
         compiler_params=params(),
         cost_estimate=cost(),
         name="turned",
-    )(*phase_parts, pair, own, other, last)
+    )(*phase_parts, pairs, own, other, last)
 
 
 def last_kernel(
@@ -543,7 +589,7 @@
         out_shape=jax.ShapeDtypeStruct(shape, F32),
         in_specs=[vmem()] * 6,
         out_specs=any_space(),
-        scratch_shapes=[pltpu.VMEM(shape, F32), pltpu.SemaphoreType.DMA((2,))],
+        scratch_shapes=[pltpu.VMEM(shape, F32), pltpu.SemaphoreType.DMA((LAST_CHUNKS,))],
         compiler_params=params(),
         cost_estimate=cost(),
         name="last",
@@ -571,13 +617,14 @@
     near = tuple(range(quarter, 2 * quarter))
     far = tuple(range(2 * quarter, 3 * quarter))
     early = tuple(range(3 * quarter, count))
-    late = beside + far
+    late = far + beside
     cross = functools.partial(swap, axis="lo", mask=1 << top_bit)
 
-    made = first(
+    pairs, early_part, near_part, *late_parts = first(
         (early, (0,) + near) + tuple((d,) for d in late),
         piece_rows,
         col_bits,
+        top_bit,
         amplitudes,
         gates,
         phases,
@@ -585,34 +632,34 @@
         bits,
         coupled,
         layout,
-    )
-    early_part, near_part, *late_parts = made
+        pair,
+    )
     early_other = cross(early_part)
     late_parts = [swap(part, "hi", d) for part, d in zip(late_parts, late, strict=True)]
     near_other = cross(near_part)
-    early_parts = combine(top_bit, len(early), early_part, early_other, pair)
     sets = ((0,) + near + early[:-1], late + early[-1:])
-    *parts, coefficients = ready(
-        sets, piece_rows, col_bits, after(gates, early_parts[0]), phases, angles, bits, coupled, pair
-    )
+    *turns, coefficients = second_phases(
+        sets, piece_rows, rows, col_bits, after(phases, early_part), angles, bits, coupled, pair
+    )
+    early_other = after(early_other, coefficients)
+    early_parts = combine(len(early), early_part, early_other, pairs, COMBINE_COST)
     early_parts = [swap(part, "hi", d) for part, d in zip(early_parts, early, strict=True)]
-    own_part, *near_parts = combine(
-        top_bit, 1 + len(near), near_part, after(near_other, coefficients), pair
-    )
+    own_part, *near_parts = combine(1 + len(near), near_part, near_other, pairs, 1000)
     late_part = joined([after(part, own_part) for part in late_parts], LATE_COST)
     late_other = cross(late_part)
     near_parts = [swap(part, "hi", d) for part, d in zip(near_parts, near, strict=True)]
     half_part = joined(early_parts[:-1], HALF_COST)
     near_turned = turned_pieces(
-        parts[2:4], [own_part] + [after(part, half_part) for part in near_parts] + [half_part]
+        turns[:2], [own_part] + [after(part, half_part) for part in near_parts] + [half_part]
     )
     near_turned_other = swap(near_turned, "lo", 1)
+    parts = second_gates(sets, piece_rows, after(gates, near_turned))
     late_turned = turned(
-        top_bit, parts[6:], pair, late_part, after(late_other, near_turned), early_parts[-1]
+        turns[2:], pairs, late_part, after(late_other, parts[0]), early_parts[-1]
     )
     late_turned_other = swap(late_turned, "lo", 1)
     total = middle(parts[:2], coefficients, near_turned, near_turned_other)
-    return last(parts[4:6], coefficients, late_turned, late_turned_other, total)
+    return last(parts[2:], coefficients, late_turned, late_turned_other, total)
 
 
 def solution(mesh):

time: 41.2 us -> 40.2 us (0.976)
  Pallas kernels: 13.4 us -> 11.1 us
  waiting for transfers between devices: 8.08 us -> 9.56 us
    pallas_call x4 -> x5, Pallas kernels: 5.74 us -> 3.84 us  [the longest x1 2.62 us: second_gates(): pl.pallas_call(functools.partial(gates_kernel, sets, piece_rows), out_sha...]
    ppermute x12, waiting for transfers between devices: 8.08 us -> 9.56 us  [swap(): lax.ppermute(value, axis, [(i, i ^ mask) for i in range(lax.axis_size(axi...]
  transfers between devices with their start and end apart: 12 -> 12, of which waited for: 6 -> 7; matrix products, arithmetic and copies ran while one was open for 0% -> 0% of each run, Pallas kernels for 17% -> 13%
where the time goes in v4:
time: 40.2 us; the launch traced here: 40 us
  starting transfers between devices  19.2 us (48%)
  Pallas kernels  11.1 us (28%)
  waiting for transfers between devices  9.56 us (24%)
    ppermute x12, starting transfers between devices, swap(): lax.ppermute(value, axis, [(i, i ^ mask) for i in range(lax.axis_size(axi...  19.2 us
    ppermute x12, waiting for transfers between devices, swap(): lax.ppermute(value, axis, [(i, i ^ mask) for i in range(lax.axis_size(axi...  9.56 us
    pallas_call x1, Pallas kernels, first(): pl.pallas_call(functools.partial(first_kernel, groups, piece_rows, col_bi...  4.17 us
    pallas_call x1, Pallas kernels, second_gates(): pl.pallas_call(functools.partial(gates_kernel, sets, piece_rows), out_sha...  2.62 us
    pallas_call x1, Pallas kernels, last(): pl.pallas_call(last_kernel, out_shape=jax.ShapeDtypeStruct(shape, F32), i...  1.91 us
    pallas_call x1, Pallas kernels, middle(): pl.pallas_call(middle_kernel, out_shape=jax.ShapeDtypeStruct((2, parts[0]...  1.13 us
    pallas_call x1, Pallas kernels, second_phases(): pl.pallas_call(functools.partial(phases_kernel, sets, piece_rows, col_bit...  0.89 us
  transfers between devices with their start and end apart: 12, of which 7 were waited for; matrix products, arithmetic and copies ran while one was open for 0% of the time, Pallas kernels for 13%

profile of v4, /device:TPU:0, one launch (start us, length us, event | category | flops | bytes accessed | tf_op | source)
XLA Modules:
  0.0 40.0 jit_solution(15556861742787793382)
XLA Ops:
  0.0 0.0 copy-start.3
  0.0 0.0 copy-start
  0.0 0.0 copy-start.1
  0.0 0.0 copy-start.4
  0.0 0.0 copy-start.2
  0.0 4.2 %first.1 = (f32[8,256]{1,0:T(8,128)S(1)}, f32[2,128,256]{2,1,0:T(8,128)S(1)}, f32[2,192,256]{2,1,0:T(8,128)S(1)}, f32[2,64,256]{2,1,0:T(8,128)S(1)}, f32[2,64,25...) custom-call(f32[2,1,512,256]{3,2,1,0:T(8,128)} %amplitudes_hbm.1, f32[2,2,512,512]{3,2,1,0:T(8,128)} %gates_hbm.2, ...), custom_call_target="tpu_custom_call" | custom-call | flops 1000 | bytes 1000 | tf_op jit(solution)/shard_map/first/pallas_call | solution.py:281
  4.2 3.0 %collective-permute-start.2 = (f32[2,128,256]{2,1,0:T(8,128)S(1)}, f32[2,128,256]{2,1,0:T(8,128)S(1)}, u32[]{:S(2)}, u32[]{:S(2)}) collective-permute-start(f32[2,128,256]{2,1,0:T(8,128)S(1)} %get-tuple-element.34.own_ref), channel_id=1, source_target_pairs={{0,2},{1,3},{2,0},{3,1},{4,6},{5,7},{6,4},{7,5},{8,10},{9,11},{10,... | collective-permute-start | bytes 786440 | tf_op jit(solution)/shard_map/ppermute | solution.py:600
  7.2 0.1 collective-permute-start
  7.3 3.0 %collective-permute-start.5 = (f32[2,64,256]{2,1,0:T(8,128)S(1)}, f32[2,64,256]{2,1,0:T(8,128)S(1)}, u32[]{:S(2)}, u32[]{:S(2)}) collective-permute-start(f32[2,64,256]{2,1,0:T(8,128)S(1)} %get-tuple-element.53), channel_id=1, source_target_pairs={{0,16},{4,20},{8,24},{12,28},{16,0},{20,4},{24,8},{28,12},{1,17},{... | collective-permute-start | bytes 393224 | tf_op jit(solution)/shard_map/ppermute | solution.py:600
  10.3 1.3 %collective-permute-start.6 = (f32[2,64,256]{2,1,0:T(8,128)S(1)}, f32[2,64,256]{2,1,0:T(8,128)S(1)}, u32[]{:S(2)}, u32[]{:S(2)}) collective-permute-start(f32[2,64,256]{2,1,0:T(8,128)S(1)} %get-tuple-element.55), channel_id=1, source_target_pairs={{0,20},{4,16},{8,28},{12,24},{16,4},{20,0},{24,12},{28,8},{1,21},{... | collective-permute-start | bytes 393224 | tf_op jit(solution)/shard_map/ppermute | solution.py:600
  11.6 0.2 collective-permute-start.7
  11.8 0.0 copy-done.3
  11.8 0.0 copy-done
  11.8 0.0 copy-done.1
  11.8 0.0 copy-done.4
  11.9 0.0 copy-done.2
  11.9 0.9 %second_phases.1 = (f32[256,128]{1,0:T(8,128)S(1)}, f32[256,128]{1,0:T(8,128)S(1)}, f32[256,128]{1,0:T(8,128)S(1)}, f32[256,128]{1,0:T(8,128)S(1)}, f32[8,256]{1,0:T(8,128)S(1)}) custom-call(f32[2,17]{1,0:T(2,128)S(1)} %copy-done.1, f32[1,2]{1,0:T(1,128)S(1)} %bitcast.2, s32[17]{0:T(128)S(1)} %copy-done.4, s32[2,17]{1,0:T(2,128)S(1)} %copy-done.2, ...), custom_call_target="tpu_custom_call" | custom-call | flops 1000 | bytes 1000 | tf_op jit(solution)/shard_map/second_phases/pallas_call | solution.py:357
  12.8 1.6 %collective-permute-done.2.other_ref = f32[2,128,256]{2,1,0:T(8,128)S(1)} collective-permute-done((f32[2,128,256]{2,1,0:T(8,128)S(1)}, f32[2,128,256]{2,1,0:T(8,128)S(1)}, u32[]{:S(2)}, u32[]{:S(2)}) %collective-permute-start.2) | collective-permute-done | bytes 262176 | tf_op jit(solution)/shard_map/ppermute | solution.py:600
  14.3 0.1 combine.3
  14.4 4.2 %collective-permute-start.3 = (f32[2,64,256]{2,1,0:T(8,128)S(1)}, f32[2,64,256]{2,1,0:T(8,128)S(1)}, u32[]{:S(2)}, u32[]{:S(2)}) collective-permute-start(f32[2,64,256]{2,1,0:T(8,128)S(1)} %get-tuple-element.44), channel_id=1, source_target_pairs={{0,24},{4,28},{8,16},{12,20},{16,8},{20,12},{24,0},{28,4},{1,25},{... | collective-permute-start | bytes 393224 | tf_op jit(solution)/shard_map/ppermute | solution.py:600
  18.6 3.3 %collective-permute-done.other_ref = f32[2,192,256]{2,1,0:T(8,128)S(1)} collective-permute-done((f32[2,192,256]{2,1,0:T(8,128)S(1)}, f32[2,192,256]{2,1,0:T(8,128)S(1)}, u32[]{:S(2)}, u32[]{:S(2)}) %collective-permute-start) | collective-permute-done | bytes 393248 | tf_op jit(solution)/shard_map/ppermute | solution.py:600
  21.9 0.1 combine.2
  22.0 2.8 %collective-permute-start.4 = (f32[2,64,256]{2,1,0:T(8,128)S(1)}, f32[2,64,256]{2,1,0:T(8,128)S(1)}, u32[]{:S(2)}, u32[]{:S(2)}) collective-permute-start(f32[2,64,256]{2,1,0:T(8,128)S(1)} %get-tuple-element.46), channel_id=1, source_target_pairs={{0,12},{4,8},{8,4},{12,0},{16,28},{20,24},{24,20},{28,16},{1,13},{... | collective-permute-start | bytes 393224 | tf_op jit(solution)/shard_map/ppermute | solution.py:600
  24.9 0.0 collective-permute-done.5.refs_0_
  24.9 0.5 %collective-permute-start.1 = (f32[2,64,256]{2,1,0:T(8,128)S(1)}, f32[2,64,256]{2,1,0:T(8,128)S(1)}, u32[]{:S(2)}, u32[]{:S(2)}) collective-permute-start(f32[2,64,256]{2,1,0:T(8,128)S(1)} %get-tuple-element.41), channel_id=1, source_target_pairs={{0,8},{4,12},{8,0},{12,4},{16,24},{20,28},{24,16},{28,20},{1,9},{5... | collective-permute-start | bytes 393224 | tf_op jit(solution)/shard_map/ppermute | solution.py:600
  25.3 1.3 %collective-permute-done.6.refs_1_ = f32[2,64,256]{2,1,0:T(8,128)S(1)} collective-permute-done((f32[2,64,256]{2,1,0:T(8,128)S(1)}, f32[2,64,256]{2,1,0:T(8,128)S(1)}, u32[]{:S(2)}, u32[]{:S(2)}) %collective-permute-start.6) | collective-permute-done | bytes 131104 | tf_op jit(solution)/shard_map/ppermute | solution.py:600
  26.7 0.0 collective-permute-done.7.refs_2_
  26.7 1.6 %collective-permute-start.8 = (f32[2,192,256]{2,1,0:T(8,128)S(1)}, f32[2,192,256]{2,1,0:T(8,128)S(1)}, u32[]{:S(2)}, u32[]{:S(2)}) collective-permute-start(f32[2,192,256]{2,1,0:T(8,128)S(1)} %joined.3.own_ref), channel_id=1, source_target_pairs={{0,2},{1,3},{2,0},{3,1},{4,6},{5,7},{6,4},{7,5},{8,10},{9,11},{10,... | collective-permute-start | bytes 1179656 | tf_op jit(solution)/shard_map/ppermute | solution.py:600
  28.3 2.3 %collective-permute-start.9 = (f32[2,64,256]{2,1,0:T(8,128)S(1)}, f32[2,64,256]{2,1,0:T(8,128)S(1)}, u32[]{:S(2)}, u32[]{:S(2)}) collective-permute-start(f32[2,64,256]{2,1,0:T(8,128)S(1)} %get-tuple-element.61), channel_id=1, source_target_pairs={{0,28},{4,24},{8,20},{12,16},{16,12},{20,8},{24,4},{28,0},{1,29},{... | collective-permute-start | bytes 393224 | tf_op jit(solution)/shard_map/ppermute | solution.py:600
  30.6 0.0 collective-permute-done.3.refs_0_
  30.6 0.0 collective-permute-done.4.refs_2_
  30.6 0.3 collective-permute-done.1.refs_1_
  30.9 0.1 turned_pieces.1.own_ref
  31.0 0.1 collective-permute-start.11
  31.0 2.6 %second_gates.1 = (bf16[512,512]{1,0:T(8,128)(2,1)S(1)}, bf16[512,512]{1,0:T(8,128)(2,1)S(1)}, bf16[512,512]{1,0:T(8,128)(2,1)S(1)}, bf16[512,512]{1,0:T(8,128)(2,1)S(1)}) custom-call(f32[2,2,512,512]{3,2,1,0:T(8,128)} %gates_hbm.2), custom_call_target="tpu_custom_call" | custom-call | flops 1000 | bytes 1000 | tf_op jit(solution)/shard_map/second_gates/pallas_call | solution.py:404
  33.7 1.9 %collective-permute-done.8.other_ref = f32[2,192,256]{2,1,0:T(8,128)S(1)} collective-permute-done((f32[2,192,256]{2,1,0:T(8,128)S(1)}, f32[2,192,256]{2,1,0:T(8,128)S(1)}, u32[]{:S(2)}, u32[]{:S(2)}) %collective-permute-start.8) | collective-permute-done | bytes 393248 | tf_op jit(solution)/shard_map/ppermute | solution.py:600
  35.6 0.4 %collective-permute-done.9.last_ref = f32[2,64,256]{2,1,0:T(8,128)S(1)} collective-permute-done((f32[2,64,256]{2,1,0:T(8,128)S(1)}, f32[2,64,256]{2,1,0:T(8,128)S(1)}, u32[]{:S(2)}, u32[]{:S(2)}) %collective-permute-start.9) | collective-permute-done | bytes 131104 | tf_op jit(solution)/shard_map/ppermute | solution.py:600
  36.0 0.2 turned.1.own_ref
  36.2 0.1 collective-permute-start.10
  36.2 0.0 collective-permute-done.11.other_ref
  36.3 1.1 %middle.1.sum_ref = f32[2,512,256]{2,1,0:T(8,128)S(1)} custom-call(bf16[512,512]{1,0:T(8,128)(2,1)S(1)} %get-tuple-element.59.high_ref, bf16[512,512]{1,0:T(8,128)(2,1)S(1)} %get-tuple-element.62.low_ref, f32[8,256]{1,0:T(8,128)S(1)} %get-tuple-element.42.coefficients_ref, f32[2,256,256]{2,1,0:T(8,128)S(1)} %turned_pieces.1.own_ref, ...), custom_call_target="tpu_custom_call" | custom-call | flops 1000 | bytes 1000 | tf_op jit(solution)/shard_map/middle/pallas_call | solution.py:522
  37.4 0.8 %collective-permute-done.10.other_ref = f32[2,256,256]{2,1,0:T(8,128)S(1)} collective-permute-done((f32[2,256,256]{2,1,0:T(8,128)S(1)}, f32[2,256,256]{2,1,0:T(8,128)S(1)}, u32[]{:S(2)}, u32[]{:S(2)}) %collective-permute-start.10) | collective-permute-done | bytes 524320 | tf_op jit(solution)/shard_map/ppermute | solution.py:600
  38.1 1.9 %last.1 = f32[2,1,512,256]{3,2,1,0:T(8,128)} custom-call(bf16[512,512]{1,0:T(8,128)(2,1)S(1)} %get-tuple-element.49.high_ref, bf16[512,512]{1,0:T(8,128)(2,1)S(1)} %get-tuple-element.50.low_ref, f32[8,256]{1,0:T(8,128)S(1)} %get-tuple-element.42.coefficients_ref, f32[2,256,256]{2,1,0:T(8,128)S(1)} %turned.1.own_ref, ...), custom_call_target="tpu_custom_call" | custom-call | flops 1000 | bytes 1000 | tf_op jit(solution)/shard_map/last/pallas_call | solution.py:587
  (2 shorter events, 0.0 us)
Async XLA Ops:
  0.0 11.8 %copy-start.3 = (f32[2,1]{0,1:T(1,128)S(1)}, f32[2,1]{0,1:T(1,128)}, u32[]{:S(2)}) copy-start(f32[2,1]{0,1:T(1,128)} %param.11) | copy-start | bytes 28
  0.0 11.8 %copy-start = (f32[2,2,2,2]{3,2,1,0:T(2,128)S(1)}, f32[2,2,2,2]{3,2,1,0:T(2,128)}, u32[]{:S(2)}) copy-start(f32[2,2,2,2]{3,2,1,0:T(2,128)} %pair_ref.1) | copy-start | bytes 196
  0.0 11.8 %copy-start.1 = (f32[2,17]{1,0:T(2,128)S(1)}, f32[2,17]{1,0:T(2,128)}, u32[]{:S(2)}) copy-start(f32[2,17]{1,0:T(2,128)} %phases_ref) | copy-start | bytes 412
  0.0 11.8 %copy-start.4 = (s32[17]{0:T(128)S(1)}, s32[17]{0:T(128)}, u32[]{:S(2)}) copy-start(s32[17]{0:T(128)} %bits_ref.1) | copy-start | bytes 208
  0.0 11.8 %copy-start.2 = (s32[2,17]{1,0:T(2,128)S(1)}, s32[2,17]{1,0:T(2,128)}, u32[]{:S(2)}) copy-start(s32[2,17]{1,0:T(2,128)} %coupled_ref.1) | copy-start | bytes 412
  4.2 10.1 %collective-permute-start.2 = (f32[2,128,256]{2,1,0:T(8,128)S(1)}, f32[2,128,256]{2,1,0:T(8,128)S(1)}, u32[]{:S(2)}, u32[]{:S(2)}) collective-permute-start(f32[2,128,256]{2,1,0:T(8,128)S(1)} %get-tuple-element.34.own_ref), channel_id=1, source_target_pairs={{0,2},{1,3},{2,0},{3,1},{4,6},{5,7},{6,4},{7,5},{8,10},{9,11},{10,... | collective-permute-start | bytes 786440 | tf_op jit(solution)/shard_map/ppermute | solution.py:600
  7.2 14.7 %collective-permute-start = (f32[2,192,256]{2,1,0:T(8,128)S(1)}, f32[2,192,256]{2,1,0:T(8,128)S(1)}, u32[]{:S(2)}, u32[]{:S(2)}) collective-permute-start(f32[2,192,256]{2,1,0:T(8,128)S(1)} %get-tuple-element.39.own_ref), channel_id=1, source_target_pairs={{0,2},{1,3},{2,0},{3,1},{4,6},{5,7},{6,4},{7,5},{8,10},{9,11},{10,... | collective-permute-start | bytes 1179656 | tf_op jit(solution)/shard_map/ppermute | solution.py:600
  7.3 17.6 %collective-permute-start.5 = (f32[2,64,256]{2,1,0:T(8,128)S(1)}, f32[2,64,256]{2,1,0:T(8,128)S(1)}, u32[]{:S(2)}, u32[]{:S(2)}) collective-permute-start(f32[2,64,256]{2,1,0:T(8,128)S(1)} %get-tuple-element.53), channel_id=1, source_target_pairs={{0,16},{4,20},{8,24},{12,28},{16,0},{20,4},{24,8},{28,12},{1,17},{... | collective-permute-start | bytes 393224 | tf_op jit(solution)/shard_map/ppermute | solution.py:600
  10.3 16.4 %collective-permute-start.6 = (f32[2,64,256]{2,1,0:T(8,128)S(1)}, f32[2,64,256]{2,1,0:T(8,128)S(1)}, u32[]{:S(2)}, u32[]{:S(2)}) collective-permute-start(f32[2,64,256]{2,1,0:T(8,128)S(1)} %get-tuple-element.55), channel_id=1, source_target_pairs={{0,20},{4,16},{8,28},{12,24},{16,4},{20,0},{24,12},{28,8},{1,21},{... | collective-permute-start | bytes 393224 | tf_op jit(solution)/shard_map/ppermute | solution.py:600
  11.6 15.1 %collective-permute-start.7 = (f32[2,64,256]{2,1,0:T(8,128)S(1)}, f32[2,64,256]{2,1,0:T(8,128)S(1)}, u32[]{:S(2)}, u32[]{:S(2)}) collective-permute-start(f32[2,64,256]{2,1,0:T(8,128)S(1)} %get-tuple-element.57), channel_id=1, source_target_pairs={{0,4},{4,0},{8,12},{12,8},{16,20},{20,16},{24,28},{28,24},{1,5},{5... | collective-permute-start | bytes 393224 | tf_op jit(solution)/shard_map/ppermute | solution.py:600
  14.4 16.2 %collective-permute-start.3 = (f32[2,64,256]{2,1,0:T(8,128)S(1)}, f32[2,64,256]{2,1,0:T(8,128)S(1)}, u32[]{:S(2)}, u32[]{:S(2)}) collective-permute-start(f32[2,64,256]{2,1,0:T(8,128)S(1)} %get-tuple-element.44), channel_id=1, source_target_pairs={{0,24},{4,28},{8,16},{12,20},{16,8},{20,12},{24,0},{28,4},{1,25},{... | collective-permute-start | bytes 393224 | tf_op jit(solution)/shard_map/ppermute | solution.py:600
  22.0 8.6 %collective-permute-start.4 = (f32[2,64,256]{2,1,0:T(8,128)S(1)}, f32[2,64,256]{2,1,0:T(8,128)S(1)}, u32[]{:S(2)}, u32[]{:S(2)}) collective-permute-start(f32[2,64,256]{2,1,0:T(8,128)S(1)} %get-tuple-element.46), channel_id=1, source_target_pairs={{0,12},{4,8},{8,4},{12,0},{16,28},{20,24},{24,20},{28,16},{1,13},{... | collective-permute-start | bytes 393224 | tf_op jit(solution)/shard_map/ppermute | solution.py:600
  24.9 6.0 %collective-permute-start.1 = (f32[2,64,256]{2,1,0:T(8,128)S(1)}, f32[2,64,256]{2,1,0:T(8,128)S(1)}, u32[]{:S(2)}, u32[]{:S(2)}) collective-permute-start(f32[2,64,256]{2,1,0:T(8,128)S(1)} %get-tuple-element.41), channel_id=1, source_target_pairs={{0,8},{4,12},{8,0},{12,4},{16,24},{20,28},{24,16},{28,20},{1,9},{5... | collective-permute-start | bytes 393224 | tf_op jit(solution)/shard_map/ppermute | solution.py:600
  26.7 8.8 %collective-permute-start.8 = (f32[2,192,256]{2,1,0:T(8,128)S(1)}, f32[2,192,256]{2,1,0:T(8,128)S(1)}, u32[]{:S(2)}, u32[]{:S(2)}) collective-permute-start(f32[2,192,256]{2,1,0:T(8,128)S(1)} %joined.3.own_ref), channel_id=1, source_target_pairs={{0,2},{1,3},{2,0},{3,1},{4,6},{5,7},{6,4},{7,5},{8,10},{9,11},{10,... | collective-permute-start | bytes 1179656 | tf_op jit(solution)/shard_map/ppermute | solution.py:600
  28.3 7.7 %collective-permute-start.9 = (f32[2,64,256]{2,1,0:T(8,128)S(1)}, f32[2,64,256]{2,1,0:T(8,128)S(1)}, u32[]{:S(2)}, u32[]{:S(2)}) collective-permute-start(f32[2,64,256]{2,1,0:T(8,128)S(1)} %get-tuple-element.61), channel_id=1, source_target_pairs={{0,28},{4,24},{8,20},{12,16},{16,12},{20,8},{24,4},{28,0},{1,29},{... | collective-permute-start | bytes 393224 | tf_op jit(solution)/shard_map/ppermute | solution.py:600
  31.0 5.3 %collective-permute-start.11 = (f32[2,256,256]{2,1,0:T(8,128)S(1)}, f32[2,256,256]{2,1,0:T(8,128)S(1)}, u32[]{:S(2)}, u32[]{:S(2)}) collective-permute-start(f32[2,256,256]{2,1,0:T(8,128)S(1)} %turned_pieces.1.own_ref), channel_id=1, source_target_pairs={{0,1},{1,0},{2,3},{3,2},{4,5},{5,4},{6,7},{7,6},{8,9},{9,8},{10,11... | collective-permute-start | bytes 1572872 | tf_op jit(solution)/shard_map/ppermute | solution.py:600
  36.2 2.0 %collective-permute-start.10 = (f32[2,256,256]{2,1,0:T(8,128)S(1)}, f32[2,256,256]{2,1,0:T(8,128)S(1)}, u32[]{:S(2)}, u32[]{:S(2)}) collective-permute-start(f32[2,256,256]{2,1,0:T(8,128)S(1)} %turned.1.own_ref), channel_id=1, source_target_pairs={{0,1},{1,0},{2,3},{3,2},{4,5},{5,4},{6,7},{7,6},{8,9},{9,8},{10,11... | collective-permute-start | bytes 1572872 | tf_op jit(solution)/shard_map/ppermute | solution.py:600

commit v5 on v4

--- a/solution.py
+++ b/solution.py
@@ -616,7 +616,7 @@
     beside = tuple(range(1, quarter))
     near = tuple(range(quarter, 2 * quarter))
     far = tuple(range(2 * quarter, 3 * quarter))
-    early = tuple(range(3 * quarter, count))
+    early = tuple(reversed(range(3 * quarter, count)))
     late = far + beside
     cross = functools.partial(swap, axis="lo", mask=1 << top_bit)
 

time: 40.2 us -> 39.9 us (level)
  waiting for transfers between devices: 9.56 us -> 8.24 us
  starting transfers between devices: 19.2 us -> 20.2 us
    ppermute x12, waiting for transfers between devices: 9.56 us -> 8.24 us  [swap(): lax.ppermute(value, axis, [(i, i ^ mask) for i in range(lax.axis_size(axi...]
    ppermute x12, starting transfers between devices: 19.2 us -> 20.2 us  [swap(): lax.ppermute(value, axis, [(i, i ^ mask) for i in range(lax.axis_size(axi...]
where the time goes in v5:
time: 39.9 us; the launch traced here: 39.7 us
  starting transfers between devices  20.2 us (51%)
  Pallas kernels  11.1 us (28%)
  waiting for transfers between devices  8.24 us (21%)
    ppermute x12, starting transfers between devices, swap(): lax.ppermute(value, axis, [(i, i ^ mask) for i in range(lax.axis_size(axi...  20.2 us
    ppermute x12, waiting for transfers between devices, swap(): lax.ppermute(value, axis, [(i, i ^ mask) for i in range(lax.axis_size(axi...  8.24 us
    pallas_call x1, Pallas kernels, first(): pl.pallas_call(functools.partial(first_kernel, groups, piece_rows, col_bi...  4.17 us
    pallas_call x1, Pallas kernels, second_gates(): pl.pallas_call(functools.partial(gates_kernel, sets, piece_rows), out_sha...  2.62 us
    pallas_call x1, Pallas kernels, last(): pl.pallas_call(last_kernel, out_shape=jax.ShapeDtypeStruct(shape, F32), i...  1.9 us
    pallas_call x1, Pallas kernels, middle(): pl.pallas_call(middle_kernel, out_shape=jax.ShapeDtypeStruct((2, parts[0]...  1.13 us
    pallas_call x1, Pallas kernels, second_phases(): pl.pallas_call(functools.partial(phases_kernel, sets, piece_rows, col_bit...  0.89 us
  transfers between devices with their start and end apart: 12, of which 7 were waited for; matrix products, arithmetic and copies ran while one was open for 0% of the time, Pallas kernels for 13%

profile of v5, /device:TPU:0, one launch (start us, length us, event | category | flops | bytes accessed | tf_op | source)
XLA Modules:
  0.0 39.7 jit_solution(4542954977454456497)
XLA Ops:
  0.0 0.0 copy-start.3
  0.0 0.0 copy-start
  0.0 0.0 copy-start.1
  0.0 0.0 copy-start.4
  0.0 0.0 copy-start.2
  0.0 4.2 %first.1 = (f32[8,256]{1,0:T(8,128)S(1)}, f32[2,128,256]{2,1,0:T(8,128)S(1)}, f32[2,192,256]{2,1,0:T(8,128)S(1)}, f32[2,64,256]{2,1,0:T(8,128)S(1)}, f32[2,64,25...) custom-call(f32[2,1,512,256]{3,2,1,0:T(8,128)} %amplitudes_hbm.1, f32[2,2,512,512]{3,2,1,0:T(8,128)} %gates_hbm.2, ...), custom_call_target="tpu_custom_call" | custom-call | flops 1000 | bytes 1000 | tf_op jit(solution)/shard_map/first/pallas_call | solution.py:281
  4.2 3.0 %collective-permute-start.2 = (f32[2,128,256]{2,1,0:T(8,128)S(1)}, f32[2,128,256]{2,1,0:T(8,128)S(1)}, u32[]{:S(2)}, u32[]{:S(2)}) collective-permute-start(f32[2,128,256]{2,1,0:T(8,128)S(1)} %get-tuple-element.34.own_ref), channel_id=1, source_target_pairs={{0,2},{1,3},{2,0},{3,1},{4,6},{5,7},{6,4},{7,5},{8,10},{9,11},{10,... | collective-permute-start | bytes 786440 | tf_op jit(solution)/shard_map/ppermute | solution.py:600
  7.2 0.1 collective-permute-start
  7.3 3.0 %collective-permute-start.5 = (f32[2,64,256]{2,1,0:T(8,128)S(1)}, f32[2,64,256]{2,1,0:T(8,128)S(1)}, u32[]{:S(2)}, u32[]{:S(2)}) collective-permute-start(f32[2,64,256]{2,1,0:T(8,128)S(1)} %get-tuple-element.53), channel_id=1, source_target_pairs={{0,16},{4,20},{8,24},{12,28},{16,0},{20,4},{24,8},{28,12},{1,17},{... | collective-permute-start | bytes 393224 | tf_op jit(solution)/shard_map/ppermute | solution.py:600
  10.3 1.3 %collective-permute-start.6 = (f32[2,64,256]{2,1,0:T(8,128)S(1)}, f32[2,64,256]{2,1,0:T(8,128)S(1)}, u32[]{:S(2)}, u32[]{:S(2)}) collective-permute-start(f32[2,64,256]{2,1,0:T(8,128)S(1)} %get-tuple-element.55), channel_id=1, source_target_pairs={{0,20},{4,16},{8,28},{12,24},{16,4},{20,0},{24,12},{28,8},{1,21},{... | collective-permute-start | bytes 393224 | tf_op jit(solution)/shard_map/ppermute | solution.py:600
  11.6 0.2 collective-permute-start.7
  11.8 0.0 copy-done.3
  11.8 0.0 copy-done
  11.8 0.0 copy-done.1
  11.8 0.0 copy-done.4
  11.9 0.0 copy-done.2
  11.9 0.9 %second_phases.1 = (f32[256,128]{1,0:T(8,128)S(1)}, f32[256,128]{1,0:T(8,128)S(1)}, f32[256,128]{1,0:T(8,128)S(1)}, f32[256,128]{1,0:T(8,128)S(1)}, f32[8,256]{1,0:T(8,128)S(1)}) custom-call(f32[2,17]{1,0:T(2,128)S(1)} %copy-done.1, f32[1,2]{1,0:T(1,128)S(1)} %bitcast.2, s32[17]{0:T(128)S(1)} %copy-done.4, s32[2,17]{1,0:T(2,128)S(1)} %copy-done.2, ...), custom_call_target="tpu_custom_call" | custom-call | flops 1000 | bytes 1000 | tf_op jit(solution)/shard_map/second_phases/pallas_call | solution.py:357
  12.8 1.6 %collective-permute-done.2.other_ref = f32[2,128,256]{2,1,0:T(8,128)S(1)} collective-permute-done((f32[2,128,256]{2,1,0:T(8,128)S(1)}, f32[2,128,256]{2,1,0:T(8,128)S(1)}, u32[]{:S(2)}, u32[]{:S(2)}) %collective-permute-start.2) | collective-permute-done | bytes 262176 | tf_op jit(solution)/shard_map/ppermute | solution.py:600
  14.3 0.1 combine.3
  14.4 5.2 %collective-permute-start.3 = (f32[2,64,256]{2,1,0:T(8,128)S(1)}, f32[2,64,256]{2,1,0:T(8,128)S(1)}, u32[]{:S(2)}, u32[]{:S(2)}) collective-permute-start(f32[2,64,256]{2,1,0:T(8,128)S(1)} %get-tuple-element.44), channel_id=1, source_target_pairs={{0,28},{4,24},{8,20},{12,16},{16,12},{20,8},{24,4},{28,0},{1,29},{... | collective-permute-start | bytes 393224 | tf_op jit(solution)/shard_map/ppermute | solution.py:600
  19.6 2.3 %collective-permute-done.other_ref = f32[2,192,256]{2,1,0:T(8,128)S(1)} collective-permute-done((f32[2,192,256]{2,1,0:T(8,128)S(1)}, f32[2,192,256]{2,1,0:T(8,128)S(1)}, u32[]{:S(2)}, u32[]{:S(2)}) %collective-permute-start) | collective-permute-done | bytes 393248 | tf_op jit(solution)/shard_map/ppermute | solution.py:600
  21.9 0.1 combine.2
  22.0 2.8 %collective-permute-start.4 = (f32[2,64,256]{2,1,0:T(8,128)S(1)}, f32[2,64,256]{2,1,0:T(8,128)S(1)}, u32[]{:S(2)}, u32[]{:S(2)}) collective-permute-start(f32[2,64,256]{2,1,0:T(8,128)S(1)} %get-tuple-element.46), channel_id=1, source_target_pairs={{0,12},{4,8},{8,4},{12,0},{16,28},{20,24},{24,20},{28,16},{1,13},{... | collective-permute-start | bytes 393224 | tf_op jit(solution)/shard_map/ppermute | solution.py:600
  24.9 0.0 collective-permute-done.5.refs_0_
  24.9 0.5 %collective-permute-start.1 = (f32[2,64,256]{2,1,0:T(8,128)S(1)}, f32[2,64,256]{2,1,0:T(8,128)S(1)}, u32[]{:S(2)}, u32[]{:S(2)}) collective-permute-start(f32[2,64,256]{2,1,0:T(8,128)S(1)} %get-tuple-element.41), channel_id=1, source_target_pairs={{0,8},{4,12},{8,0},{12,4},{16,24},{20,28},{24,16},{28,20},{1,9},{5... | collective-permute-start | bytes 393224 | tf_op jit(solution)/shard_map/ppermute | solution.py:600
  25.3 1.3 %collective-permute-done.6.refs_1_ = f32[2,64,256]{2,1,0:T(8,128)S(1)} collective-permute-done((f32[2,64,256]{2,1,0:T(8,128)S(1)}, f32[2,64,256]{2,1,0:T(8,128)S(1)}, u32[]{:S(2)}, u32[]{:S(2)}) %collective-permute-start.6) | collective-permute-done | bytes 131104 | tf_op jit(solution)/shard_map/ppermute | solution.py:600
  26.7 0.0 collective-permute-done.7.refs_2_
  26.7 1.6 %collective-permute-start.8 = (f32[2,192,256]{2,1,0:T(8,128)S(1)}, f32[2,192,256]{2,1,0:T(8,128)S(1)}, u32[]{:S(2)}, u32[]{:S(2)}) collective-permute-start(f32[2,192,256]{2,1,0:T(8,128)S(1)} %joined.3.own_ref), channel_id=1, source_target_pairs={{0,2},{1,3},{2,0},{3,1},{4,6},{5,7},{6,4},{7,5},{8,10},{9,11},{10,... | collective-permute-start | bytes 1179656 | tf_op jit(solution)/shard_map/ppermute | solution.py:600
  28.3 2.4 %collective-permute-start.9 = (f32[2,64,256]{2,1,0:T(8,128)S(1)}, f32[2,64,256]{2,1,0:T(8,128)S(1)}, u32[]{:S(2)}, u32[]{:S(2)}) collective-permute-start(f32[2,64,256]{2,1,0:T(8,128)S(1)} %get-tuple-element.61), channel_id=1, source_target_pairs={{0,24},{4,28},{8,16},{12,20},{16,8},{20,12},{24,0},{28,4},{1,25},{... | collective-permute-start | bytes 393224 | tf_op jit(solution)/shard_map/ppermute | solution.py:600
  30.7 0.0 collective-permute-done.3.refs_0_
  30.7 0.0 collective-permute-done.4.refs_2_
  30.7 0.2 collective-permute-done.1.refs_1_
  30.9 0.1 turned_pieces.1.own_ref
  31.0 0.1 collective-permute-start.11
  31.0 2.6 %second_gates.1 = (bf16[512,512]{1,0:T(8,128)(2,1)S(1)}, bf16[512,512]{1,0:T(8,128)(2,1)S(1)}, bf16[512,512]{1,0:T(8,128)(2,1)S(1)}, bf16[512,512]{1,0:T(8,128)(2,1)S(1)}) custom-call(f32[2,2,512,512]{3,2,1,0:T(8,128)} %gates_hbm.2), custom_call_target="tpu_custom_call" | custom-call | flops 1000 | bytes 1000 | tf_op jit(solution)/shard_map/second_gates/pallas_call | solution.py:404
  33.7 1.9 %collective-permute-done.8.other_ref = f32[2,192,256]{2,1,0:T(8,128)S(1)} collective-permute-done((f32[2,192,256]{2,1,0:T(8,128)S(1)}, f32[2,192,256]{2,1,0:T(8,128)S(1)}, u32[]{:S(2)}, u32[]{:S(2)}) %collective-permute-start.8) | collective-permute-done | bytes 393248 | tf_op jit(solution)/shard_map/ppermute | solution.py:600
  35.6 0.1 collective-permute-done.9.last_ref
  35.7 0.2 turned.1.own_ref
  35.9 0.1 collective-permute-start.10
  35.9 0.0 collective-permute-done.11.other_ref
  36.0 1.1 %middle.1.sum_ref = f32[2,512,256]{2,1,0:T(8,128)S(1)} custom-call(bf16[512,512]{1,0:T(8,128)(2,1)S(1)} %get-tuple-element.59.high_ref, bf16[512,512]{1,0:T(8,128)(2,1)S(1)} %get-tuple-element.62.low_ref, f32[8,256]{1,0:T(8,128)S(1)} %get-tuple-element.42.coefficients_ref, f32[2,256,256]{2,1,0:T(8,128)S(1)} %turned_pieces.1.own_ref, ...), custom_call_target="tpu_custom_call" | custom-call | flops 1000 | bytes 1000 | tf_op jit(solution)/shard_map/middle/pallas_call | solution.py:522
  37.1 0.8 %collective-permute-done.10.other_ref = f32[2,256,256]{2,1,0:T(8,128)S(1)} collective-permute-done((f32[2,256,256]{2,1,0:T(8,128)S(1)}, f32[2,256,256]{2,1,0:T(8,128)S(1)}, u32[]{:S(2)}, u32[]{:S(2)}) %collective-permute-start.10) | collective-permute-done | bytes 524320 | tf_op jit(solution)/shard_map/ppermute | solution.py:600
  37.8 1.9 %last.1 = f32[2,1,512,256]{3,2,1,0:T(8,128)} custom-call(bf16[512,512]{1,0:T(8,128)(2,1)S(1)} %get-tuple-element.49.high_ref, bf16[512,512]{1,0:T(8,128)(2,1)S(1)} %get-tuple-element.50.low_ref, f32[8,256]{1,0:T(8,128)S(1)} %get-tuple-element.42.coefficients_ref, f32[2,256,256]{2,1,0:T(8,128)S(1)} %turned.1.own_ref, ...), custom_call_target="tpu_custom_call" | custom-call | flops 1000 | bytes 1000 | tf_op jit(solution)/shard_map/last/pallas_call | solution.py:587
  (2 shorter events, 0.0 us)
Async XLA Ops:
  0.0 11.8 %copy-start.3 = (f32[2,1]{0,1:T(1,128)S(1)}, f32[2,1]{0,1:T(1,128)}, u32[]{:S(2)}) copy-start(f32[2,1]{0,1:T(1,128)} %param.11) | copy-start | bytes 28
  0.0 11.8 %copy-start = (f32[2,2,2,2]{3,2,1,0:T(2,128)S(1)}, f32[2,2,2,2]{3,2,1,0:T(2,128)}, u32[]{:S(2)}) copy-start(f32[2,2,2,2]{3,2,1,0:T(2,128)} %pair_ref.1) | copy-start | bytes 196
  0.0 11.8 %copy-start.1 = (f32[2,17]{1,0:T(2,128)S(1)}, f32[2,17]{1,0:T(2,128)}, u32[]{:S(2)}) copy-start(f32[2,17]{1,0:T(2,128)} %phases_ref) | copy-start | bytes 412
  0.0 11.8 %copy-start.4 = (s32[17]{0:T(128)S(1)}, s32[17]{0:T(128)}, u32[]{:S(2)}) copy-start(s32[17]{0:T(128)} %bits_ref.1) | copy-start | bytes 208
  0.0 11.8 %copy-start.2 = (s32[2,17]{1,0:T(2,128)S(1)}, s32[2,17]{1,0:T(2,128)}, u32[]{:S(2)}) copy-start(s32[2,17]{1,0:T(2,128)} %coupled_ref.1) | copy-start | bytes 412
  4.2 10.1 %collective-permute-start.2 = (f32[2,128,256]{2,1,0:T(8,128)S(1)}, f32[2,128,256]{2,1,0:T(8,128)S(1)}, u32[]{:S(2)}, u32[]{:S(2)}) collective-permute-start(f32[2,128,256]{2,1,0:T(8,128)S(1)} %get-tuple-element.34.own_ref), channel_id=1, source_target_pairs={{0,2},{1,3},{2,0},{3,1},{4,6},{5,7},{6,4},{7,5},{8,10},{9,11},{10,... | collective-permute-start | bytes 786440 | tf_op jit(solution)/shard_map/ppermute | solution.py:600
  7.2 14.7 %collective-permute-start = (f32[2,192,256]{2,1,0:T(8,128)S(1)}, f32[2,192,256]{2,1,0:T(8,128)S(1)}, u32[]{:S(2)}, u32[]{:S(2)}) collective-permute-start(f32[2,192,256]{2,1,0:T(8,128)S(1)} %get-tuple-element.39.own_ref), channel_id=1, source_target_pairs={{0,2},{1,3},{2,0},{3,1},{4,6},{5,7},{6,4},{7,5},{8,10},{9,11},{10,... | collective-permute-start | bytes 1179656 | tf_op jit(solution)/shard_map/ppermute | solution.py:600
  7.3 17.6 %collective-permute-start.5 = (f32[2,64,256]{2,1,0:T(8,128)S(1)}, f32[2,64,256]{2,1,0:T(8,128)S(1)}, u32[]{:S(2)}, u32[]{:S(2)}) collective-permute-start(f32[2,64,256]{2,1,0:T(8,128)S(1)} %get-tuple-element.53), channel_id=1, source_target_pairs={{0,16},{4,20},{8,24},{12,28},{16,0},{20,4},{24,8},{28,12},{1,17},{... | collective-permute-start | bytes 393224 | tf_op jit(solution)/shard_map/ppermute | solution.py:600
  10.3 16.4 %collective-permute-start.6 = (f32[2,64,256]{2,1,0:T(8,128)S(1)}, f32[2,64,256]{2,1,0:T(8,128)S(1)}, u32[]{:S(2)}, u32[]{:S(2)}) collective-permute-start(f32[2,64,256]{2,1,0:T(8,128)S(1)} %get-tuple-element.55), channel_id=1, source_target_pairs={{0,20},{4,16},{8,28},{12,24},{16,4},{20,0},{24,12},{28,8},{1,21},{... | collective-permute-start | bytes 393224 | tf_op jit(solution)/shard_map/ppermute | solution.py:600
  11.6 15.1 %collective-permute-start.7 = (f32[2,64,256]{2,1,0:T(8,128)S(1)}, f32[2,64,256]{2,1,0:T(8,128)S(1)}, u32[]{:S(2)}, u32[]{:S(2)}) collective-permute-start(f32[2,64,256]{2,1,0:T(8,128)S(1)} %get-tuple-element.57), channel_id=1, source_target_pairs={{0,4},{4,0},{8,12},{12,8},{16,20},{20,16},{24,28},{28,24},{1,5},{5... | collective-permute-start | bytes 393224 | tf_op jit(solution)/shard_map/ppermute | solution.py:600
  14.4 16.3 %collective-permute-start.3 = (f32[2,64,256]{2,1,0:T(8,128)S(1)}, f32[2,64,256]{2,1,0:T(8,128)S(1)}, u32[]{:S(2)}, u32[]{:S(2)}) collective-permute-start(f32[2,64,256]{2,1,0:T(8,128)S(1)} %get-tuple-element.44), channel_id=1, source_target_pairs={{0,28},{4,24},{8,20},{12,16},{16,12},{20,8},{24,4},{28,0},{1,29},{... | collective-permute-start | bytes 393224 | tf_op jit(solution)/shard_map/ppermute | solution.py:600
  22.0 8.7 %collective-permute-start.4 = (f32[2,64,256]{2,1,0:T(8,128)S(1)}, f32[2,64,256]{2,1,0:T(8,128)S(1)}, u32[]{:S(2)}, u32[]{:S(2)}) collective-permute-start(f32[2,64,256]{2,1,0:T(8,128)S(1)} %get-tuple-element.46), channel_id=1, source_target_pairs={{0,12},{4,8},{8,4},{12,0},{16,28},{20,24},{24,20},{28,16},{1,13},{... | collective-permute-start | bytes 393224 | tf_op jit(solution)/shard_map/ppermute | solution.py:600
  24.9 6.0 %collective-permute-start.1 = (f32[2,64,256]{2,1,0:T(8,128)S(1)}, f32[2,64,256]{2,1,0:T(8,128)S(1)}, u32[]{:S(2)}, u32[]{:S(2)}) collective-permute-start(f32[2,64,256]{2,1,0:T(8,128)S(1)} %get-tuple-element.41), channel_id=1, source_target_pairs={{0,8},{4,12},{8,0},{12,4},{16,24},{20,28},{24,16},{28,20},{1,9},{5... | collective-permute-start | bytes 393224 | tf_op jit(solution)/shard_map/ppermute | solution.py:600
  26.7 8.8 %collective-permute-start.8 = (f32[2,192,256]{2,1,0:T(8,128)S(1)}, f32[2,192,256]{2,1,0:T(8,128)S(1)}, u32[]{:S(2)}, u32[]{:S(2)}) collective-permute-start(f32[2,192,256]{2,1,0:T(8,128)S(1)} %joined.3.own_ref), channel_id=1, source_target_pairs={{0,2},{1,3},{2,0},{3,1},{4,6},{5,7},{6,4},{7,5},{8,10},{9,11},{10,... | collective-permute-start | bytes 1179656 | tf_op jit(solution)/shard_map/ppermute | solution.py:600
  28.3 7.4 %collective-permute-start.9 = (f32[2,64,256]{2,1,0:T(8,128)S(1)}, f32[2,64,256]{2,1,0:T(8,128)S(1)}, u32[]{:S(2)}, u32[]{:S(2)}) collective-permute-start(f32[2,64,256]{2,1,0:T(8,128)S(1)} %get-tuple-element.61), channel_id=1, source_target_pairs={{0,24},{4,28},{8,16},{12,20},{16,8},{20,12},{24,0},{28,4},{1,25},{... | collective-permute-start | bytes 393224 | tf_op jit(solution)/shard_map/ppermute | solution.py:600
  31.0 5.0 %collective-permute-start.11 = (f32[2,256,256]{2,1,0:T(8,128)S(1)}, f32[2,256,256]{2,1,0:T(8,128)S(1)}, u32[]{:S(2)}, u32[]{:S(2)}) collective-permute-start(f32[2,256,256]{2,1,0:T(8,128)S(1)} %turned_pieces.1.own_ref), channel_id=1, source_target_pairs={{0,1},{1,0},{2,3},{3,2},{4,5},{5,4},{6,7},{7,6},{8,9},{9,8},{10,11... | collective-permute-start | bytes 1572872 | tf_op jit(solution)/shard_map/ppermute | solution.py:600
  35.9 2.0 %collective-permute-start.10 = (f32[2,256,256]{2,1,0:T(8,128)S(1)}, f32[2,256,256]{2,1,0:T(8,128)S(1)}, u32[]{:S(2)}, u32[]{:S(2)}) collective-permute-start(f32[2,256,256]{2,1,0:T(8,128)S(1)} %turned.1.own_ref), channel_id=1, source_target_pairs={{0,1},{1,0},{2,3},{3,2},{4,5},{5,4},{6,7},{7,6},{8,9},{9,8},{10,11... | collective-permute-start | bytes 1572872 | tf_op jit(solution)/shard_map/ppermute | solution.py:600

commit v6 on v5

--- a/solution.py
+++ b/solution.py
@@ -13,7 +13,7 @@
 MIDDLE_COST = 3000000000
 HALF_COST = 1000
 CHUNKS = 2
-LAST_CHUNKS = 4
+LAST_PARTS = (2, 1, 1)
 COMBINE_COST = 1500001000
 LATE_COST = 1000
 
@@ -563,11 +563,12 @@
 ):
     cols = own_ref.shape[2]
     right_high, right_low = mixed_parts(coefficients_ref, own_ref, other_ref)
-    count = sems.shape[0]
-    step = out_ref.shape[2] // count
+    unit = out_ref.shape[2] // sum(LAST_PARTS)
     copies = []
-    for i in range(count):
-        part = pl.ds(i * step, step)
+    start = 0
+    for i, size in enumerate(LAST_PARTS):
+        part = pl.ds(start, size * unit)
+        start += size * unit
         out = product(high_ref[part, :], low_ref[part, :], right_high, right_low)
         out_ref[0, 0, part] = sum_ref[0, part] + out[:, :cols]
         out_ref[1, 0, part] = sum_ref[1, part] + out[:, cols:]
@@ -589,7 +590,7 @@
         out_shape=jax.ShapeDtypeStruct(shape, F32),
         in_specs=[vmem()] * 6,
         out_specs=any_space(),
-        scratch_shapes=[pltpu.VMEM(shape, F32), pltpu.SemaphoreType.DMA((LAST_CHUNKS,))],
+        scratch_shapes=[pltpu.VMEM(shape, F32), pltpu.SemaphoreType.DMA((len(LAST_PARTS),))],
         compiler_params=params(),
         cost_estimate=cost(),
         name="last",

time: 39.9 us -> 39.9 us (level)
  no operation moved by 1% of the time
where the time goes in v6:
time: 39.9 us; the launch traced here: 39.7 us
  starting transfers between devices  20.2 us (51%)
  Pallas kernels  11.1 us (28%)
  waiting for transfers between devices  8.24 us (21%)
    ppermute x12, starting transfers between devices, swap(): lax.ppermute(value, axis, [(i, i ^ mask) for i in range(lax.axis_size(axi...  20.2 us
    ppermute x12, waiting for transfers between devices, swap(): lax.ppermute(value, axis, [(i, i ^ mask) for i in range(lax.axis_size(axi...  8.24 us
    pallas_call x1, Pallas kernels, first(): pl.pallas_call(functools.partial(first_kernel, groups, piece_rows, col_bi...  4.17 us
    pallas_call x1, Pallas kernels, second_gates(): pl.pallas_call(functools.partial(gates_kernel, sets, piece_rows), out_sha...  2.62 us
    pallas_call x1, Pallas kernels, last(): pl.pallas_call(last_kernel, out_shape=jax.ShapeDtypeStruct(shape, F32), i...  1.89 us
    pallas_call x1, Pallas kernels, middle(): pl.pallas_call(middle_kernel, out_shape=jax.ShapeDtypeStruct((2, parts[0]...  1.13 us
    pallas_call x1, Pallas kernels, second_phases(): pl.pallas_call(functools.partial(phases_kernel, sets, piece_rows, col_bit...  0.89 us
  transfers between devices with their start and end apart: 12, of which 7 were waited for; matrix products, arithmetic and copies ran while one was open for 0% of the time, Pallas kernels for 13%

profile of v6, /device:TPU:0, one launch (start us, length us, event | category | flops | bytes accessed | tf_op | source)
XLA Modules:
  0.0 39.7 jit_solution(12719085038354639839)
XLA Ops:
  0.0 0.0 copy-start.3
  0.0 0.0 copy-start
  0.0 0.0 copy-start.1
  0.0 0.0 copy-start.4
  0.0 0.0 copy-start.2
  0.0 4.2 %first.1 = (f32[8,256]{1,0:T(8,128)S(1)}, f32[2,128,256]{2,1,0:T(8,128)S(1)}, f32[2,192,256]{2,1,0:T(8,128)S(1)}, f32[2,64,256]{2,1,0:T(8,128)S(1)}, f32[2,64,25...) custom-call(f32[2,1,512,256]{3,2,1,0:T(8,128)} %amplitudes_hbm.1, f32[2,2,512,512]{3,2,1,0:T(8,128)} %gates_hbm.2, ...), custom_call_target="tpu_custom_call" | custom-call | flops 1000 | bytes 1000 | tf_op jit(solution)/shard_map/first/pallas_call | solution.py:281
  4.2 3.0 %collective-permute-start.2 = (f32[2,128,256]{2,1,0:T(8,128)S(1)}, f32[2,128,256]{2,1,0:T(8,128)S(1)}, u32[]{:S(2)}, u32[]{:S(2)}) collective-permute-start(f32[2,128,256]{2,1,0:T(8,128)S(1)} %get-tuple-element.34.own_ref), channel_id=1, source_target_pairs={{0,2},{1,3},{2,0},{3,1},{4,6},{5,7},{6,4},{7,5},{8,10},{9,11},{10,... | collective-permute-start | bytes 786440 | tf_op jit(solution)/shard_map/ppermute | solution.py:601
  7.2 0.1 collective-permute-start
  7.3 3.0 %collective-permute-start.5 = (f32[2,64,256]{2,1,0:T(8,128)S(1)}, f32[2,64,256]{2,1,0:T(8,128)S(1)}, u32[]{:S(2)}, u32[]{:S(2)}) collective-permute-start(f32[2,64,256]{2,1,0:T(8,128)S(1)} %get-tuple-element.53), channel_id=1, source_target_pairs={{0,16},{4,20},{8,24},{12,28},{16,0},{20,4},{24,8},{28,12},{1,17},{... | collective-permute-start | bytes 393224 | tf_op jit(solution)/shard_map/ppermute | solution.py:601
  10.3 1.3 %collective-permute-start.6 = (f32[2,64,256]{2,1,0:T(8,128)S(1)}, f32[2,64,256]{2,1,0:T(8,128)S(1)}, u32[]{:S(2)}, u32[]{:S(2)}) collective-permute-start(f32[2,64,256]{2,1,0:T(8,128)S(1)} %get-tuple-element.55), channel_id=1, source_target_pairs={{0,20},{4,16},{8,28},{12,24},{16,4},{20,0},{24,12},{28,8},{1,21},{... | collective-permute-start | bytes 393224 | tf_op jit(solution)/shard_map/ppermute | solution.py:601
  11.6 0.2 collective-permute-start.7
  11.8 0.0 copy-done.3
  11.8 0.0 copy-done
  11.8 0.0 copy-done.1
  11.8 0.0 copy-done.4
  11.9 0.0 copy-done.2
  11.9 0.9 %second_phases.1 = (f32[256,128]{1,0:T(8,128)S(1)}, f32[256,128]{1,0:T(8,128)S(1)}, f32[256,128]{1,0:T(8,128)S(1)}, f32[256,128]{1,0:T(8,128)S(1)}, f32[8,256]{1,0:T(8,128)S(1)}) custom-call(f32[2,17]{1,0:T(2,128)S(1)} %copy-done.1, f32[1,2]{1,0:T(1,128)S(1)} %bitcast.2, s32[17]{0:T(128)S(1)} %copy-done.4, s32[2,17]{1,0:T(2,128)S(1)} %copy-done.2, ...), custom_call_target="tpu_custom_call" | custom-call | flops 1000 | bytes 1000 | tf_op jit(solution)/shard_map/second_phases/pallas_call | solution.py:357
  12.8 1.6 %collective-permute-done.2.other_ref = f32[2,128,256]{2,1,0:T(8,128)S(1)} collective-permute-done((f32[2,128,256]{2,1,0:T(8,128)S(1)}, f32[2,128,256]{2,1,0:T(8,128)S(1)}, u32[]{:S(2)}, u32[]{:S(2)}) %collective-permute-start.2) | collective-permute-done | bytes 262176 | tf_op jit(solution)/shard_map/ppermute | solution.py:601
  14.3 0.1 combine.3
  14.4 5.2 %collective-permute-start.3 = (f32[2,64,256]{2,1,0:T(8,128)S(1)}, f32[2,64,256]{2,1,0:T(8,128)S(1)}, u32[]{:S(2)}, u32[]{:S(2)}) collective-permute-start(f32[2,64,256]{2,1,0:T(8,128)S(1)} %get-tuple-element.44), channel_id=1, source_target_pairs={{0,28},{4,24},{8,20},{12,16},{16,12},{20,8},{24,4},{28,0},{1,29},{... | collective-permute-start | bytes 393224 | tf_op jit(solution)/shard_map/ppermute | solution.py:601
  19.6 2.3 %collective-permute-done.other_ref = f32[2,192,256]{2,1,0:T(8,128)S(1)} collective-permute-done((f32[2,192,256]{2,1,0:T(8,128)S(1)}, f32[2,192,256]{2,1,0:T(8,128)S(1)}, u32[]{:S(2)}, u32[]{:S(2)}) %collective-permute-start) | collective-permute-done | bytes 393248 | tf_op jit(solution)/shard_map/ppermute | solution.py:601
  21.9 0.1 combine.2
  22.0 2.8 %collective-permute-start.4 = (f32[2,64,256]{2,1,0:T(8,128)S(1)}, f32[2,64,256]{2,1,0:T(8,128)S(1)}, u32[]{:S(2)}, u32[]{:S(2)}) collective-permute-start(f32[2,64,256]{2,1,0:T(8,128)S(1)} %get-tuple-element.46), channel_id=1, source_target_pairs={{0,12},{4,8},{8,4},{12,0},{16,28},{20,24},{24,20},{28,16},{1,13},{... | collective-permute-start | bytes 393224 | tf_op jit(solution)/shard_map/ppermute | solution.py:601
  24.9 0.0 collective-permute-done.5.refs_0_
  24.9 0.5 %collective-permute-start.1 = (f32[2,64,256]{2,1,0:T(8,128)S(1)}, f32[2,64,256]{2,1,0:T(8,128)S(1)}, u32[]{:S(2)}, u32[]{:S(2)}) collective-permute-start(f32[2,64,256]{2,1,0:T(8,128)S(1)} %get-tuple-element.41), channel_id=1, source_target_pairs={{0,8},{4,12},{8,0},{12,4},{16,24},{20,28},{24,16},{28,20},{1,9},{5... | collective-permute-start | bytes 393224 | tf_op jit(solution)/shard_map/ppermute | solution.py:601
  25.3 1.3 %collective-permute-done.6.refs_1_ = f32[2,64,256]{2,1,0:T(8,128)S(1)} collective-permute-done((f32[2,64,256]{2,1,0:T(8,128)S(1)}, f32[2,64,256]{2,1,0:T(8,128)S(1)}, u32[]{:S(2)}, u32[]{:S(2)}) %collective-permute-start.6) | collective-permute-done | bytes 131104 | tf_op jit(solution)/shard_map/ppermute | solution.py:601
  26.7 0.0 collective-permute-done.7.refs_2_
  26.7 1.6 %collective-permute-start.8 = (f32[2,192,256]{2,1,0:T(8,128)S(1)}, f32[2,192,256]{2,1,0:T(8,128)S(1)}, u32[]{:S(2)}, u32[]{:S(2)}) collective-permute-start(f32[2,192,256]{2,1,0:T(8,128)S(1)} %joined.3.own_ref), channel_id=1, source_target_pairs={{0,2},{1,3},{2,0},{3,1},{4,6},{5,7},{6,4},{7,5},{8,10},{9,11},{10,... | collective-permute-start | bytes 1179656 | tf_op jit(solution)/shard_map/ppermute | solution.py:601
  28.3 2.4 %collective-permute-start.9 = (f32[2,64,256]{2,1,0:T(8,128)S(1)}, f32[2,64,256]{2,1,0:T(8,128)S(1)}, u32[]{:S(2)}, u32[]{:S(2)}) collective-permute-start(f32[2,64,256]{2,1,0:T(8,128)S(1)} %get-tuple-element.61), channel_id=1, source_target_pairs={{0,24},{4,28},{8,16},{12,20},{16,8},{20,12},{24,0},{28,4},{1,25},{... | collective-permute-start | bytes 393224 | tf_op jit(solution)/shard_map/ppermute | solution.py:601
  30.7 0.0 collective-permute-done.3.refs_0_
  30.7 0.0 collective-permute-done.4.refs_2_
  30.7 0.2 collective-permute-done.1.refs_1_
  30.9 0.1 turned_pieces.1.own_ref
  31.0 0.1 collective-permute-start.11
  31.0 2.6 %second_gates.1 = (bf16[512,512]{1,0:T(8,128)(2,1)S(1)}, bf16[512,512]{1,0:T(8,128)(2,1)S(1)}, bf16[512,512]{1,0:T(8,128)(2,1)S(1)}, bf16[512,512]{1,0:T(8,128)(2,1)S(1)}) custom-call(f32[2,2,512,512]{3,2,1,0:T(8,128)} %gates_hbm.2), custom_call_target="tpu_custom_call" | custom-call | flops 1000 | bytes 1000 | tf_op jit(solution)/shard_map/second_gates/pallas_call | solution.py:404
  33.7 1.9 %collective-permute-done.8.other_ref = f32[2,192,256]{2,1,0:T(8,128)S(1)} collective-permute-done((f32[2,192,256]{2,1,0:T(8,128)S(1)}, f32[2,192,256]{2,1,0:T(8,128)S(1)}, u32[]{:S(2)}, u32[]{:S(2)}) %collective-permute-start.8) | collective-permute-done | bytes 393248 | tf_op jit(solution)/shard_map/ppermute | solution.py:601
  35.6 0.1 collective-permute-done.9.last_ref
  35.7 0.2 turned.1.own_ref
  35.9 0.1 collective-permute-start.10
  35.9 0.0 collective-permute-done.11.other_ref
  36.0 1.1 %middle.1.sum_ref = f32[2,512,256]{2,1,0:T(8,128)S(1)} custom-call(bf16[512,512]{1,0:T(8,128)(2,1)S(1)} %get-tuple-element.59.high_ref, bf16[512,512]{1,0:T(8,128)(2,1)S(1)} %get-tuple-element.62.low_ref, f32[8,256]{1,0:T(8,128)S(1)} %get-tuple-element.42.coefficients_ref, f32[2,256,256]{2,1,0:T(8,128)S(1)} %turned_pieces.1.own_ref, ...), custom_call_target="tpu_custom_call" | custom-call | flops 1000 | bytes 1000 | tf_op jit(solution)/shard_map/middle/pallas_call | solution.py:522
  37.1 0.8 %collective-permute-done.10.other_ref = f32[2,256,256]{2,1,0:T(8,128)S(1)} collective-permute-done((f32[2,256,256]{2,1,0:T(8,128)S(1)}, f32[2,256,256]{2,1,0:T(8,128)S(1)}, u32[]{:S(2)}, u32[]{:S(2)}) %collective-permute-start.10) | collective-permute-done | bytes 524320 | tf_op jit(solution)/shard_map/ppermute | solution.py:601
  37.8 1.9 %last.1 = f32[2,1,512,256]{3,2,1,0:T(8,128)} custom-call(bf16[512,512]{1,0:T(8,128)(2,1)S(1)} %get-tuple-element.49.high_ref, bf16[512,512]{1,0:T(8,128)(2,1)S(1)} %get-tuple-element.50.low_ref, f32[8,256]{1,0:T(8,128)S(1)} %get-tuple-element.42.coefficients_ref, f32[2,256,256]{2,1,0:T(8,128)S(1)} %turned.1.own_ref, ...), custom_call_target="tpu_custom_call" | custom-call | flops 1000 | bytes 1000 | tf_op jit(solution)/shard_map/last/pallas_call | solution.py:588
  (2 shorter events, 0.0 us)
Async XLA Ops:
  0.0 11.8 %copy-start.3 = (f32[2,1]{0,1:T(1,128)S(1)}, f32[2,1]{0,1:T(1,128)}, u32[]{:S(2)}) copy-start(f32[2,1]{0,1:T(1,128)} %param.11) | copy-start | bytes 28
  0.0 11.8 %copy-start = (f32[2,2,2,2]{3,2,1,0:T(2,128)S(1)}, f32[2,2,2,2]{3,2,1,0:T(2,128)}, u32[]{:S(2)}) copy-start(f32[2,2,2,2]{3,2,1,0:T(2,128)} %pair_ref.1) | copy-start | bytes 196
  0.0 11.8 %copy-start.1 = (f32[2,17]{1,0:T(2,128)S(1)}, f32[2,17]{1,0:T(2,128)}, u32[]{:S(2)}) copy-start(f32[2,17]{1,0:T(2,128)} %phases_ref) | copy-start | bytes 412
  0.0 11.8 %copy-start.4 = (s32[17]{0:T(128)S(1)}, s32[17]{0:T(128)}, u32[]{:S(2)}) copy-start(s32[17]{0:T(128)} %bits_ref.1) | copy-start | bytes 208
  0.0 11.8 %copy-start.2 = (s32[2,17]{1,0:T(2,128)S(1)}, s32[2,17]{1,0:T(2,128)}, u32[]{:S(2)}) copy-start(s32[2,17]{1,0:T(2,128)} %coupled_ref.1) | copy-start | bytes 412
  4.2 10.1 %collective-permute-start.2 = (f32[2,128,256]{2,1,0:T(8,128)S(1)}, f32[2,128,256]{2,1,0:T(8,128)S(1)}, u32[]{:S(2)}, u32[]{:S(2)}) collective-permute-start(f32[2,128,256]{2,1,0:T(8,128)S(1)} %get-tuple-element.34.own_ref), channel_id=1, source_target_pairs={{0,2},{1,3},{2,0},{3,1},{4,6},{5,7},{6,4},{7,5},{8,10},{9,11},{10,... | collective-permute-start | bytes 786440 | tf_op jit(solution)/shard_map/ppermute | solution.py:601
  7.2 14.7 %collective-permute-start = (f32[2,192,256]{2,1,0:T(8,128)S(1)}, f32[2,192,256]{2,1,0:T(8,128)S(1)}, u32[]{:S(2)}, u32[]{:S(2)}) collective-permute-start(f32[2,192,256]{2,1,0:T(8,128)S(1)} %get-tuple-element.39.own_ref), channel_id=1, source_target_pairs={{0,2},{1,3},{2,0},{3,1},{4,6},{5,7},{6,4},{7,5},{8,10},{9,11},{10,... | collective-permute-start | bytes 1179656 | tf_op jit(solution)/shard_map/ppermute | solution.py:601
  7.3 17.6 %collective-permute-start.5 = (f32[2,64,256]{2,1,0:T(8,128)S(1)}, f32[2,64,256]{2,1,0:T(8,128)S(1)}, u32[]{:S(2)}, u32[]{:S(2)}) collective-permute-start(f32[2,64,256]{2,1,0:T(8,128)S(1)} %get-tuple-element.53), channel_id=1, source_target_pairs={{0,16},{4,20},{8,24},{12,28},{16,0},{20,4},{24,8},{28,12},{1,17},{... | collective-permute-start | bytes 393224 | tf_op jit(solution)/shard_map/ppermute | solution.py:601
  10.3 16.4 %collective-permute-start.6 = (f32[2,64,256]{2,1,0:T(8,128)S(1)}, f32[2,64,256]{2,1,0:T(8,128)S(1)}, u32[]{:S(2)}, u32[]{:S(2)}) collective-permute-start(f32[2,64,256]{2,1,0:T(8,128)S(1)} %get-tuple-element.55), channel_id=1, source_target_pairs={{0,20},{4,16},{8,28},{12,24},{16,4},{20,0},{24,12},{28,8},{1,21},{... | collective-permute-start | bytes 393224 | tf_op jit(solution)/shard_map/ppermute | solution.py:601
  11.6 15.1 %collective-permute-start.7 = (f32[2,64,256]{2,1,0:T(8,128)S(1)}, f32[2,64,256]{2,1,0:T(8,128)S(1)}, u32[]{:S(2)}, u32[]{:S(2)}) collective-permute-start(f32[2,64,256]{2,1,0:T(8,128)S(1)} %get-tuple-element.57), channel_id=1, source_target_pairs={{0,4},{4,0},{8,12},{12,8},{16,20},{20,16},{24,28},{28,24},{1,5},{5... | collective-permute-start | bytes 393224 | tf_op jit(solution)/shard_map/ppermute | solution.py:601
  14.4 16.3 %collective-permute-start.3 = (f32[2,64,256]{2,1,0:T(8,128)S(1)}, f32[2,64,256]{2,1,0:T(8,128)S(1)}, u32[]{:S(2)}, u32[]{:S(2)}) collective-permute-start(f32[2,64,256]{2,1,0:T(8,128)S(1)} %get-tuple-element.44), channel_id=1, source_target_pairs={{0,28},{4,24},{8,20},{12,16},{16,12},{20,8},{24,4},{28,0},{1,29},{... | collective-permute-start | bytes 393224 | tf_op jit(solution)/shard_map/ppermute | solution.py:601
  22.0 8.7 %collective-permute-start.4 = (f32[2,64,256]{2,1,0:T(8,128)S(1)}, f32[2,64,256]{2,1,0:T(8,128)S(1)}, u32[]{:S(2)}, u32[]{:S(2)}) collective-permute-start(f32[2,64,256]{2,1,0:T(8,128)S(1)} %get-tuple-element.46), channel_id=1, source_target_pairs={{0,12},{4,8},{8,4},{12,0},{16,28},{20,24},{24,20},{28,16},{1,13},{... | collective-permute-start | bytes 393224 | tf_op jit(solution)/shard_map/ppermute | solution.py:601
  24.9 6.0 %collective-permute-start.1 = (f32[2,64,256]{2,1,0:T(8,128)S(1)}, f32[2,64,256]{2,1,0:T(8,128)S(1)}, u32[]{:S(2)}, u32[]{:S(2)}) collective-permute-start(f32[2,64,256]{2,1,0:T(8,128)S(1)} %get-tuple-element.41), channel_id=1, source_target_pairs={{0,8},{4,12},{8,0},{12,4},{16,24},{20,28},{24,16},{28,20},{1,9},{5... | collective-permute-start | bytes 393224 | tf_op jit(solution)/shard_map/ppermute | solution.py:601
  26.7 8.8 %collective-permute-start.8 = (f32[2,192,256]{2,1,0:T(8,128)S(1)}, f32[2,192,256]{2,1,0:T(8,128)S(1)}, u32[]{:S(2)}, u32[]{:S(2)}) collective-permute-start(f32[2,192,256]{2,1,0:T(8,128)S(1)} %joined.3.own_ref), channel_id=1, source_target_pairs={{0,2},{1,3},{2,0},{3,1},{4,6},{5,7},{6,4},{7,5},{8,10},{9,11},{10,... | collective-permute-start | bytes 1179656 | tf_op jit(solution)/shard_map/ppermute | solution.py:601
  28.3 7.4 %collective-permute-start.9 = (f32[2,64,256]{2,1,0:T(8,128)S(1)}, f32[2,64,256]{2,1,0:T(8,128)S(1)}, u32[]{:S(2)}, u32[]{:S(2)}) collective-permute-start(f32[2,64,256]{2,1,0:T(8,128)S(1)} %get-tuple-element.61), channel_id=1, source_target_pairs={{0,24},{4,28},{8,16},{12,20},{16,8},{20,12},{24,0},{28,4},{1,25},{... | collective-permute-start | bytes 393224 | tf_op jit(solution)/shard_map/ppermute | solution.py:601
  31.0 5.0 %collective-permute-start.11 = (f32[2,256,256]{2,1,0:T(8,128)S(1)}, f32[2,256,256]{2,1,0:T(8,128)S(1)}, u32[]{:S(2)}, u32[]{:S(2)}) collective-permute-start(f32[2,256,256]{2,1,0:T(8,128)S(1)} %turned_pieces.1.own_ref), channel_id=1, source_target_pairs={{0,1},{1,0},{2,3},{3,2},{4,5},{5,4},{6,7},{7,6},{8,9},{9,8},{10,11... | collective-permute-start | bytes 1572872 | tf_op jit(solution)/shard_map/ppermute | solution.py:601
  35.9 2.0 %collective-permute-start.10 = (f32[2,256,256]{2,1,0:T(8,128)S(1)}, f32[2,256,256]{2,1,0:T(8,128)S(1)}, u32[]{:S(2)}, u32[]{:S(2)}) collective-permute-start(f32[2,256,256]{2,1,0:T(8,128)S(1)} %turned.1.own_ref), channel_id=1, source_target_pairs={{0,1},{1,0},{2,3},{3,2},{4,5},{5,4},{6,7},{7,6},{8,9},{9,8},{10,11... | collective-permute-start | bytes 1572872 | tf_op jit(solution)/shard_map/ppermute | solution.py:601

commit v7 on v6

--- a/solution.py
+++ b/solution.py
@@ -105,6 +105,12 @@
     real_high, real_low = split(real)
     imag_high, imag_low = split(imag)
     return signed_block(real_high, imag_high), signed_block(real_low, imag_low)
+
+
+def wide_product(left_high, left_low, right_high, right_low):
+    left = jnp.concatenate([left_high, left_high, left_low], axis=1)
+    right = jnp.concatenate([right_high, right_low, right_high], axis=0)
+    return dot(left, right)
 
 
 def product(left_high, left_low, right_high, right_low):
@@ -513,7 +519,7 @@
 def middle_kernel(high_ref, low_ref, coefficients_ref, own_ref, other_ref, out_ref):
     cols = out_ref.shape[2]
     right_high, right_low = mixed_parts(coefficients_ref, own_ref, other_ref)
-    out = product(high_ref[...], low_ref[...], right_high, right_low)
+    out = wide_product(high_ref[...], low_ref[...], right_high, right_low)
     out_ref[0] = out[:, :cols]
     out_ref[1] = out[:, cols:]
 
@@ -569,7 +575,7 @@
     for i, size in enumerate(LAST_PARTS):
         part = pl.ds(start, size * unit)
         start += size * unit
-        out = product(high_ref[part, :], low_ref[part, :], right_high, right_low)
+        out = wide_product(high_ref[part, :], low_ref[part, :], right_high, right_low)
         out_ref[0, 0, part] = sum_ref[0, part] + out[:, :cols]
         out_ref[1, 0, part] = sum_ref[1, part] + out[:, cols:]
         copies.append(

time: 39.9 us -> 39.8 us (level)
  no operation moved by 1% of the time
where the time goes in v7:
time: 39.8 us; the launch traced here: 39.7 us
  starting transfers between devices  20.2 us (51%)
  Pallas kernels  11 us (28%)
  waiting for transfers between devices  8.29 us (21%)
    ppermute x12, starting transfers between devices, swap(): lax.ppermute(value, axis, [(i, i ^ mask) for i in range(lax.axis_size(axi...  20.2 us
    ppermute x12, waiting for transfers between devices, swap(): lax.ppermute(value, axis, [(i, i ^ mask) for i in range(lax.axis_size(axi...  8.29 us
    pallas_call x1, Pallas kernels, first(): pl.pallas_call(functools.partial(first_kernel, groups, piece_rows, col_bi...  4.17 us
    pallas_call x1, Pallas kernels, second_gates(): pl.pallas_call(functools.partial(gates_kernel, sets, piece_rows), out_sha...  2.62 us
    pallas_call x1, Pallas kernels, last(): pl.pallas_call(last_kernel, out_shape=jax.ShapeDtypeStruct(shape, F32), i...  1.85 us
    pallas_call x1, Pallas kernels, middle(): pl.pallas_call(middle_kernel, out_shape=jax.ShapeDtypeStruct((2, parts[0]...  1.08 us
    pallas_call x1, Pallas kernels, second_phases(): pl.pallas_call(functools.partial(phases_kernel, sets, piece_rows, col_bit...  0.89 us
  transfers between devices with their start and end apart: 12, of which 7 were waited for; matrix products, arithmetic and copies ran while one was open for 0% of the time, Pallas kernels for 13%

profile of v7, /device:TPU:0, one launch (start us, length us, event | category | flops | bytes accessed | tf_op | source)
XLA Modules:
  0.0 39.7 jit_solution(17915795662892641902)
XLA Ops:
  0.0 0.0 copy-start.3
  0.0 0.0 copy-start
  0.0 0.0 copy-start.1
  0.0 0.0 copy-start.4
  0.0 0.0 copy-start.2
  0.0 4.2 %first.1 = (f32[8,256]{1,0:T(8,128)S(1)}, f32[2,128,256]{2,1,0:T(8,128)S(1)}, f32[2,192,256]{2,1,0:T(8,128)S(1)}, f32[2,64,256]{2,1,0:T(8,128)S(1)}, f32[2,64,25...) custom-call(f32[2,1,512,256]{3,2,1,0:T(8,128)} %amplitudes_hbm.1, f32[2,2,512,512]{3,2,1,0:T(8,128)} %gates_hbm.2, ...), custom_call_target="tpu_custom_call" | custom-call | flops 1000 | bytes 1000 | tf_op jit(solution)/shard_map/first/pallas_call | solution.py:287
  4.2 3.0 %collective-permute-start.2 = (f32[2,128,256]{2,1,0:T(8,128)S(1)}, f32[2,128,256]{2,1,0:T(8,128)S(1)}, u32[]{:S(2)}, u32[]{:S(2)}) collective-permute-start(f32[2,128,256]{2,1,0:T(8,128)S(1)} %get-tuple-element.34.own_ref), channel_id=1, source_target_pairs={{0,2},{1,3},{2,0},{3,1},{4,6},{5,7},{6,4},{7,5},{8,10},{9,11},{10,... | collective-permute-start | bytes 786440 | tf_op jit(solution)/shard_map/ppermute | solution.py:607
  7.2 0.1 collective-permute-start
  7.3 3.0 %collective-permute-start.5 = (f32[2,64,256]{2,1,0:T(8,128)S(1)}, f32[2,64,256]{2,1,0:T(8,128)S(1)}, u32[]{:S(2)}, u32[]{:S(2)}) collective-permute-start(f32[2,64,256]{2,1,0:T(8,128)S(1)} %get-tuple-element.53), channel_id=1, source_target_pairs={{0,16},{4,20},{8,24},{12,28},{16,0},{20,4},{24,8},{28,12},{1,17},{... | collective-permute-start | bytes 393224 | tf_op jit(solution)/shard_map/ppermute | solution.py:607
  10.3 1.3 %collective-permute-start.6 = (f32[2,64,256]{2,1,0:T(8,128)S(1)}, f32[2,64,256]{2,1,0:T(8,128)S(1)}, u32[]{:S(2)}, u32[]{:S(2)}) collective-permute-start(f32[2,64,256]{2,1,0:T(8,128)S(1)} %get-tuple-element.55), channel_id=1, source_target_pairs={{0,20},{4,16},{8,28},{12,24},{16,4},{20,0},{24,12},{28,8},{1,21},{... | collective-permute-start | bytes 393224 | tf_op jit(solution)/shard_map/ppermute | solution.py:607
  11.6 0.2 collective-permute-start.7
  11.8 0.0 copy-done.3
  11.8 0.0 copy-done
  11.8 0.0 copy-done.1
  11.8 0.0 copy-done.4
  11.9 0.0 copy-done.2
  11.9 0.9 %second_phases.1 = (f32[256,128]{1,0:T(8,128)S(1)}, f32[256,128]{1,0:T(8,128)S(1)}, f32[256,128]{1,0:T(8,128)S(1)}, f32[256,128]{1,0:T(8,128)S(1)}, f32[8,256]{1,0:T(8,128)S(1)}) custom-call(f32[2,17]{1,0:T(2,128)S(1)} %copy-done.1, f32[1,2]{1,0:T(1,128)S(1)} %bitcast.2, s32[17]{0:T(128)S(1)} %copy-done.4, s32[2,17]{1,0:T(2,128)S(1)} %copy-done.2, ...), custom_call_target="tpu_custom_call" | custom-call | flops 1000 | bytes 1000 | tf_op jit(solution)/shard_map/second_phases/pallas_call | solution.py:363
  12.8 1.6 %collective-permute-done.2.other_ref = f32[2,128,256]{2,1,0:T(8,128)S(1)} collective-permute-done((f32[2,128,256]{2,1,0:T(8,128)S(1)}, f32[2,128,256]{2,1,0:T(8,128)S(1)}, u32[]{:S(2)}, u32[]{:S(2)}) %collective-permute-start.2) | collective-permute-done | bytes 262176 | tf_op jit(solution)/shard_map/ppermute | solution.py:607
  14.3 0.1 combine.3
  14.4 5.2 %collective-permute-start.3 = (f32[2,64,256]{2,1,0:T(8,128)S(1)}, f32[2,64,256]{2,1,0:T(8,128)S(1)}, u32[]{:S(2)}, u32[]{:S(2)}) collective-permute-start(f32[2,64,256]{2,1,0:T(8,128)S(1)} %get-tuple-element.44), channel_id=1, source_target_pairs={{0,28},{4,24},{8,20},{12,16},{16,12},{20,8},{24,4},{28,0},{1,29},{... | collective-permute-start | bytes 393224 | tf_op jit(solution)/shard_map/ppermute | solution.py:607
  19.6 2.3 %collective-permute-done.other_ref = f32[2,192,256]{2,1,0:T(8,128)S(1)} collective-permute-done((f32[2,192,256]{2,1,0:T(8,128)S(1)}, f32[2,192,256]{2,1,0:T(8,128)S(1)}, u32[]{:S(2)}, u32[]{:S(2)}) %collective-permute-start) | collective-permute-done | bytes 393248 | tf_op jit(solution)/shard_map/ppermute | solution.py:607
  21.9 0.1 combine.2
  22.0 2.8 %collective-permute-start.4 = (f32[2,64,256]{2,1,0:T(8,128)S(1)}, f32[2,64,256]{2,1,0:T(8,128)S(1)}, u32[]{:S(2)}, u32[]{:S(2)}) collective-permute-start(f32[2,64,256]{2,1,0:T(8,128)S(1)} %get-tuple-element.46), channel_id=1, source_target_pairs={{0,12},{4,8},{8,4},{12,0},{16,28},{20,24},{24,20},{28,16},{1,13},{... | collective-permute-start | bytes 393224 | tf_op jit(solution)/shard_map/ppermute | solution.py:607
  24.9 0.0 collective-permute-done.5.refs_0_
  24.9 0.5 %collective-permute-start.1 = (f32[2,64,256]{2,1,0:T(8,128)S(1)}, f32[2,64,256]{2,1,0:T(8,128)S(1)}, u32[]{:S(2)}, u32[]{:S(2)}) collective-permute-start(f32[2,64,256]{2,1,0:T(8,128)S(1)} %get-tuple-element.41), channel_id=1, source_target_pairs={{0,8},{4,12},{8,0},{12,4},{16,24},{20,28},{24,16},{28,20},{1,9},{5... | collective-permute-start | bytes 393224 | tf_op jit(solution)/shard_map/ppermute | solution.py:607
  25.3 1.3 %collective-permute-done.6.refs_1_ = f32[2,64,256]{2,1,0:T(8,128)S(1)} collective-permute-done((f32[2,64,256]{2,1,0:T(8,128)S(1)}, f32[2,64,256]{2,1,0:T(8,128)S(1)}, u32[]{:S(2)}, u32[]{:S(2)}) %collective-permute-start.6) | collective-permute-done | bytes 131104 | tf_op jit(solution)/shard_map/ppermute | solution.py:607
  26.7 0.0 collective-permute-done.7.refs_2_
  26.7 1.6 %collective-permute-start.8 = (f32[2,192,256]{2,1,0:T(8,128)S(1)}, f32[2,192,256]{2,1,0:T(8,128)S(1)}, u32[]{:S(2)}, u32[]{:S(2)}) collective-permute-start(f32[2,192,256]{2,1,0:T(8,128)S(1)} %joined.3.own_ref), channel_id=1, source_target_pairs={{0,2},{1,3},{2,0},{3,1},{4,6},{5,7},{6,4},{7,5},{8,10},{9,11},{10,... | collective-permute-start | bytes 1179656 | tf_op jit(solution)/shard_map/ppermute | solution.py:607
  28.3 2.4 %collective-permute-start.9 = (f32[2,64,256]{2,1,0:T(8,128)S(1)}, f32[2,64,256]{2,1,0:T(8,128)S(1)}, u32[]{:S(2)}, u32[]{:S(2)}) collective-permute-start(f32[2,64,256]{2,1,0:T(8,128)S(1)} %get-tuple-element.61), channel_id=1, source_target_pairs={{0,24},{4,28},{8,16},{12,20},{16,8},{20,12},{24,0},{28,4},{1,25},{... | collective-permute-start | bytes 393224 | tf_op jit(solution)/shard_map/ppermute | solution.py:607
  30.7 0.0 collective-permute-done.3.refs_0_
  30.7 0.0 collective-permute-done.4.refs_2_
  30.7 0.2 collective-permute-done.1.refs_1_
  30.9 0.1 turned_pieces.1.own_ref
  31.0 0.1 collective-permute-start.11
  31.0 2.6 %second_gates.1 = (bf16[512,512]{1,0:T(8,128)(2,1)S(1)}, bf16[512,512]{1,0:T(8,128)(2,1)S(1)}, bf16[512,512]{1,0:T(8,128)(2,1)S(1)}, bf16[512,512]{1,0:T(8,128)(2,1)S(1)}) custom-call(f32[2,2,512,512]{3,2,1,0:T(8,128)} %gates_hbm.2), custom_call_target="tpu_custom_call" | custom-call | flops 1000 | bytes 1000 | tf_op jit(solution)/shard_map/second_gates/pallas_call | solution.py:410
  33.7 1.9 %collective-permute-done.8.other_ref = f32[2,192,256]{2,1,0:T(8,128)S(1)} collective-permute-done((f32[2,192,256]{2,1,0:T(8,128)S(1)}, f32[2,192,256]{2,1,0:T(8,128)S(1)}, u32[]{:S(2)}, u32[]{:S(2)}) %collective-permute-start.8) | collective-permute-done | bytes 393248 | tf_op jit(solution)/shard_map/ppermute | solution.py:607
  35.6 0.1 collective-permute-done.9.last_ref
  35.7 0.2 turned.1.own_ref
  35.9 0.1 collective-permute-start.10
  35.9 0.0 collective-permute-done.11.other_ref
  36.0 1.1 %middle.1.sum_ref = f32[2,512,256]{2,1,0:T(8,128)S(1)} custom-call(bf16[512,512]{1,0:T(8,128)(2,1)S(1)} %get-tuple-element.59.high_ref, bf16[512,512]{1,0:T(8,128)(2,1)S(1)} %get-tuple-element.62.low_ref, f32[8,256]{1,0:T(8,128)S(1)} %get-tuple-element.42.coefficients_ref, f32[2,256,256]{2,1,0:T(8,128)S(1)} %turned_pieces.1.own_ref, ...), custom_call_target="tpu_custom_call" | custom-call | flops 1000 | bytes 1000 | tf_op jit(solution)/shard_map/middle/pallas_call | solution.py:528
  37.0 0.8 %collective-permute-done.10.other_ref = f32[2,256,256]{2,1,0:T(8,128)S(1)} collective-permute-done((f32[2,256,256]{2,1,0:T(8,128)S(1)}, f32[2,256,256]{2,1,0:T(8,128)S(1)}, u32[]{:S(2)}, u32[]{:S(2)}) %collective-permute-start.10) | collective-permute-done | bytes 524320 | tf_op jit(solution)/shard_map/ppermute | solution.py:607
  37.8 1.8 %last.1 = f32[2,1,512,256]{3,2,1,0:T(8,128)} custom-call(bf16[512,512]{1,0:T(8,128)(2,1)S(1)} %get-tuple-element.49.high_ref, bf16[512,512]{1,0:T(8,128)(2,1)S(1)} %get-tuple-element.50.low_ref, f32[8,256]{1,0:T(8,128)S(1)} %get-tuple-element.42.coefficients_ref, f32[2,256,256]{2,1,0:T(8,128)S(1)} %turned.1.own_ref, ...), custom_call_target="tpu_custom_call" | custom-call | flops 1000 | bytes 1000 | tf_op jit(solution)/shard_map/last/pallas_call | solution.py:594
  (2 shorter events, 0.0 us)
Async XLA Ops:
  0.0 11.8 %copy-start.3 = (f32[2,1]{0,1:T(1,128)S(1)}, f32[2,1]{0,1:T(1,128)}, u32[]{:S(2)}) copy-start(f32[2,1]{0,1:T(1,128)} %param.11) | copy-start | bytes 28
  0.0 11.8 %copy-start = (f32[2,2,2,2]{3,2,1,0:T(2,128)S(1)}, f32[2,2,2,2]{3,2,1,0:T(2,128)}, u32[]{:S(2)}) copy-start(f32[2,2,2,2]{3,2,1,0:T(2,128)} %pair_ref.1) | copy-start | bytes 196
  0.0 11.8 %copy-start.1 = (f32[2,17]{1,0:T(2,128)S(1)}, f32[2,17]{1,0:T(2,128)}, u32[]{:S(2)}) copy-start(f32[2,17]{1,0:T(2,128)} %phases_ref) | copy-start | bytes 412
  0.0 11.8 %copy-start.4 = (s32[17]{0:T(128)S(1)}, s32[17]{0:T(128)}, u32[]{:S(2)}) copy-start(s32[17]{0:T(128)} %bits_ref.1) | copy-start | bytes 208
  0.0 11.8 %copy-start.2 = (s32[2,17]{1,0:T(2,128)S(1)}, s32[2,17]{1,0:T(2,128)}, u32[]{:S(2)}) copy-start(s32[2,17]{1,0:T(2,128)} %coupled_ref.1) | copy-start | bytes 412
  4.2 10.1 %collective-permute-start.2 = (f32[2,128,256]{2,1,0:T(8,128)S(1)}, f32[2,128,256]{2,1,0:T(8,128)S(1)}, u32[]{:S(2)}, u32[]{:S(2)}) collective-permute-start(f32[2,128,256]{2,1,0:T(8,128)S(1)} %get-tuple-element.34.own_ref), channel_id=1, source_target_pairs={{0,2},{1,3},{2,0},{3,1},{4,6},{5,7},{6,4},{7,5},{8,10},{9,11},{10,... | collective-permute-start | bytes 786440 | tf_op jit(solution)/shard_map/ppermute | solution.py:607
  7.2 14.7 %collective-permute-start = (f32[2,192,256]{2,1,0:T(8,128)S(1)}, f32[2,192,256]{2,1,0:T(8,128)S(1)}, u32[]{:S(2)}, u32[]{:S(2)}) collective-permute-start(f32[2,192,256]{2,1,0:T(8,128)S(1)} %get-tuple-element.39.own_ref), channel_id=1, source_target_pairs={{0,2},{1,3},{2,0},{3,1},{4,6},{5,7},{6,4},{7,5},{8,10},{9,11},{10,... | collective-permute-start | bytes 1179656 | tf_op jit(solution)/shard_map/ppermute | solution.py:607
  7.3 17.6 %collective-permute-start.5 = (f32[2,64,256]{2,1,0:T(8,128)S(1)}, f32[2,64,256]{2,1,0:T(8,128)S(1)}, u32[]{:S(2)}, u32[]{:S(2)}) collective-permute-start(f32[2,64,256]{2,1,0:T(8,128)S(1)} %get-tuple-element.53), channel_id=1, source_target_pairs={{0,16},{4,20},{8,24},{12,28},{16,0},{20,4},{24,8},{28,12},{1,17},{... | collective-permute-start | bytes 393224 | tf_op jit(solution)/shard_map/ppermute | solution.py:607
  10.3 16.4 %collective-permute-start.6 = (f32[2,64,256]{2,1,0:T(8,128)S(1)}, f32[2,64,256]{2,1,0:T(8,128)S(1)}, u32[]{:S(2)}, u32[]{:S(2)}) collective-permute-start(f32[2,64,256]{2,1,0:T(8,128)S(1)} %get-tuple-element.55), channel_id=1, source_target_pairs={{0,20},{4,16},{8,28},{12,24},{16,4},{20,0},{24,12},{28,8},{1,21},{... | collective-permute-start | bytes 393224 | tf_op jit(solution)/shard_map/ppermute | solution.py:607
  11.6 15.1 %collective-permute-start.7 = (f32[2,64,256]{2,1,0:T(8,128)S(1)}, f32[2,64,256]{2,1,0:T(8,128)S(1)}, u32[]{:S(2)}, u32[]{:S(2)}) collective-permute-start(f32[2,64,256]{2,1,0:T(8,128)S(1)} %get-tuple-element.57), channel_id=1, source_target_pairs={{0,4},{4,0},{8,12},{12,8},{16,20},{20,16},{24,28},{28,24},{1,5},{5... | collective-permute-start | bytes 393224 | tf_op jit(solution)/shard_map/ppermute | solution.py:607
  14.4 16.3 %collective-permute-start.3 = (f32[2,64,256]{2,1,0:T(8,128)S(1)}, f32[2,64,256]{2,1,0:T(8,128)S(1)}, u32[]{:S(2)}, u32[]{:S(2)}) collective-permute-start(f32[2,64,256]{2,1,0:T(8,128)S(1)} %get-tuple-element.44), channel_id=1, source_target_pairs={{0,28},{4,24},{8,20},{12,16},{16,12},{20,8},{24,4},{28,0},{1,29},{... | collective-permute-start | bytes 393224 | tf_op jit(solution)/shard_map/ppermute | solution.py:607
  22.0 8.7 %collective-permute-start.4 = (f32[2,64,256]{2,1,0:T(8,128)S(1)}, f32[2,64,256]{2,1,0:T(8,128)S(1)}, u32[]{:S(2)}, u32[]{:S(2)}) collective-permute-start(f32[2,64,256]{2,1,0:T(8,128)S(1)} %get-tuple-element.46), channel_id=1, source_target_pairs={{0,12},{4,8},{8,4},{12,0},{16,28},{20,24},{24,20},{28,16},{1,13},{... | collective-permute-start | bytes 393224 | tf_op jit(solution)/shard_map/ppermute | solution.py:607
  24.9 6.0 %collective-permute-start.1 = (f32[2,64,256]{2,1,0:T(8,128)S(1)}, f32[2,64,256]{2,1,0:T(8,128)S(1)}, u32[]{:S(2)}, u32[]{:S(2)}) collective-permute-start(f32[2,64,256]{2,1,0:T(8,128)S(1)} %get-tuple-element.41), channel_id=1, source_target_pairs={{0,8},{4,12},{8,0},{12,4},{16,24},{20,28},{24,16},{28,20},{1,9},{5... | collective-permute-start | bytes 393224 | tf_op jit(solution)/shard_map/ppermute | solution.py:607
  26.7 8.8 %collective-permute-start.8 = (f32[2,192,256]{2,1,0:T(8,128)S(1)}, f32[2,192,256]{2,1,0:T(8,128)S(1)}, u32[]{:S(2)}, u32[]{:S(2)}) collective-permute-start(f32[2,192,256]{2,1,0:T(8,128)S(1)} %joined.3.own_ref), channel_id=1, source_target_pairs={{0,2},{1,3},{2,0},{3,1},{4,6},{5,7},{6,4},{7,5},{8,10},{9,11},{10,... | collective-permute-start | bytes 1179656 | tf_op jit(solution)/shard_map/ppermute | solution.py:607
  28.3 7.4 %collective-permute-start.9 = (f32[2,64,256]{2,1,0:T(8,128)S(1)}, f32[2,64,256]{2,1,0:T(8,128)S(1)}, u32[]{:S(2)}, u32[]{:S(2)}) collective-permute-start(f32[2,64,256]{2,1,0:T(8,128)S(1)} %get-tuple-element.61), channel_id=1, source_target_pairs={{0,24},{4,28},{8,16},{12,20},{16,8},{20,12},{24,0},{28,4},{1,25},{... | collective-permute-start | bytes 393224 | tf_op jit(solution)/shard_map/ppermute | solution.py:607
  31.0 5.0 %collective-permute-start.11 = (f32[2,256,256]{2,1,0:T(8,128)S(1)}, f32[2,256,256]{2,1,0:T(8,128)S(1)}, u32[]{:S(2)}, u32[]{:S(2)}) collective-permute-start(f32[2,256,256]{2,1,0:T(8,128)S(1)} %turned_pieces.1.own_ref), channel_id=1, source_target_pairs={{0,1},{1,0},{2,3},{3,2},{4,5},{5,4},{6,7},{7,6},{8,9},{9,8},{10,11... | collective-permute-start | bytes 1572872 | tf_op jit(solution)/shard_map/ppermute | solution.py:607
  35.9 2.0 %collective-permute-start.10 = (f32[2,256,256]{2,1,0:T(8,128)S(1)}, f32[2,256,256]{2,1,0:T(8,128)S(1)}, u32[]{:S(2)}, u32[]{:S(2)}) collective-permute-start(f32[2,256,256]{2,1,0:T(8,128)S(1)} %turned.1.own_ref), channel_id=1, source_target_pairs={{0,1},{1,0},{2,3},{3,2},{4,5},{5,4},{6,7},{7,6},{8,9},{9,8},{10,11... | collective-permute-start | bytes 1572872 | tf_op jit(solution)/shard_map/ppermute | solution.py:607
